TPU v7x, 32 devices: a whole 2x2x4 slice. The times are simulated.
32 devices in a mesh: rep: 16 (over z, x, core), grp: 2 (over y).
Axes of the slice: x: 2, y: 2, z: 4, core: 2. Of those that a mesh axis runs over, the one named last changes fastest.
Arguments:
- tokens: bfloat16 [16, 1024, 768], P('rep', 'grp'), may hold values from -6 to 6
- segment_ids: int32 [16, 1024], P('rep', 'grp'), may hold values from 0 to 2, as said below
- expert_ids: int32 [16, 1024, 1], P('rep', 'grp'), may hold values from 0 to 7; in each aligned block of 512 rows (0 to 511, 512 to 1023, ..., all dimensions but the last counted through in order) at most 128 rows name the same one
- rel_bucket: int32 [2047], replicated, may hold values from 0 to 31
- query_key_value_weight: bfloat16 [768, 2304], P('grp'), may hold values from -0.21875 to 0.21875
- output_weight: bfloat16 [768, 768], P('grp'), may hold values from -1.75 to 1.75
- router_weight: bfloat16 [768, 8], P('grp'), may hold values from -0.21875 to 0.21875
- gain_attn: bfloat16 [768], P('grp'), may hold values from 0.5 to 1.5
- gain_ffn: bfloat16 [768], P('grp'), may hold values from 0.5 to 1.5
- rel_table: bfloat16 [32, 12], P('grp'), may hold values from -4 to 4
- w_up: bfloat16 [24576, 768], P('grp'), may hold values from -0.21875 to 0.21875
- w_down: bfloat16 [24576, 768], P('grp'), may hold values from -1.25 to 1.25
- out_grad: bfloat16 [16, 1024, 768], P('rep', 'grp'), may hold values from -6 to 6
Outputs:
- layer_out: bfloat16 [16, 1024, 768], P('rep', 'grp')
- tokens_grad: float32 [16, 1024, 768], P('rep', 'grp')
- grad_w_qkv: float32 [768, 2304], P('grp')
- grad_w_out: float32 [768, 768], P('grp')
- grad_w_router: float32 [768, 8], P('grp')
- grad_gain_attn: float32 [768], P('grp')
- grad_gain_ffn: float32 [768], P('grp')
- grad_rel_table: float32 [32, 12], P('grp')
- grad_w_up: float32 [24576, 768], P('grp')
- grad_w_down: float32 [24576, 768], P('grp')
Inputs may be any that keep to these rules, and one draw needn't show every extreme that they name: `segment_ids`: ids never fall along a sequence. `expert_ids`: in each aligned block of 512 positions of a sequence at most 128 tokens name one expert.
All inputs are finite; a program needn't handle non-finite values.
Results may differ from a plain program's by a relative error of at most 0.025.
Values may be sent and summed in bfloat16 or wider, within the bound.
No kernel may reach another device: no remote copies, remote signals or barrier semaphores. Data moves between devices by JAX's collectives and lax.ppermute only.
A program may use at most 512 MiB of HBM per device.

v0:
```python
import jax
import jax.numpy as jnp
from jax import lax
from jax.sharding import PartitionSpec as P

eps_norm = 1e-06
neg_fill = -1e30


def rms_parts(values, gain_vec):
    inverse = lax.rsqrt(jnp.mean(values * values, axis=-1, keepdims=True) + eps_norm)
    return (inverse, values * inverse * gain_vec)


def rms_back(grad_normed, values, inverse, gain_vec):
    scaled = grad_normed * gain_vec
    grad_gain = jnp.sum(grad_normed * values * inverse, axis=(0, 1))
    grad_values = inverse * (
        scaled - values * inverse * inverse * jnp.mean(scaled * values, axis=-1, keepdims=True)
    )
    return (grad_values, grad_gain)


def skewed(window, rows, cols):
    width = rows + cols
    head_count = window.shape[0]
    padded = jnp.pad(window, ((0, 0), (0, 1)))
    tiled = jnp.broadcast_to(padded[:, None, :], (head_count, rows, width)).reshape(
        head_count, rows * width
    )
    cut = tiled[:, rows - 1 : rows - 1 + rows * (width - 1)].reshape(head_count, rows, width - 1)
    return cut[:, :, :cols]


def unskewed(grid, rows, cols):
    width = rows + cols
    head_count = grid.shape[0]
    padded = jnp.pad(grid, ((0, 0), (0, 0), (0, rows - 1)))
    flat = padded.reshape(head_count, rows * (width - 1))
    flat = jnp.pad(flat, ((0, 0), (rows - 1, 1)))
    return jnp.sum(flat.reshape(head_count, rows, width), axis=1)[:, : width - 1]


def attention_scores(queries, key_heads, seg_own, seg_keys, pos_bias, score_scale):
    scores = (
        jnp.einsum("sqhd,skhd->shqk", queries, key_heads, preferred_element_type=jnp.float32)
        * score_scale
        + pos_bias[None]
    )
    same_doc = seg_own[:, :, None] == seg_keys[:, None, :]
    return jnp.where(same_doc[:, None], scores, neg_fill)


def expert_forward(expert_in, up_rows, down_rows):
    pre_act = jnp.einsum("erd,efd->erf", expert_in, up_rows, preferred_element_type=jnp.float32)
    activated = jax.nn.gelu(pre_act, approximate=True).astype(jnp.bfloat16)
    expert_out = jnp.einsum(
        "erf,efd->erd", activated, down_rows, preferred_element_type=jnp.float32
    ).astype(jnp.bfloat16)
    return (pre_act, activated, expert_out)


def expert_backward(expert_in, pre_act, activated, grad_out, up_rows, down_rows):
    grad_act = jnp.einsum("erd,efd->erf", grad_out, down_rows, preferred_element_type=jnp.float32)
    gelu_value, gelu_pull = jax.vjp(
        lambda pre_value: jax.nn.gelu(pre_value, approximate=True), pre_act
    )
    grad_pre = gelu_pull(grad_act)[0].astype(jnp.bfloat16)
    grad_down = jnp.einsum("erf,erd->efd", activated, grad_out, preferred_element_type=jnp.float32)
    grad_up = jnp.einsum("erf,erd->efd", grad_pre, expert_in, preferred_element_type=jnp.float32)
    grad_in = jnp.einsum(
        "erf,efd->erd", grad_pre, up_rows, preferred_element_type=jnp.float32
    ).astype(jnp.bfloat16)
    return (grad_up, grad_down, grad_in)


def local(
    tokens,
    segment_ids,
    expert_ids,
    rel_bucket,
    query_key_value_weight,
    output_weight,
    router_weight,
    gain_attn,
    gain_ffn,
    rel_table,
    w_up,
    w_down,
    out_grad,
):
    groups = lax.axis_size("grp")
    grp_index = lax.axis_index("grp")
    seq_count, span_len, model_width = tokens.shape
    length = span_len * groups
    head_count = rel_table.shape[1]
    head_dim = model_width // head_count
    buckets = rel_table.shape[0] * groups
    experts = router_weight.shape[1]
    slot_most = span_len // 4
    hidden = w_up.shape[0] * groups // experts
    score_scale = head_dim ** (-0.5)
    full_qkv, full_out, full_router, full_gain_attn, full_gain_ffn, full_table = (
        lax.all_gather(query_key_value_weight, "grp", axis=0, tiled=True),
        lax.all_gather(output_weight, "grp", axis=0, tiled=True),
        lax.all_gather(router_weight, "grp", axis=0, tiled=True),
        lax.all_gather(gain_attn, "grp", axis=0, tiled=True),
        lax.all_gather(gain_ffn, "grp", axis=0, tiled=True),
        lax.all_gather(rel_table, "grp", axis=0, tiled=True),
    )
    gain_one = full_gain_attn.astype(jnp.float32)
    gain_two = full_gain_ffn.astype(jnp.float32)
    input_tokens = tokens.astype(jnp.float32)
    inverse_one, normalized_input = rms_parts(input_tokens, gain_one)
    normalized_input = normalized_input.astype(jnp.bfloat16)
    projected_output = jnp.einsum(
        "std,de->ste", normalized_input, full_qkv, preferred_element_type=jnp.float32
    ).astype(jnp.bfloat16)
    queries = projected_output[..., :model_width].reshape(seq_count, span_len, head_count, head_dim)
    keys_own = projected_output[..., model_width : 2 * model_width]
    values_own = projected_output[..., 2 * model_width :]
    keys_all, values_all, seg_all = (
        lax.all_gather(keys_own, "grp", axis=1, tiled=True),
        lax.all_gather(values_own, "grp", axis=1, tiled=True),
        lax.all_gather(segment_ids, "grp", axis=1, tiled=True),
    )
    bucket_hot = (rel_bucket[None, :] == jnp.arange(buckets)[:, None]).astype(jnp.bfloat16)
    bias_line = jnp.einsum("bh,bo->ho", full_table, bucket_hot, preferred_element_type=jnp.float32)
    window_start = length - (grp_index + 1) * span_len
    window_len = span_len + length - 1
    bias_window = lax.dynamic_slice_in_dim(bias_line, window_start, window_len, 1)
    pos_bias = skewed(bias_window, span_len, length)
    key_heads = keys_all.reshape(seq_count, length, head_count, head_dim)
    value_heads = values_all.reshape(seq_count, length, head_count, head_dim)
    scores = attention_scores(queries, key_heads, segment_ids, seg_all, pos_bias, score_scale)
    row_max = jnp.max(scores, axis=-1, keepdims=True)
    log_total = row_max + jnp.log(jnp.sum(jnp.exp(scores - row_max), axis=-1, keepdims=True))
    attn_probs = jnp.exp(scores - log_total).astype(jnp.bfloat16)
    attention_result = jnp.einsum(
        "shqk,skhd->sqhd", attn_probs, value_heads, preferred_element_type=jnp.float32
    )
    attention_result = attention_result.astype(jnp.bfloat16).reshape(
        seq_count, span_len, model_width
    )
    residual_stream = input_tokens + jnp.einsum(
        "std,de->ste", attention_result, full_out, preferred_element_type=jnp.float32
    )
    inverse_two, normalized_feedforward = rms_parts(residual_stream, gain_two)
    normalized_feedforward = normalized_feedforward.astype(jnp.bfloat16)
    router_logits = jnp.einsum(
        "std,de->ste", normalized_feedforward, full_router, preferred_element_type=jnp.float32
    )
    router = jax.nn.softmax(router_logits, axis=-1)
    chosen = expert_ids[..., 0][..., None] == jnp.arange(experts)
    chosen_int = chosen.astype(jnp.int32)
    chosen_float = chosen.astype(jnp.float32)
    gate_prob = jnp.sum(router * chosen_float, axis=-1)
    strict_lower = (jnp.arange(span_len)[:, None] > jnp.arange(span_len)[None, :]).astype(
        jnp.bfloat16
    )
    earlier = jnp.einsum(
        "tu,sue->ste", strict_lower, chosen.astype(jnp.bfloat16), preferred_element_type=jnp.float32
    )
    slot_rank = jnp.sum(earlier * chosen_float, axis=-1).astype(jnp.int32)
    slot_index = jnp.sum(chosen_int * jnp.arange(experts), axis=-1) * slot_most + slot_rank
    dispatch = (slot_index[..., None] == jnp.arange(experts * slot_most)).astype(jnp.bfloat16)
    expert_in = jnp.einsum(
        "stc,std->csd", dispatch, normalized_feedforward, preferred_element_type=jnp.float32
    )
    expert_in = expert_in.astype(jnp.bfloat16).reshape(experts, slot_most * seq_count, model_width)
    up_all, down_all = (
        lax.all_gather(w_up, "grp", axis=0, tiled=True),
        lax.all_gather(w_down, "grp", axis=0, tiled=True),
    )
    pre_act, activated, expert_out = expert_forward(
        expert_in,
        up_all.reshape(experts, hidden, model_width),
        down_all.reshape(experts, hidden, model_width),
    )
    returned = jnp.einsum(
        "stc,csd->std",
        dispatch,
        expert_out.reshape(experts * slot_most, seq_count, model_width),
        preferred_element_type=jnp.float32,
    )
    layer_out = (residual_stream + gate_prob[..., None] * returned).astype(jnp.bfloat16)
    cotangent = out_grad.astype(jnp.float32)
    grad_gate = jnp.sum(cotangent * returned, axis=-1)
    grad_returned = (gate_prob[..., None] * cotangent).astype(jnp.bfloat16)
    grad_expert_out = jnp.einsum(
        "stc,std->csd", dispatch, grad_returned, preferred_element_type=jnp.float32
    )
    grad_expert_out = grad_expert_out.astype(jnp.bfloat16).reshape(
        experts, slot_most * seq_count, model_width
    )
    up_again, down_again = (
        lax.all_gather(w_up, "grp", axis=0, tiled=True),
        lax.all_gather(w_down, "grp", axis=0, tiled=True),
    )
    grad_up, grad_down, grad_in = expert_backward(
        expert_in,
        pre_act,
        activated,
        grad_expert_out,
        up_again.reshape(experts, hidden, model_width),
        down_again.reshape(experts, hidden, model_width),
    )
    grad_up_own, grad_down_own = (
        lax.psum_scatter(
            grad_up.reshape(experts * hidden, model_width).astype(jnp.bfloat16),
            "grp",
            scatter_dimension=0,
            tiled=True,
        ).astype(jnp.float32),
        lax.psum_scatter(
            grad_down.reshape(experts * hidden, model_width).astype(jnp.bfloat16),
            "grp",
            scatter_dimension=0,
            tiled=True,
        ).astype(jnp.float32),
    )
    grad_from_experts = jnp.einsum(
        "stc,csd->std",
        dispatch,
        grad_in.reshape(experts * slot_most, seq_count, model_width),
        preferred_element_type=jnp.float32,
    )
    grad_logits = (grad_gate[..., None] * router * (chosen_float - gate_prob[..., None])).astype(
        jnp.bfloat16
    )
    grad_router = jnp.einsum(
        "std,ste->de", normalized_feedforward, grad_logits, preferred_element_type=jnp.float32
    )
    grad_normed_ffn = grad_from_experts + jnp.einsum(
        "ste,de->std", grad_logits, full_router, preferred_element_type=jnp.float32
    )
    grad_mid, grad_gain_ffn = rms_back(grad_normed_ffn, residual_stream, inverse_two, gain_two)
    grad_residual = cotangent + grad_mid
    grad_attn = grad_residual.astype(jnp.bfloat16)
    grad_wout = jnp.einsum(
        "std,ste->de", attention_result, grad_attn, preferred_element_type=jnp.float32
    )
    grad_attended = jnp.einsum(
        "ste,de->std", grad_attn, full_out, preferred_element_type=jnp.float32
    )
    grad_attended = grad_attended.astype(jnp.bfloat16).reshape(
        seq_count, span_len, head_count, head_dim
    )
    keys_back, values_back, seg_back = (
        lax.all_gather(keys_own, "grp", axis=1, tiled=True),
        lax.all_gather(values_own, "grp", axis=1, tiled=True),
        lax.all_gather(segment_ids, "grp", axis=1, tiled=True),
    )
    key_back_heads = keys_back.reshape(seq_count, length, head_count, head_dim)
    value_back_heads = values_back.reshape(seq_count, length, head_count, head_dim)
    scores_back = attention_scores(
        queries, key_back_heads, segment_ids, seg_back, pos_bias, score_scale
    )
    probs_back = jnp.exp(scores_back - log_total)
    grad_probs = jnp.einsum(
        "sqhd,skhd->shqk", grad_attended, value_back_heads, preferred_element_type=jnp.float32
    )
    row_delta = jnp.sum(probs_back * grad_probs, axis=-1, keepdims=True)
    grad_scores = (probs_back * (grad_probs - row_delta)).astype(jnp.bfloat16)
    grad_queries = (
        jnp.einsum(
            "shqk,skhd->sqhd", grad_scores, key_back_heads, preferred_element_type=jnp.float32
        )
        * score_scale
    )
    grad_queries = grad_queries.astype(jnp.bfloat16).reshape(seq_count, span_len, model_width)
    grad_window = unskewed(jnp.sum(grad_scores, axis=0, dtype=jnp.float32), span_len, length)
    hot_window = lax.dynamic_slice_in_dim(bucket_hot, window_start, window_len, 1).astype(
        jnp.float32
    )
    grad_table = jnp.einsum("bo,ho->bh", hot_window, grad_window, precision=lax.Precision.HIGHEST)
    key_terms = (
        jnp.einsum("shqk,sqhd->skhd", grad_scores, queries, preferred_element_type=jnp.float32)
        * score_scale
    )
    value_terms = jnp.einsum(
        "shqk,sqhd->skhd",
        probs_back.astype(jnp.bfloat16),
        grad_attended,
        preferred_element_type=jnp.float32,
    )
    grad_keys, grad_values = (
        lax.psum_scatter(
            key_terms.reshape(seq_count, length, model_width).astype(jnp.bfloat16),
            "grp",
            scatter_dimension=1,
            tiled=True,
        ).astype(jnp.float32),
        lax.psum_scatter(
            value_terms.reshape(seq_count, length, model_width).astype(jnp.bfloat16),
            "grp",
            scatter_dimension=1,
            tiled=True,
        ).astype(jnp.float32),
    )
    grad_mixed = jnp.concatenate(
        [grad_queries, grad_keys.astype(jnp.bfloat16), grad_values.astype(jnp.bfloat16)], axis=-1
    )
    grad_qkv = jnp.einsum(
        "std,ste->de", normalized_input, grad_mixed, preferred_element_type=jnp.float32
    )
    grad_normed = jnp.einsum(
        "ste,de->std", grad_mixed, full_qkv, preferred_element_type=jnp.float32
    )
    grad_input_part, grad_gain_attn = rms_back(grad_normed, input_tokens, inverse_one, gain_one)
    tokens_grad = grad_residual + grad_input_part
    share_qkv, share_out, share_router, share_gain_attn, share_gain_ffn, share_table = (
        lax.psum_scatter(
            grad_qkv.astype(jnp.bfloat16), "grp", scatter_dimension=0, tiled=True
        ).astype(jnp.float32),
        lax.psum_scatter(
            grad_wout.astype(jnp.bfloat16), "grp", scatter_dimension=0, tiled=True
        ).astype(jnp.float32),
        lax.psum_scatter(
            grad_router.astype(jnp.bfloat16), "grp", scatter_dimension=0, tiled=True
        ).astype(jnp.float32),
        lax.psum_scatter(
            grad_gain_attn.astype(jnp.bfloat16), "grp", scatter_dimension=0, tiled=True
        ).astype(jnp.float32),
        lax.psum_scatter(
            grad_gain_ffn.astype(jnp.bfloat16), "grp", scatter_dimension=0, tiled=True
        ).astype(jnp.float32),
        lax.psum_scatter(
            grad_table.astype(jnp.bfloat16), "grp", scatter_dimension=0, tiled=True
        ).astype(jnp.float32),
    )
    sum_qkv, sum_out, sum_router, sum_gain_attn, sum_gain_ffn, sum_table, sum_up, sum_down = (
        lax.psum(share_qkv.astype(jnp.bfloat16), "rep").astype(jnp.float32),
        lax.psum(share_out.astype(jnp.bfloat16), "rep").astype(jnp.float32),
        lax.psum(share_router.astype(jnp.bfloat16), "rep").astype(jnp.float32),
        lax.psum(share_gain_attn.astype(jnp.bfloat16), "rep").astype(jnp.float32),
        lax.psum(share_gain_ffn.astype(jnp.bfloat16), "rep").astype(jnp.float32),
        lax.psum(share_table.astype(jnp.bfloat16), "rep").astype(jnp.float32),
        lax.psum(grad_up_own.astype(jnp.bfloat16), "rep").astype(jnp.float32),
        lax.psum(grad_down_own.astype(jnp.bfloat16), "rep").astype(jnp.float32),
    )
    return (
        layer_out,
        tokens_grad,
        sum_qkv,
        sum_out,
        sum_router,
        sum_gain_attn,
        sum_gain_ffn,
        sum_table,
        sum_up,
        sum_down,
    )


def solution(mesh):
    return jax.shard_map(
        local,
        mesh=mesh,
        in_specs=(
            P("rep", "grp", None),
            P("rep", "grp"),
            P("rep", "grp", None),
            P(),
            P("grp", None),
            P("grp", None),
            P("grp", None),
            P("grp"),
            P("grp"),
            P("grp", None),
            P("grp", None),
            P("grp", None),
            P("rep", "grp", None),
        ),
        out_specs=(
            P("rep", "grp", None),
            P("rep", "grp", None),
            P("grp", None),
            P("grp", None),
            P("grp", None),
            P("grp"),
            P("grp"),
            P("grp", None),
            P("grp", None),
            P("grp", None),
        ),
        check_vma=False,
    )
```

profile of v0, /device:TPU:0, one launch (start us, length us, event | category | flops | bytes accessed | tf_op | source)
XLA Modules:
  0.0 2842.9 jit_solution(14405698727176616848)
XLA Ops:
  15.3 46.3 %all-gather.9.cloned.1.call-done = bf16[768,2304]{1,0:T(8,128)(2,1)} async-done(((bf16[384,2304]{1,0:T(8,128)(2,1)}), bf16[768,2304]{1,0:T(8,128)(2,1)}) %all-gather.9.cloned.1.call-update) | async-done | bytes 3538960 | tf_op jit(solution)/shard_map/all_gather | solution.py:104
  87.3 30.2 %pad.20 = f32[16,512,1536]{2,1,0:T(8,128)} pad(f32[12,512,1536]{2,1,0:T(8,128)} %broadcast_in_dim.15, f32[]{:T(128)} %constant.20.clone.1), padding=0_4x0_0x0_0 | pad | bytes 88080384
  117.6 48.1 %copy.63 = f32[2,8,512,1536]{3,1,2,0:T(8,128)} copy(f32[2,8,512,1536]{3,2,1,0:T(8,128)} %bitcast.165) | data formatting | bytes 100663296
  165.7 41.9 %slice.27 = f32[12,785920]{1,0:T(8,128)} slice(f32[12,786432]{1,0:T(8,128)} %bitcast.167), slice={[0:12], [511:786431]} | slice | bytes 75448320 | tf_op jit(solution)/shard_map/slice | solution.py:31
  207.6 86.2 %reshape.580 = f32[12,512,1535]{2,1,0:T(8,128)} reshape(f32[12,785920]{1,0:T(8,128)} %slice.27) | data formatting | bytes 75448320 | tf_op jit(solution)/shard_map/reshape | solution.py:31
  313.6 16.9 fusion.90
  367.8 219.2 %all-gather.19.cloned.1.call-done = bf16[24576,768]{1,0:T(8,128)(2,1)} async-done(((bf16[12288,768]{1,0:T(8,128)(2,1)}), bf16[24576,768]{1,0:T(8,128)(2,1)}) %all-gather.19.cloned.1.call-update) | async-done | bytes 37748752 | tf_op jit(solution)/shard_map/all_gather | solution.py:173
  587.0 27.4 fusion.93
  614.4 411.1 %all-gather.17.cloned.1.call-done = bf16[24576,768]{1,0:T(8,128)(2,1)} async-done(((bf16[12288,768]{1,0:T(8,128)(2,1)}), bf16[24576,768]{1,0:T(8,128)(2,1)}) %all-gather.17.cloned.1.call-update) | async-done | bytes 37748752 | tf_op jit(solution)/shard_map/all_gather | solution.py:172
  1025.5 27.2 fusion.8
  1052.7 20.0 convolution_convert_fusion.5
  1077.9 18.7 convolution_convert_fusion.4
  1117.1 17.7 multiply_reduce_fusion
  1134.8 16.7 multiply_convert_fusion
  1189.9 18.2 convolution_convert_fusion.1
  1221.9 69.5 %reshape.594 = bf16[12,785920]{1,0:T(8,128)(2,1)} reshape(bf16[12,512,1535]{2,1,0:T(8,128)(2,1)} %pad.15) | data formatting | bytes 37724160 | tf_op jit(solution)/shard_map/reshape | solution.py:39
  1291.5 22.7 convolution_convert_fusion
  1314.3 27.8 pad_convert_fusion
  1342.1 46.1 %copy.64 = f32[2,8,512,1536]{3,2,1,0:T(8,128)} copy(f32[2,8,512,1536]{3,1,2,0:T(8,128)} %bitcast.166) | data formatting | bytes 100663296
  1403.2 271.8 %reduce-scatter.21.cloned.1.call-done = bf16[12288,768]{1,0:T(8,128)(2,1)} async-done(((bf16[24576,768]{1,0:T(8,128)(2,1)}), bf16[12288,768]{1,0:T(8,128)(2,1)}) %reduce-scatter.21.cloned.1.call-update) | async-done | bytes 18874384 | tf_op jit(solution)/shard_map/reduce_scatter | solution.py:209
  1674.9 416.7 %reduce-scatter.23.cloned.1.call-done = bf16[12288,768]{1,0:T(8,128)(2,1)} async-done(((bf16[24576,768]{1,0:T(8,128)(2,1)}), bf16[12288,768]{1,0:T(8,128)(2,1)}) %reduce-scatter.23.cloned.1.call-update) | async-done | bytes 18874384 | tf_op jit(solution)/shard_map/reduce_scatter | solution.py:215
  2117.2 64.0 %all-reduce.5 = (bf16[384,8]{0,1:T(8,128)(2,1)S(1)}, bf16[384]{0:T(512)(128)(2,1)S(1)}, bf16[384]{0:T(512)(128)(2,1)S(1)}, bf16[16,12]{1,0:T(8,128)(2,1)S(1)}) all-reduce(bf16[384,8]{0,1:T(8,128)(2,1)S(1)} %copy.60, bf16[384]{0:T(512)(128)(2,1)S(1)} %dynamic-slice.5, ...), channel_id=1, replica_groups=mesh['rep'=16,'grp'=2] {'rep'}, use_global_device_ids=true, to_apply=%region_20.21 | all-reduce | flops 4032 | bytes 16128 | tf_op jit(solution)/shard_map/psum | solution.py:335
  2186.6 606.8 %all-reduce.10.cloned.1.call-done = (bf16[384,2304]{1,0:T(8,128)(2,1)}, bf16[384,768]{1,0:T(8,128)(2,1)}, bf16[12288,768]{1,0:T(8,128)(2,1)}, bf16[12288,768]{1,0:T(8,128)(2,1)}) async-done(((bf16[384,2304]{1,0:T(8,128)(2,1)}, bf16[384,768]{1,0:T(8,128)(2,1)}, bf16[12288,768]{1,0:T(8,128)(2,1)}, bf16[12288,768]{1,0:T(8,128)(2,1)}), (bf16[384,2304]{1,0:T(8,128)(2,1)}, bf16[384,768]{1,0:T(8,128)(2,1)}, ...) | async-done | bytes 40108048 | tf_op jit(solution)/shard_map/psum | solution.py:333
  2798.0 24.8 convert_element_type.294
  (196 shorter events, 231.6 us)
Async XLA Ops:
  7.2 54.5 %all-gather.9.cloned.1.call-start = ((), (), s32[]{:S(2)}) async-start(), calls=%async_computation.8 | async-start | bytes 5308416 | tf_op jit(solution)/shard_map/all_gather | solution.py:104
  7.9 301.7 %all-gather.11.cloned.1.call-start = ((), (), s32[]{:S(2)}) async-start(), calls=%async_computation.9 | async-start | bytes 2359296 | tf_op jit(solution)/shard_map/all_gather | solution.py:124
  13.9 47.7 %copy-start.26 = (f32[768]{0:T(1024)}, f32[768]{0:T(1024)S(1)}, u32[]{:S(2)}) copy-start(f32[768]{0:T(1024)S(1)} %reshape.603) | copy-start | bytes 9220
  15.3 46.4 %copy-start.29 = (f32[512]{0:T(512)}, f32[512]{0:T(512)S(1)}, u32[]{:S(2)}) copy-start(f32[512]{0:T(512)S(1)} %add_rsqrt_fusion.1) | copy-start | bytes 6148
  67.3 244.1 %all-gather.13.cloned.1.call-start = ((), (), s32[]{:S(2)}) async-start(), calls=%async_computation.10 | async-start | bytes 2359296 | tf_op jit(solution)/shard_map/all_gather | solution.py:123
  68.1 284.6 %all-gather.15.cloned.1.call-start = ((), (), s32[]{:S(2)}) async-start(), calls=%async_computation.11 | async-start | bytes 1769472 | tf_op jit(solution)/shard_map/all_gather | solution.py:105
  68.6 518.4 %all-gather.19.cloned.1.call-start = ((), (), s32[]{:S(2)}) async-start(), calls=%async_computation.13 | async-start | bytes 56623104 | tf_op jit(solution)/shard_map/all_gather | solution.py:173
  69.2 956.3 %all-gather.17.cloned.1.call-start = ((), (), s32[]{:S(2)}) async-start(), calls=%async_computation.12 | async-start | bytes 56623104 | tf_op jit(solution)/shard_map/all_gather | solution.py:172
  69.8 1099.2 %reduce-scatter.13.cloned.1.call-start = ((), (), s32[]{:S(2)}) async-start(), calls=%async_computation.15 | async-start | bytes 2359296 | tf_op jit(solution)/shard_map/reduce_scatter | solution.py:294
  207.5 86.2 %copy-start.34 = (bf16[384]{0:T(512)(128)(2,1)S(1)}, bf16[384]{0:T(512)(128)(2,1)}, u32[]{:S(2)}) copy-start(bf16[384]{0:T(512)(128)(2,1)} %param.21) | copy-start | bytes 2308
  207.5 90.6 %copy-start.28 = (s32[1,512]{1,0:T(1,128)S(1)}, s32[1,512]{1,0:T(1,128)}, u32[]{:S(2)}) copy-start(s32[1,512]{1,0:T(1,128)} %param.14) | copy-start | bytes 6148
  207.6 95.0 %copy-start.31 = (bf16[384,8]{0,1:T(8,128)(2,1)S(1)}, bf16[384,8]{0,1:T(8,128)(2,1)}, u32[]{:S(2)}) copy-start(bf16[384,8]{0,1:T(8,128)(2,1)} %param.19) | copy-start | bytes 18436
  207.6 99.4 %copy-start.23 = (s32[1,512,1]{1,2,0:T(1,128)S(1)}, s32[1,512,1]{1,2,0:T(1,128)}, u32[]{:S(2)}) copy-start(s32[1,512,1]{1,2,0:T(1,128)} %param.15) | copy-start | bytes 6148
  361.2 225.8 %copy-start.1 = (bf16[1024,1,768]{2,0,1:T(8,128)(2,1)}, bf16[1024,1,768]{2,0,1:T(8,128)(2,1)S(1)}, u32[]{:S(2)}) copy-start(bf16[1024,1,768]{2,0,1:T(8,128)(2,1)S(1)} %copy.62) | copy-start | bytes 4718596
  1117.0 66.0 %reduce-scatter.11.cloned.1.call-start = ((), (), s32[]{:S(2)}) async-start(), calls=%async_computation.14 | async-start | bytes 2359296 | tf_op jit(solution)/shard_map/reduce_scatter | solution.py:288
  1156.8 246.3 %reduce-scatter.17.cloned.1.call-start = ((), (), s32[]{:S(2)}) async-start(), calls=%async_computation.17 | async-start | bytes 1769472 | tf_op jit(solution)/shard_map/reduce_scatter | solution.py:316
  1159.9 243.3 %reduce-scatter.15.cloned.1.call-start = ((), (), s32[]{:S(2)}) async-start(), calls=%async_computation.16 | async-start | bytes 5308416 | tf_op jit(solution)/shard_map/reduce_scatter | solution.py:313
  1188.5 486.5 %reduce-scatter.21.cloned.1.call-start = ((), (), s32[]{:S(2)}) async-start(), calls=%async_computation.19 | async-start | bytes 56623104 | tf_op jit(solution)/shard_map/reduce_scatter | solution.py:209
  1208.0 883.6 %reduce-scatter.23.cloned.1.call-start = ((), (), s32[]{:S(2)}) async-start(), calls=%async_computation.20 | async-start | bytes 56623104 | tf_op jit(solution)/shard_map/reduce_scatter | solution.py:215
  1221.9 69.5 %copy-start.2 = (bf16[1024,1,768]{2,0,1:T(8,128)(2,1)S(1)}, bf16[1024,1,768]{2,0,1:T(8,128)(2,1)}, u32[]{:S(2)}) copy-start(bf16[1024,1,768]{2,0,1:T(8,128)(2,1)} %copy-done.1) | copy-start | bytes 4718596
  1314.2 790.6 %reduce-scatter.25.cloned.1.call-start = ((), (), s32[]{:S(2)}) async-start(), calls=%async_computation.21 | async-start | bytes 294912
  1402.1 715.1 %reduce-scatter.19.cloned.1.call-start = ((), (), s32[]{:S(2)}) async-start(), calls=%async_computation.18 | async-start | bytes 12288 | tf_op jit(solution)/shard_map/reduce_scatter | solution.py:328
  1403.1 1390.3 %all-reduce.10.cloned.1.call-start = ((), (), s32[]{:S(2)}) async-start(), calls=%async_computation.22 | async-start | bytes 80216064 | tf_op jit(solution)/shard_map/psum | solution.py:333
  2105.8 77.8 %copy-start.7 = (f32[1,512,768]{2,1,0:T(8,128)S(1)}, f32[1,512,768]{2,1,0:T(8,128)}, u32[]{:S(2)}) copy-start(f32[1,512,768]{2,1,0:T(8,128)} %copy-done.5) | copy-start | bytes 4718596
  (33 other events, 383.2 us)
Sparse Core Ops, SparseCore 0:
  9.6 52.0 all-gather.8
  67.4 27.2 all-gather.10
  96.8 27.1 all-gather.12
  125.4 22.7 all-gather.14
  149.7 437.2 all-gather.18
  588.4 437.0 all-gather.16
  1117.2 26.0 reduce-scatter.12
  1156.9 26.0 reduce-scatter.10
  1185.8 21.7 reduce-scatter.16
  1210.4 47.6 reduce-scatter.14
  1261.0 413.9 reduce-scatter.20
  1677.7 413.8 reduce-scatter.22
  2093.8 10.9 reduce-scatter.24
  2107.4 9.7 reduce-scatter.18
  2121.9 671.3 all-reduce.9
where the time goes:
time: 2850 us; the launch traced here: 2840 us
  waiting for transfers between devices  2000 us (70%)
  local copies, waits for them, and re-layouts  368 us (13%)
  matrix products  245 us (9%)
  other arithmetic  122 us (4%)
  blocking collectives  91.6 us (3%)
    psum x1, waiting for transfers between devices, local(): lax.psum(share_qkv.astype(jnp.bfloat16), 'rep').astype(jnp.float32)  607 us
    reduce_scatter x1, waiting for transfers between devices, local(): lax.psum_scatter(grad_down.reshape(experts * hidden, model_width).astype(...  417 us
    all_gather x1, waiting for transfers between devices, local(): lax.all_gather(w_up, 'grp', axis=0, tiled=True)  411 us
    reduce_scatter x1, waiting for transfers between devices, local(): lax.psum_scatter(grad_up.reshape(experts * hidden, model_width).astype(jn...  272 us
    all_gather x1, waiting for transfers between devices, local(): lax.all_gather(w_down, 'grp', axis=0, tiled=True)  219 us
    unnamed x94, local copies, waits for them, and re-layouts  134 us
    reshape x1, local copies, waits for them, and re-layouts, skewed(): tiled[:, rows - 1:rows - 1 + rows * (width - 1)]  86.2 us
    reshape x1, local copies, waits for them, and re-layouts, unskewed(): flat = padded.reshape(head_count, rows * (width - 1))  69.5 us
  transfers between devices with their start and end apart: 15, of which 9 were waited for; matrix products, arithmetic and copies ran while one was open for 21% of the time, Pallas kernels for 0%

commit v1 on v0

v1 whole, which is shorter than its diff:
```python
import functools

import jax
import jax.numpy as jnp
import numpy as np
from jax import lax
from jax.experimental import pallas as pl
from jax.experimental.pallas import tpu as pltpu
from jax.sharding import PartitionSpec as P

eps_norm = 1e-06
neg_fill = -1e30
CORES = 2
PAIR = 2
INSTANCES = 4
F32 = jnp.float32
BF16 = jnp.bfloat16


def rms_parts(values, gain_vec):
    inverse = lax.rsqrt(jnp.mean(values * values, axis=-1, keepdims=True) + eps_norm)
    return (inverse, values * inverse * gain_vec)


def rms_back(grad_normed, values, inverse, gain_vec):
    scaled = grad_normed * gain_vec
    grad_gain = jnp.sum(grad_normed * values * inverse, axis=(0, 1))
    grad_values = inverse * (
        scaled - values * inverse * inverse * jnp.mean(scaled * values, axis=-1, keepdims=True)
    )
    return (grad_values, grad_gain)


def dot_nn(a, b):
    return lax.dot_general(a, b, (((1,), (0,)), ((), ())), preferred_element_type=F32)


def dot_nt(a, b):
    return lax.dot_general(a, b, (((1,), (1,)), ((), ())), preferred_element_type=F32)


def dot_tn(a, b):
    return lax.dot_general(a, b, (((0,), (0,)), ((), ())), preferred_element_type=F32)


def bias_tables(win_ref, table_ref, head, blocks, tile):
    width = win_ref.shape[-1]
    for b in range(blocks):
        row = win_ref[0, head * blocks + b : head * blocks + b + 1, :]
        spread = jnp.broadcast_to(row, (tile, width))
        table_ref[b] = pltpu.roll(spread, width - (tile - 1), 1, stride=1, stride_axis=0)


def bias_tile(table_ref, a, blocks, tile, span):
    start = span - tile - tile * a
    return jnp.concatenate([table_ref[b, :, start : start + span] for b in range(blocks)], axis=1)


def head_lanes(rows, width, head):
    lane = lax.broadcasted_iota(jnp.int32, (rows, width), 1)
    size = width // PAIR
    return (lane >= head * size) & (lane < (head + 1) * size)


def attention_kernel(scale, q_ref, k_ref, v_ref, seg_q_ref, seg_k_ref, win_ref, o_ref, table_ref):
    blocks, tile = table_ref.shape[0], table_ref.shape[1]
    span, width = q_ref.shape[1], q_ref.shape[2]
    keys, values = k_ref[0], v_ref[0]
    seg_keys = seg_k_ref[0]
    for head in range(PAIR):
        bias_tables(win_ref, table_ref, head, blocks, tile)
        mine = head_lanes(tile, width, head)
        for a in range(span // tile):
            rows = slice(a * tile, (a + 1) * tile)
            queries = q_ref[0, rows, :]
            queries = jnp.where(mine, queries * scale, jnp.zeros_like(queries))
            scores = dot_nt(queries, keys) + bias_tile(table_ref, a, blocks, tile, span)
            scores = jnp.where(seg_q_ref[0, rows, :] == seg_keys, scores, neg_fill)
            parts = jnp.exp(scores - jnp.max(scores, axis=1, keepdims=True))
            total = jnp.sum(parts, axis=1, keepdims=True)
            out = (dot_nn(parts.astype(BF16), values) / total).astype(BF16)
            if head == 0:
                o_ref[0, rows, :] = out
            else:
                o_ref[0, rows, :] = jnp.where(mine, out, o_ref[0, rows, :])


def attention_back_kernel(
    scale,
    q_ref,
    k_ref,
    v_ref,
    do_ref,
    seg_q_ref,
    seg_k_ref,
    win_ref,
    dq_ref,
    dk_ref,
    dv_ref,
    diag_ref,
    table_ref,
    sum_ref,
    dk_acc,
    dv_acc,
):
    blocks, tile = table_ref.shape[0], table_ref.shape[1]
    span, width = q_ref.shape[1], q_ref.shape[2]
    keys, values = k_ref[0], v_ref[0]
    seg_keys = seg_k_ref[0]
    dk_acc[...] = jnp.zeros_like(dk_acc)
    dv_acc[...] = jnp.zeros_like(dv_acc)
    for head in range(PAIR):
        bias_tables(win_ref, table_ref, head, blocks, tile)
        sum_ref[...] = jnp.zeros_like(sum_ref)
        mine = head_lanes(tile, width, head)
        for a in range(span // tile):
            rows = slice(a * tile, (a + 1) * tile)
            queries = q_ref[0, rows, :]
            queries = jnp.where(mine, queries * scale, jnp.zeros_like(queries))
            grad_out = do_ref[0, rows, :]
            grad_out = jnp.where(mine, grad_out, jnp.zeros_like(grad_out))
            scores = dot_nt(queries, keys) + bias_tile(table_ref, a, blocks, tile, span)
            scores = jnp.where(seg_q_ref[0, rows, :] == seg_keys, scores, neg_fill)
            parts = jnp.exp(scores - jnp.max(scores, axis=1, keepdims=True))
            probs = parts * (1.0 / jnp.sum(parts, axis=1, keepdims=True))
            grad_probs = dot_nt(grad_out, values)
            delta = jnp.sum(probs * grad_probs, axis=1, keepdims=True)
            grad_scores = (probs * (grad_probs - delta)).astype(BF16)
            dv_acc[...] += dot_tn(grad_out, probs.astype(BF16))
            dk_acc[...] += dot_tn(queries, grad_scores)
            dq = (dot_nn(grad_scores, keys) * scale.astype(np.float32)).astype(BF16)
            if head == 0:
                dq_ref[0, rows, :] = dq
            else:
                dq_ref[0, rows, :] = jnp.where(mine, dq, dq_ref[0, rows, :])
            wide = grad_scores.astype(F32)
            start = span - tile - tile * a
            for b in range(blocks):
                sum_ref[b, :, start : start + span] += wide[:, b * span : (b + 1) * span]
        for b in range(blocks):
            folded = sum_ref[b]
            lanes = folded.shape[1]
            left = tile
            while left > 1:
                left //= 2
                folded = folded[:left] + pltpu.roll(folded[left:], lanes - left, 1)
            at = head * blocks + b
            diag_ref[0, 0, at : at + 1, :] = pltpu.roll(folded, tile - 1, 1)
    dk_ref[0] = dk_acc[...].T.astype(BF16)
    dv_ref[0] = dv_acc[...].T.astype(BF16)


def attention_specs(seqs, span, length, width, pairs, blocks):
    q_spec = pl.BlockSpec((1, span, width), lambda s, h: (s, 0, h))
    k_spec = pl.BlockSpec((1, length, width), lambda s, h: (s, 0, pairs + h))
    v_spec = pl.BlockSpec((1, length, width), lambda s, h: (s, 0, 2 * pairs + h))
    seg_q_spec = pl.BlockSpec((1, span, 1), lambda s, h: (s, 0, 0))
    seg_k_spec = pl.BlockSpec((1, 1, length), lambda s, h: (s, 0, 0))
    win_spec = pl.BlockSpec((1, PAIR * blocks, 2 * span), lambda s, h: (h, 0, 0))
    return q_spec, k_spec, v_spec, seg_q_spec, seg_k_spec, win_spec


def attention(projected, seg_own, seg_all, window, span, head_count):
    seqs, length, total = projected.shape
    model = total // 3
    pairs, width = head_count // PAIR, model // head_count * PAIR
    blocks = length // span
    tile = min(span, 256)
    scale = np.asarray((model // head_count) ** (-0.5), dtype=BF16)
    q_spec, k_spec, v_spec, seg_q_spec, seg_k_spec, win_spec = attention_specs(
        seqs, span, length, width, pairs, blocks
    )
    return pl.pallas_call(
        functools.partial(attention_kernel, scale),
        grid=(seqs, pairs),
        in_specs=[q_spec, k_spec, v_spec, seg_q_spec, seg_k_spec, win_spec],
        out_specs=q_spec,
        out_shape=jax.ShapeDtypeStruct((seqs, span, model), BF16),
        scratch_shapes=[pltpu.VMEM((blocks, tile, 2 * span), F32)],
        compiler_params=pltpu.CompilerParams(vmem_limit_bytes=48 * 1024 * 1024),
        cost_estimate=pl.CostEstimate(
            flops=4 * seqs * span * length * model,
            bytes_accessed=8 * seqs * length * model,
            transcendentals=seqs * head_count * span * length,
        ),
    )(projected, projected, projected, seg_own[:, :, None], seg_all[:, None, :], window)


def attention_back(projected, grad_attended, seg_own, seg_all, window, span, head_count):
    seqs, length, total = projected.shape
    model = total // 3
    pairs, width = head_count // PAIR, model // head_count * PAIR
    blocks = length // span
    tile = min(span, 256)
    scale = np.asarray((model // head_count) ** (-0.5), dtype=BF16)
    q_spec, k_spec, v_spec, seg_q_spec, seg_k_spec, win_spec = attention_specs(
        seqs, span, length, width, pairs, blocks
    )
    key_spec = pl.BlockSpec((1, length, width), lambda s, h: (s, 0, h))
    diag_spec = pl.BlockSpec((1, 1, PAIR * blocks, 2 * span), lambda s, h: (s, h, 0, 0))
    return pl.pallas_call(
        functools.partial(attention_back_kernel, scale),
        grid=(seqs, pairs),
        in_specs=[q_spec, k_spec, v_spec, q_spec, seg_q_spec, seg_k_spec, win_spec],
        out_specs=[q_spec, key_spec, key_spec, diag_spec],
        out_shape=[
            jax.ShapeDtypeStruct((seqs, span, model), BF16),
            jax.ShapeDtypeStruct((seqs, length, model), BF16),
            jax.ShapeDtypeStruct((seqs, length, model), BF16),
            jax.ShapeDtypeStruct((seqs, pairs, PAIR * blocks, 2 * span), F32),
        ],
        scratch_shapes=[
            pltpu.VMEM((blocks, tile, 2 * span), F32),
            pltpu.VMEM((blocks, tile, 2 * span), F32),
            pltpu.VMEM((width, length), F32),
            pltpu.VMEM((width, length), F32),
        ],
        compiler_params=pltpu.CompilerParams(vmem_limit_bytes=48 * 1024 * 1024),
        cost_estimate=pl.CostEstimate(
            flops=10 * seqs * span * length * model,
            bytes_accessed=16 * seqs * length * model,
            transcendentals=seqs * head_count * span * length,
        ),
    )(
        projected,
        projected,
        projected,
        grad_attended,
        seg_own[:, :, None],
        seg_all[:, None, :],
        window,
    )


def expert_kernel(
    core_ref,
    x_ref,
    cot_ref,
    gate_ref,
    up_ref,
    down_ref,
    out_ref,
    grad_in_ref,
    grad_up_ref,
    grad_down_ref,
    grad_out,
    out_acc,
    in_acc,
):
    step = pl.program_id(1)
    rows_in = x_ref[0]

    @pl.when(step == 0)
    def _():
        grad_out[...] = (cot_ref[0].astype(F32) * gate_ref[0]).astype(BF16)
        out_acc[...] = jnp.zeros_like(out_acc)
        in_acc[...] = jnp.zeros_like(in_acc)

    grad_rows = grad_out[...]
    up, down = up_ref[0, 0], down_ref[0, 0]
    pre = dot_nt(rows_in, up)
    grad_act = dot_nt(grad_rows, down)
    slope = np.sqrt(2.0 / np.pi).astype(np.float32)
    square = pre * pre
    tanh = jnp.tanh(slope * (pre + 0.044715 * (square * pre)))
    half = 0.5 * (1.0 + tanh)
    act = (pre * half).astype(BF16)
    inner = slope * (1.0 + (3.0 * 0.044715) * square)
    grad_pre = (grad_act * (half + (0.5 * pre) * (1.0 - tanh * tanh) * inner)).astype(BF16)
    grad_down_ref[0] = dot_tn(act, grad_rows).astype(BF16)
    grad_up_ref[0] = dot_tn(grad_pre, rows_in).astype(BF16)
    out_acc[...] += dot_nn(act, down)
    in_acc[...] += dot_nn(grad_pre, up)

    @pl.when(step == pl.num_programs(1) - 1)
    def _():
        out_ref[0] = out_acc[...].astype(BF16)
        grad_in_ref[0] = in_acc[...].astype(BF16)


def run_experts(core, rows_in, cot, gate, up, down, first, count):
    _, slots, model = rows_in.shape
    part = up.shape[2]
    tile = next(t for t in (512, 384, 256, 128, part) if part % t == 0 and slots * t <= 1 << 18 or t == part)
    row_spec = pl.BlockSpec((1, slots, model), lambda e, f, c: (first + e, 0, 0))
    gate_spec = pl.BlockSpec((1, slots, 1), lambda e, f, c: (first + e, 0, 0))
    weight_spec = pl.BlockSpec((1, 1, tile, model), lambda e, f, c: (first + e, c[0], f, 0))
    out_spec = pl.BlockSpec((1, slots, model), lambda e, f, c: (e, 0, 0))
    grad_spec = pl.BlockSpec((1, tile, model), lambda e, f, c: (e, f, 0))
    return pl.pallas_call(
        expert_kernel,
        grid_spec=pltpu.PrefetchScalarGridSpec(
            num_scalar_prefetch=1,
            grid=(count, part // tile),
            in_specs=[row_spec, row_spec, gate_spec, weight_spec, weight_spec],
            out_specs=[out_spec, out_spec, grad_spec, grad_spec],
            scratch_shapes=[
                pltpu.VMEM((slots, model), BF16),
                pltpu.VMEM((slots, model), F32),
                pltpu.VMEM((slots, model), F32),
            ],
        ),
        out_shape=[
            jax.ShapeDtypeStruct((count, slots, model), BF16),
            jax.ShapeDtypeStruct((count, slots, model), BF16),
            jax.ShapeDtypeStruct((count, part, model), BF16),
            jax.ShapeDtypeStruct((count, part, model), BF16),
        ],
        compiler_params=pltpu.CompilerParams(vmem_limit_bytes=56 * 1024 * 1024),
        cost_estimate=pl.CostEstimate(
            flops=12 * count * slots * part * model,
            bytes_accessed=8 * count * part * model,
            transcendentals=count * slots * part,
        ),
    )(core, rows_in, cot, gate, up, down)


def ring_order(chips):
    return list(range(0, chips, 2)) + list(range(chips - 1 - chips % 2, 0, -2))


def ring_sum(parts, place, order):
    chips = len(order)
    hop = [
        (order[i] * CORES + c, order[(i + 1) % chips] * CORES + c)
        for i in range(chips)
        for c in range(CORES)
    ]

    def pick(index):
        return lax.dynamic_index_in_dim(parts, index % chips, 0, keepdims=False)

    held = pick(place)
    for step in range(chips - 1):
        arrived = lax.ppermute(held, "rep", hop)
        held = (arrived.astype(F32) + pick(place - step - 1 + chips).astype(F32)).astype(BF16)
    found = [((place + 1) % chips, held)]
    for step in range(chips - 1):
        held = lax.ppermute(held, "rep", hop)
        found.append(((place - step + chips) % chips, held))
    return found


def swap_cores(values, reps):
    return lax.ppermute(values, "rep", [(r, r ^ 1) for r in range(reps)])


def swap_groups(values):
    return lax.ppermute(values, "grp", [(0, 1), (1, 0)])


def local(
    tokens,
    segment_ids,
    expert_ids,
    rel_bucket,
    query_key_value_weight,
    output_weight,
    router_weight,
    gain_attn,
    gain_ffn,
    rel_table,
    w_up,
    w_down,
    out_grad,
):
    groups = lax.axis_size("grp")
    reps = lax.axis_size("rep")
    chips = reps // CORES
    grp_index = lax.axis_index("grp")
    rep_index = lax.axis_index("rep")
    core, chip = rep_index % CORES, rep_index // CORES
    seqs, span, model = tokens.shape
    length = span * groups
    head_count = rel_table.shape[1]
    buckets = rel_table.shape[0] * groups
    experts = router_weight.shape[1]
    owned = experts // groups
    most = span // 4
    slots = most * seqs
    hidden = w_up.shape[0] // owned
    part = hidden // CORES
    two = groups == 2

    def gather_rotated(values, axis):
        if two:
            return jnp.concatenate([values, swap_groups(values)], axis=axis)
        whole = lax.all_gather(values, "grp", axis=axis, tiled=True)
        return jnp.roll(whole, -grp_index * values.shape[axis], axis=axis)

    def gather_stacked(values):
        if two:
            other = swap_groups(values)
            return jnp.where(
                grp_index == 0, jnp.stack([values, other]), jnp.stack([other, values])
            )
        return lax.all_gather(values, "grp", axis=0)

    def gather_weight(values):
        if not two:
            return lax.all_gather(values, "grp", axis=0, tiled=True)
        rows = values.shape[0]
        piece = rows // CORES
        mine = swap_groups(lax.dynamic_slice_in_dim(values, core * piece, piece, 0))
        theirs = swap_cores(mine, reps)
        whole = jnp.zeros((2 * rows,) + values.shape[1:], values.dtype)
        whole = lax.dynamic_update_slice_in_dim(whole, values, grp_index * rows, 0)
        start = (1 - grp_index) * rows
        whole = lax.dynamic_update_slice_in_dim(whole, mine, start + core * piece, 0)
        return lax.dynamic_update_slice_in_dim(whole, theirs, start + (1 - core) * piece, 0)

    small = jnp.concatenate(
        [router_weight.reshape(-1), gain_attn, gain_ffn, rel_table.reshape(-1)]
    )
    small = gather_stacked(small)
    cuts = np.cumsum([router_weight.size, gain_attn.size, gain_ffn.size]).tolist()
    full_router, full_gain_attn, full_gain_ffn, full_table = jnp.split(small, cuts, axis=1)
    full_router = full_router.reshape(model, experts)
    full_table = full_table.reshape(buckets, head_count)
    gain_one = full_gain_attn.reshape(-1).astype(F32)
    gain_two = full_gain_ffn.reshape(-1).astype(F32)
    full_qkv = gather_weight(query_key_value_weight)
    tokens_all = gather_rotated(tokens, 1)
    seg_all = gather_rotated(segment_ids, 1)
    full_out = gather_weight(output_weight)

    first_expert = grp_index * owned if two else 0
    expert_of = expert_ids[..., 0]
    chosen = expert_of[..., None] == jnp.arange(experts)
    chosen_float = chosen.astype(F32)
    strict_lower = (jnp.arange(span)[:, None] > jnp.arange(span)[None, :]).astype(BF16)
    earlier = jnp.einsum("tu,sue->ste", strict_lower, chosen.astype(BF16), preferred_element_type=F32)
    slot_rank = jnp.sum(earlier * chosen_float, axis=-1).astype(jnp.int32)
    slot_index = (expert_of - first_expert + experts) % experts * most + slot_rank
    in_slot = slot_index[..., None] == jnp.arange(experts * most)
    dispatch = in_slot.astype(BF16)

    def to_slots(rows):
        placed = jnp.einsum("stc,std->csd", dispatch, rows, preferred_element_type=F32)
        return placed.astype(BF16).reshape(experts, slots, model)

    def to_side(placed):
        if two:
            return jnp.concatenate([placed[:owned], swap_groups(placed[owned:])], axis=1)
        moved = lax.all_to_all(
            placed.reshape((groups, owned) + placed.shape[1:]), "grp", 0, 0, tiled=False
        )
        return jnp.moveaxis(moved, 0, 1).reshape((owned, groups * slots) + placed.shape[2:])

    def from_side(rows):
        if two:
            return jnp.concatenate([rows[:, :slots], swap_groups(rows[:, slots:])], axis=0)
        moved = jnp.moveaxis(rows.reshape(owned, groups, slots, model), 1, 0)
        return lax.all_to_all(moved, "grp", 0, 0, tiled=False).reshape(experts, slots, model)

    def to_cores(rows):
        return jnp.concatenate([rows, swap_cores(rows, reps)], axis=1)

    cot_rows = to_cores(to_side(to_slots(out_grad)))

    input_tokens = tokens.astype(F32)
    inverse_one, normed_own = rms_parts(input_tokens, gain_one)
    normed_own = normed_own.astype(BF16)
    normed_all = rms_parts(tokens_all.astype(F32), gain_one)[1].astype(BF16)
    projected = jnp.einsum(
        "std,de->ste", normed_all, full_qkv, preferred_element_type=F32
    ).astype(BF16)

    bucket_hot = (rel_bucket[None, :] == jnp.arange(buckets)[:, None]).astype(BF16)
    bucket_hot = jnp.pad(bucket_hot, ((0, 0), (0, 1)))
    bias_line = jnp.einsum("bh,bo->ho", full_table, bucket_hot, preferred_element_type=F32)
    starts = [
        ((grp_index + b) % groups - grp_index) * span + length - span for b in range(groups)
    ]
    window = jnp.stack(
        [lax.dynamic_slice_in_dim(bias_line, at, 2 * span, 1) for at in starts], axis=1
    ).reshape(head_count // PAIR, PAIR * groups, 2 * span)

    attended = attention(projected, segment_ids, seg_all, window, span, head_count)
    residual = input_tokens + jnp.einsum(
        "std,de->ste", attended, full_out, preferred_element_type=F32
    )
    inverse_two, normed_ffn = rms_parts(residual, gain_two)
    normed_ffn = normed_ffn.astype(BF16)
    router_logits = jnp.einsum(
        "std,de->ste", normed_ffn, full_router, preferred_element_type=F32
    )
    router = jax.nn.softmax(router_logits, axis=-1)
    gate_prob = jnp.sum(router * chosen_float, axis=-1)
    gate_slots = jnp.sum(jnp.where(in_slot, gate_prob[..., None], 0.0), axis=1)
    gate_slots = jnp.moveaxis(gate_slots.reshape(seqs, experts, most), 0, 2).reshape(experts, slots)

    expert_in = to_cores(to_side(to_slots(normed_ffn)))
    gate_rows = to_cores(to_side(gate_slots))[..., None]
    up_parts = w_up.reshape(owned, CORES, part, model)
    down_parts = w_down.reshape(owned, CORES, part, model)
    core_id = core.astype(jnp.int32).reshape(1)
    batches = min(INSTANCES, owned)
    count = owned // batches
    outs, grad_ins, grad_ups, grad_downs = [], [], [], []
    for i in range(batches):
        results = run_experts(
            core_id, expert_in, cot_rows, gate_rows, up_parts, down_parts, i * count, count
        )
        for kept, result in zip((outs, grad_ins, grad_ups, grad_downs), results):
            kept.append(result)

    def finish(partials):
        rows = jnp.concatenate(partials, axis=0)
        near = rows.shape[1] // CORES
        both = rows[:, :near].astype(F32) + swap_cores(rows[:, near:], reps).astype(F32)
        placed = from_side(both.astype(BF16))
        return jnp.einsum(
            "stc,csd->std",
            dispatch,
            placed.reshape(experts * most, seqs, model),
            preferred_element_type=F32,
        )

    order = ring_order(chips)
    shard = part // chips
    gathered = []
    for grads, way in ((grad_ups, order), (grad_downs, order[::-1])):
        place = jnp.asarray(np.argsort(way), jnp.int32)[chip]
        whole = jnp.zeros((owned, CORES, chips, shard, model), F32)
        for i, grad in enumerate(grads):
            parts = jnp.moveaxis(grad.reshape(count, chips, shard, model), 1, 0)
            for index, piece in ring_sum(parts.reshape(chips, count * shard, model), place, way):
                other = swap_cores(piece, reps)
                for at, value in ((core, piece), (1 - core, other)):
                    value = value.astype(F32).reshape(count, 1, 1, shard, model)
                    whole = lax.dynamic_update_slice(whole, value, (i * count, at, index, 0, 0))
        gathered.append(whole.reshape(owned * hidden, model))

    returned = finish(outs)
    layer_out = (residual + gate_prob[..., None] * returned).astype(BF16)
    cotangent = out_grad.astype(F32)
    grad_gate = jnp.sum(cotangent * returned, axis=-1)
    grad_from_experts = finish(grad_ins)
    grad_logits = (grad_gate[..., None] * router * (chosen_float - gate_prob[..., None])).astype(
        BF16
    )
    grad_router = jnp.einsum("std,ste->de", normed_ffn, grad_logits, preferred_element_type=F32)
    grad_normed_ffn = grad_from_experts + jnp.einsum(
        "ste,de->std", grad_logits, full_router, preferred_element_type=F32
    )
    grad_mid, grad_gain_ffn = rms_back(grad_normed_ffn, residual, inverse_two, gain_two)
    grad_residual = cotangent + grad_mid
    grad_attn = grad_residual.astype(BF16)
    grad_wout = jnp.einsum("std,ste->de", attended, grad_attn, preferred_element_type=F32)
    grad_attended = jnp.einsum(
        "ste,de->std", grad_attn, full_out, preferred_element_type=F32
    ).astype(BF16)
    grad_queries, key_terms, value_terms, diagonals = attention_back(
        projected, grad_attended, segment_ids, seg_all, window, span, head_count
    )
    diagonals = jnp.sum(diagonals, axis=0).reshape(head_count, groups, 2 * span)
    hot_window = jnp.stack(
        [lax.dynamic_slice_in_dim(bucket_hot, at, 2 * span, 1) for at in starts], axis=1
    ).astype(F32)
    grad_table = jnp.einsum("bno,hno->bh", hot_window, diagonals, precision=lax.Precision.HIGHEST)

    def own_keys(terms):
        if two:
            return terms[:, :span].astype(F32) + swap_groups(terms[:, span:]).astype(F32)
        terms = jnp.roll(terms, grp_index * span, axis=1)
        return lax.psum_scatter(terms, "grp", scatter_dimension=1, tiled=True)

    grad_keys, grad_values = own_keys(key_terms), own_keys(value_terms)
    grad_mixed = jnp.concatenate(
        [grad_queries, grad_keys.astype(BF16), grad_values.astype(BF16)], axis=-1
    )
    grad_qkv = jnp.einsum("std,ste->de", normed_own, grad_mixed, preferred_element_type=F32)
    grad_normed = jnp.einsum("ste,de->std", grad_mixed, full_qkv, preferred_element_type=F32)
    grad_input_part, grad_gain_attn = rms_back(grad_normed, input_tokens, inverse_one, gain_one)
    tokens_grad = grad_residual + grad_input_part

    shares = tuple(
        lax.psum_scatter(value.astype(BF16), "grp", scatter_dimension=0, tiled=True)
        for value in (grad_qkv, grad_wout, grad_router, grad_gain_attn, grad_gain_ffn, grad_table)
    )
    sums = tuple(value.astype(F32) for value in lax.psum(shares, "rep"))
    return (layer_out, tokens_grad) + sums + tuple(gathered)


def solution(mesh):
    return jax.shard_map(
        local,
        mesh=mesh,
        in_specs=(
            P("rep", "grp", None),
            P("rep", "grp"),
            P("rep", "grp", None),
            P(),
            P("grp", None),
            P("grp", None),
            P("grp", None),
            P("grp"),
            P("grp"),
            P("grp", None),
            P("grp", None),
            P("grp", None),
            P("rep", "grp", None),
        ),
        out_specs=(
            P("rep", "grp", None),
            P("rep", "grp", None),
            P("grp", None),
            P("grp", None),
            P("grp", None),
            P("grp"),
            P("grp"),
            P("grp", None),
            P("grp", None),
            P("grp", None),
        ),
        check_vma=False,
    )
```

time: 2850 us -> 1050 us (0.37)
  waiting for transfers between devices: 2000 us -> 402 us
  local copies, waits for them, and re-layouts: 368 us -> 96.7 us
  matrix products: 245 us -> 33.6 us
  starting transfers between devices: 0.6 us -> 134 us
  other arithmetic: 122 us -> 213 us
  Pallas kernels: 0 us -> 63.9 us
  blocking collectives: 91.6 us -> 62.6 us
    reduce_scatter x7 -> x3, waiting for transfers between devices: 703 us -> 0.01 us  [local(): lax.psum_scatter(value.astype(BF16), 'grp', scatter_dimension=0, tiled=True)]
    all_gather x6 -> x0, waiting for transfers between devices: 677 us -> none  [the longest x1 411 us: local(): lax.all_gather(w_up, 'grp', axis=0, tiled=True)]
    psum x1, waiting for transfers between devices: 607 us -> 54.7 us  [local(): sums = tuple((value.astype(F32) for value in lax.psum(shares, 'rep')))]
    ppermute x0 -> x195, waiting for transfers between devices: none -> 347 us  [the longest x56 198 us: ring_sum(): held = lax.ppermute(held, 'rep', hop)]
    dot_general x27 -> x15, matrix products: 243 us -> 33.1 us  [the longest x1 7.03 us: local(): jnp.einsum('std,de->ste', normed_all, full_qkv, preferred_element_type=F32)]
    reshape x4 -> x6, local copies, waits for them, and re-layouts: 160 us -> 2.12 us  [the longest x1 0.94 us: local(): full_router = full_router.reshape(model, experts)]
    ppermute x0 -> x195, starting transfers between devices: none -> 134 us  [the longest x56 63.9 us: ring_sum(): arrived = lax.ppermute(held, 'rep', hop)]
    dynamic_update_slice x0 -> x128, other arithmetic: none -> 126 us  [local(): whole = lax.dynamic_update_slice(whole, value, (i * count, at, index, 0, 0))]
  transfers between devices with their start and end apart: 15 -> 200, of which waited for: 9 -> 90; matrix products, arithmetic and copies ran while one was open for 21% -> 27% of each run, Pallas kernels for 0% -> 5%
where the time goes in v1:
time: 1050 us; the launch traced here: 1040 us
  waiting for transfers between devices  402 us (38%)
  other arithmetic  213 us (20%)
  starting transfers between devices  134 us (13%)
  local copies, waits for them, and re-layouts  96.7 us (9%)
  Pallas kernels  63.9 us (6%)
  blocking collectives  62.6 us (6%)
  matrix products  33.6 us (3%)
  between operations  31.4 us (3%)
    ppermute x56, waiting for transfers between devices, ring_sum(): held = lax.ppermute(held, 'rep', hop)  198 us
    dynamic_update_slice x128, other arithmetic, local(): whole = lax.dynamic_update_slice(whole, value, (i * count, at, index, 0, 0))  126 us
    ppermute x56, waiting for transfers between devices, ring_sum(): arrived = lax.ppermute(held, 'rep', hop)  109 us
    ppermute x56, starting transfers between devices, ring_sum(): arrived = lax.ppermute(held, 'rep', hop)  63.9 us
    psum x1, blocking collectives, local(): sums = tuple((value.astype(F32) for value in lax.psum(shares, 'rep')))  57.7 us
    psum x1, waiting for transfers between devices, local(): sums = tuple((value.astype(F32) for value in lax.psum(shares, 'rep')))  54.7 us
    ppermute x56, starting transfers between devices, ring_sum(): held = lax.ppermute(held, 'rep', hop)  52.7 us
    ppermute x12, waiting for transfers between devices, swap_groups(): return lax.ppermute(values, 'grp', [(0, 1), (1, 0)])  40.4 us
  transfers between devices with their start and end apart: 200, of which 90 were waited for; matrix products, arithmetic and copies ran while one was open for 27% of the time, Pallas kernels for 5%

profile of v1, /device:TPU:0, one launch (start us, length us, event | category | flops | bytes accessed | tf_op | source)
XLA Modules:
  0.0 1037.6 jit_solution(530091631262395008)
XLA Ops:
  35.0 19.4 %collective-permute-done.4 = s32[1,512]{1,0:T(1,128)S(1)} collective-permute-done((s32[1,512]{1,0:T(1,128)}, s32[1,512]{1,0:T(1,128)S(1)}, u32[]{:S(2)}, u32[]{:S(2)}) %collective-permute-start.4) | collective-permute-done | bytes 2080 | tf_op jit(solution)/shard_map/ppermute | solution.py:349
  62.5 7.0 fusion.q_ref.k_ref.v_ref
  69.6 18.9 %shard_map.222 = bf16[1,512,768]{2,1,0:T(8,128)(2,1)S(1)} custom-call(bf16[1,1024,2304]{2,1,0:T(8,128)(2,1)S(1)} %fusion.q_ref.k_ref.v_ref, bf16[1,1024,2304]{2,1,0:T(8,128)(2,1)S(1)} %fusion.q_ref.k_ref.v_ref, bf16[1,1024,2304]{2,1,0:T(8,128)(2,1)S(1)} %fusion.q_ref.k_ref.v_ref, s32[1,512,1]{2,1,0:T(8,128)S(1)} %copy.49.seg_q_ref, ...), custom_call_target="tpu_custom_call" | custom-call | flops 1610612736 | bytes 6291456 | tf_op jit(solution)/shard_map/pallas_call | solution.py:173
  104.7 14.0 %collective-permute-done.7 = bf16[4,128,768]{2,1,0:T(8,128)(2,1)} collective-permute-done((bf16[4,128,768]{2,1,0:T(8,128)(2,1)}, bf16[4,128,768]{2,1,0:T(8,128)(2,1)}, u32[]{:S(2)}, u32[]{:S(2)}) %collective-permute-start.7) | collective-permute-done | bytes 786464 | tf_op jit(solution)/shard_map/ppermute | solution.py:349
  158.1 13.1 %shard_map.223 = (bf16[1,512,768]{2,1,0:T(8,128)(2,1)}, bf16[1,512,768]{2,1,0:T(8,128)(2,1)}, bf16[1,1536,768]{2,1,0:T(8,128)(2,1)}, bf16[1,1536,768]{2,1,0:T(8,128)(2,1)}) custom-call(s32[1]{0:T(128)} %bitcast.14.core_ref, bf16[4,512,768]{2,1,0:T(8,128)(2,1)} %pad_maximum_fusion.x_ref, bf16[4,512,768]{2,1,0:T(8,128)(2,1)} %pad_maximum_fusion.1.cot_ref, ...), custom_call_target="tpu_custom_call" | custom-call | flops 7247757312 | bytes 9437184 | tf_op jit(solution)/shard_map/pallas_call | solution.py:290
  174.0 12.7 %shard_map.227 = (bf16[4,512,768]{2,1,0:T(8,128)(2,1)}, bf16[1,512,768]{2,1,0:T(8,128)(2,1)}, bf16[1,1536,768]{2,1,0:T(8,128)(2,1)}, bf16[1,1536,768]{2,1,0:T(8,128)(2,1)}) fusion(bf16[4,512,768]{2,1,0:T(8,128)(2,1)} %get-tuple-element.128, s32[1]{0:T(128)} %bitcast.14.core_ref, bf16[4,512,768]{2,1,0:T(8,128)(2,1)} %pad_maximum_fusion.x_ref, ...), kind=kCustom, calls=%fused_computation.363 | custom fusion | flops 7247757312 | bytes 50340352 | tf_op jit(solution)/shard_map/pallas_call | solution.py:290
  186.6 12.9 %shard_map.226 = (bf16[4,512,768]{2,1,0:T(8,128)(2,1)}, bf16[1,512,768]{2,1,0:T(8,128)(2,1)}, bf16[1,1536,768]{2,1,0:T(8,128)(2,1)}, bf16[1,1536,768]{2,1,0:T(8,128)(2,1)}) fusion(bf16[4,512,768]{2,1,0:T(8,128)(2,1)} %get-tuple-element.60, s32[1]{0:T(128)} %bitcast.14.core_ref, bf16[4,512,768]{2,1,0:T(8,128)(2,1)} %pad_maximum_fusion.x_ref, ...), kind=kCustom, calls=%fused_computation.362 | custom fusion | flops 7247757312 | bytes 50340352 | tf_op jit(solution)/shard_map/pallas_call | solution.py:290
  199.5 12.4 %shard_map.225 = (bf16[4,512,768]{2,1,0:T(8,128)(2,1)}, bf16[1,512,768]{2,1,0:T(8,128)(2,1)}, bf16[1,1536,768]{2,1,0:T(8,128)(2,1)}, bf16[1,1536,768]{2,1,0:T(8,128)(2,1)S(1)}) fusion(bf16[4,512,768]{2,1,0:T(8,128)(2,1)} %get-tuple-element.68, s32[1]{0:T(128)} %bitcast.14.core_ref, bf16[4,512,768]{2,1,0:T(8,128)(2,1)} %pad_maximum_fusion.x_ref, ...), kind=kCustom, calls=%fused_computation.361 | custom fusion | flops 7247757312 | bytes 50340352 | tf_op jit(solution)/shard_map/pallas_call | solution.py:290
  289.0 6.2 collective-permute-done.152
  318.6 6.0 collective-permute-done.153
  333.3 6.4 collective-permute-done.66
  348.3 6.2 collective-permute-done.154
  377.8 6.0 collective-permute-done.155
  426.1 12.6 %broadcast.273.clone.1 = f32[4,2,8,192,768]{4,3,2,1,0:T(8,128)} broadcast(f32[]{:T(128)} %constant.596.clone.1), dimensions={} | broadcast | bytes 37748740 | tf_op jit(solution)/shard_map/broadcast.5
  438.7 10.5 %copy-done.5 = f32[4,2,8,192,768]{4,3,2,1,0:T(8,128)} copy-done((f32[4,2,8,192,768]{4,3,2,1,0:T(8,128)}, f32[4,2,8,192,768]{4,3,2,1,0:T(8,128)S(1)}, u32[]{:S(2)}) %copy-start.5) | copy-done | bytes 37748760
  463.8 31.8 %shard_map.224 = (bf16[1,512,768]{2,1,0:T(8,128)(2,1)S(1)}, bf16[1,1024,768]{2,1,0:T(8,128)(2,1)S(1)}, bf16[1,1024,768]{2,1,0:T(8,128)(2,1)S(1)}, f32[1,6,4,1024]{3,2,1,0:T(4,128)S(1)}) custom-call(bf16[1,1024,2304]{2,1,0:T(8,128)(2,1)} %copy-done, bf16[1,1024,2304]{2,1,0:T(8,128)(2,1)} %copy-done, bf16[1,1024,2304]{2,1,0:T(8,128)(2,1)} %copy-done, ...), custom_call_target="tpu_custom_call" | custom-call | flops 4026531840 | bytes 12582912 | tf_op jit(solution)/shard_map/pallas_call | solution.py:201
  535.2 6.1 collective-permute-done.31
  571.6 57.7 %all-reduce.3 = (bf16[384,8]{0,1:T(8,128)(2,1)S(1)}, bf16[384]{0:T(512)(128)(2,1)S(1)}, bf16[384]{0:T(512)(128)(2,1)S(1)}, bf16[16,12]{1,0:T(8,128)(2,1)S(1)}) all-reduce(bf16[384,8]{0,1:T(8,128)(2,1)S(1)} %copy.59, bf16[384]{0:T(512)(128)(2,1)S(1)} %dynamic-slice.1, ...), channel_id=1, replica_groups=mesh['rep'=16,'grp'=2] {'rep'}, use_global_device_ids=true, to_apply=%region_16.17 | all-reduce | flops 4032 | bytes 16128 | tf_op jit(solution)/shard_map/psum | solution.py:582
  636.9 6.4 collective-permute-done.121
  644.9 7.2 collective-permute-done.35
  706.1 6.1 collective-permute-done.137
  929.0 6.4 collective-permute-done.101
  942.9 7.9 collective-permute-done.103
  968.6 54.7 %all-reduce.8.cloned.1.call-done = (bf16[384,2304]{1,0:T(8,128)(2,1)}, bf16[384,768]{1,0:T(8,128)(2,1)}) async-done(((bf16[384,2304]{1,0:T(8,128)(2,1)}, bf16[384,768]{1,0:T(8,128)(2,1)}), (bf16[384,2304]{1,0:T(8,128)(2,1)}, bf16[384,768]{1,0:T(8,128)(2,1)})) %all-reduce.8.cloned.1.call-update) | async-done | bytes 2359312 | tf_op jit(solution)/shard_map/psum | solution.py:582
  (767 shorter events, 657.5 us)
Async XLA Ops:
  7.2 509.5 %reduce-scatter.13.cloned.1.call-start = ((), (), s32[]{:S(2)}) async-start(), calls=%async_computation.7 | async-start | bytes 294912
  8.3 48.3 %collective-permute-start.5 = (bf16[192,768]{1,0:T(8,128)(2,1)S(1)}, bf16[192,768]{1,0:T(8,128)(2,1)S(1)}, u32[]{:S(2)}, u32[]{:S(2)}) collective-permute-start(bf16[192,768]{1,0:T(8,128)(2,1)S(1)} %constant_dynamic-slice_fusion), channel_id=1, source_target_pairs={{0,1},{1,0},{2,3},{3,2},{4,5},{5,4},{6,7},{7,6},{8,9},{9,8},{10,11... | collective-permute-start | bytes 884744 | tf_op jit(solution)/shard_map/ppermute | solution.py:349
  103.3 47.9 %collective-permute-start.10 = (bf16[4,256,768]{2,1,0:T(8,128)(2,1)}, bf16[4,256,768]{2,1,0:T(8,128)(2,1)}, u32[]{:S(2)}, u32[]{:S(2)}) collective-permute-start(bf16[4,256,768]{2,1,0:T(8,128)(2,1)} %pad_maximum_fusion.3), channel_id=1, source_target_pairs={{0,2},{2,0},{4,6},{6,4},{8,10},{10,8},{12,14},{14,12},{16,18},{18,... | collective-permute-start | bytes 4718600 | tf_op jit(solution)/shard_map/ppermute | solution.py:345
  214.4 174.0 %collective-permute-start.13 = (bf16[4,256,768]{2,1,0:T(8,128)(2,1)S(1)}, bf16[4,256,768]{2,1,0:T(8,128)(2,1)S(1)}, u32[]{:S(2)}, u32[]{:S(2)}) collective-permute-start(bf16[4,256,768]{2,1,0:T(8,128)(2,1)S(1)} %slice.103), channel_id=1, source_target_pairs={{0,2},{2,0},{4,6},{6,4},{8,10},{10,8},{12,14},{14,12},{16,18},{18,... | collective-permute-start | bytes 4718600 | tf_op jit(solution)/shard_map/ppermute | solution.py:345
  224.2 166.3 %collective-permute-start.15 = (bf16[4,256,768]{2,1,0:T(8,128)(2,1)S(1)}, bf16[4,256,768]{2,1,0:T(8,128)(2,1)S(1)}, u32[]{:S(2)}, u32[]{:S(2)}) collective-permute-start(bf16[4,256,768]{2,1,0:T(8,128)(2,1)S(1)} %slice.107), channel_id=1, source_target_pairs={{0,2},{2,0},{4,6},{6,4},{8,10},{10,8},{12,14},{14,12},{16,18},{18,... | collective-permute-start | bytes 4718600 | tf_op jit(solution)/shard_map/ppermute | solution.py:345
  403.3 47.8 %collective-permute-start.14 = (bf16[4,128,768]{2,1,0:T(8,128)(2,1)}, bf16[4,128,768]{2,1,0:T(8,128)(2,1)}, u32[]{:S(2)}, u32[]{:S(2)}) collective-permute-start(bf16[4,128,768]{2,1,0:T(8,128)(2,1)} %get-tuple-element.107), channel_id=1, source_target_pairs={{0,1},{1,0},{2,3},{3,2},{4,5},{5,4},{6,7},{7,6},{8,9},{9,8},{10,11... | collective-permute-start | bytes 2359304 | tf_op jit(solution)/shard_map/ppermute | solution.py:349
  404.7 49.6 %collective-permute-start.16 = (bf16[4,128,768]{2,1,0:T(8,128)(2,1)}, bf16[4,128,768]{2,1,0:T(8,128)(2,1)}, u32[]{:S(2)}, u32[]{:S(2)}) collective-permute-start(bf16[4,128,768]{2,1,0:T(8,128)(2,1)} %get-tuple-element.105), channel_id=1, source_target_pairs={{0,1},{1,0},{2,3},{3,2},{4,5},{5,4},{6,7},{7,6},{8,9},{9,8},{10,11... | collective-permute-start | bytes 2359304 | tf_op jit(solution)/shard_map/ppermute | solution.py:349
  413.2 277.9 %collective-permute-start.47 = (bf16[192,768]{1,0:T(8,128)(2,1)}, bf16[192,768]{1,0:T(8,128)(2,1)}, u32[]{:S(2)}, u32[]{:S(2)}) collective-permute-start(bf16[192,768]{1,0:T(8,128)(2,1)} %fusion.109), channel_id=1, source_target_pairs={{0,8},{2,10},{8,16},{10,18},{16,24},{18,26},{24,28},{26,30},{28,20... | collective-permute-start | bytes 884744 | tf_op jit(solution)/shard_map/ppermute | solution.py:335
  424.2 82.8 %collective-permute-start.26 = (bf16[192,768]{1,0:T(8,128)(2,1)}, bf16[192,768]{1,0:T(8,128)(2,1)}, u32[]{:S(2)}, u32[]{:S(2)}) collective-permute-start(bf16[192,768]{1,0:T(8,128)(2,1)} %get-tuple-element.101), channel_id=1, source_target_pairs={{0,2},{2,0},{4,6},{6,4},{8,10},{10,8},{12,14},{14,12},{16,18},{18,... | collective-permute-start | bytes 884744 | tf_op jit(solution)/shard_map/ppermute | solution.py:345
  424.3 85.2 %collective-permute-start.27 = (bf16[192,768]{1,0:T(8,128)(2,1)}, bf16[192,768]{1,0:T(8,128)(2,1)}, u32[]{:S(2)}, u32[]{:S(2)}) collective-permute-start(bf16[192,768]{1,0:T(8,128)(2,1)} %get-tuple-element.101), channel_id=1, source_target_pairs={{0,8},{2,10},{8,16},{10,18},{16,24},{18,26},{24,28},{26,30},{28,20... | collective-permute-start | bytes 884744 | tf_op jit(solution)/shard_map/ppermute | solution.py:339
  451.1 61.6 %collective-permute-start.114 = (bf16[192,768]{1,0:T(8,128)(2,1)}, bf16[192,768]{1,0:T(8,128)(2,1)}, u32[]{:S(2)}, u32[]{:S(2)}) collective-permute-start(bf16[192,768]{1,0:T(8,128)(2,1)} %get-tuple-element.93), channel_id=1, source_target_pairs={{0,2},{2,0},{4,6},{6,4},{8,10},{10,8},{12,14},{14,12},{16,18},{18,... | collective-permute-start | bytes 884744 | tf_op jit(solution)/shard_map/ppermute | solution.py:345
  454.3 60.3 %collective-permute-start.115 = (bf16[192,768]{1,0:T(8,128)(2,1)}, bf16[192,768]{1,0:T(8,128)(2,1)}, u32[]{:S(2)}, u32[]{:S(2)}) collective-permute-start(bf16[192,768]{1,0:T(8,128)(2,1)} %get-tuple-element.93), channel_id=1, source_target_pairs={{4,12},{6,14},{12,20},{14,22},{20,28},{22,30},{28,24},{30,26},{24,... | collective-permute-start | bytes 884744 | tf_op jit(solution)/shard_map/ppermute | solution.py:339
  498.6 73.0 %reduce-scatter.11.cloned.1.call-start = ((), (), s32[]{:S(2)}) async-start(), calls=%async_computation.6 | async-start | bytes 12288 | tf_op jit(solution)/shard_map/reduce_scatter | solution.py:579
  500.6 419.1 %reduce-scatter.9.cloned.1.call-start = ((), (), s32[]{:S(2)}) async-start(), calls=%async_computation.5 | async-start | bytes 1769472 | tf_op jit(solution)/shard_map/reduce_scatter | solution.py:579
  507.0 412.6 %reduce-scatter.7.cloned.1.call-start = ((), (), s32[]{:S(2)}) async-start(), calls=%async_computation.4 | async-start | bytes 5308416 | tf_op jit(solution)/shard_map/reduce_scatter | solution.py:579
  544.8 252.1 %collective-permute-start.69 = (bf16[192,768]{1,0:T(8,128)(2,1)}, bf16[192,768]{1,0:T(8,128)(2,1)}, u32[]{:S(2)}, u32[]{:S(2)}) collective-permute-start(bf16[192,768]{1,0:T(8,128)(2,1)} %fusion.102), channel_id=1, source_target_pairs={{0,8},{2,10},{8,16},{10,18},{16,24},{18,26},{24,28},{26,30},{28,20... | collective-permute-start | bytes 884744 | tf_op jit(solution)/shard_map/ppermute | solution.py:335
  548.3 333.2 %collective-permute-start.91 = (bf16[192,768]{1,0:T(8,128)(2,1)}, bf16[192,768]{1,0:T(8,128)(2,1)}, u32[]{:S(2)}, u32[]{:S(2)}) collective-permute-start(bf16[192,768]{1,0:T(8,128)(2,1)} %fusion.95), channel_id=1, source_target_pairs={{0,8},{2,10},{8,16},{10,18},{16,24},{18,26},{24,28},{26,30},{28,20... | collective-permute-start | bytes 884744 | tf_op jit(solution)/shard_map/ppermute | solution.py:335
  549.5 82.2 %collective-permute-start.32 = (bf16[192,768]{1,0:T(8,128)(2,1)}, bf16[192,768]{1,0:T(8,128)(2,1)}, u32[]{:S(2)}, u32[]{:S(2)}) collective-permute-start(bf16[192,768]{1,0:T(8,128)(2,1)} %collective-permute-done.31), channel_id=1, source_target_pairs={{0,2},{2,0},{4,6},{6,4},{8,10},{10,8},{12,14},{14,12},{16,18},{18,... | collective-permute-start | bytes 884744 | tf_op jit(solution)/shard_map/ppermute | solution.py:345
  556.7 76.9 %collective-permute-start.33 = (bf16[192,768]{1,0:T(8,128)(2,1)}, bf16[192,768]{1,0:T(8,128)(2,1)}, u32[]{:S(2)}, u32[]{:S(2)}) collective-permute-start(bf16[192,768]{1,0:T(8,128)(2,1)} %collective-permute-done.31), channel_id=1, source_target_pairs={{0,8},{2,10},{8,16},{10,18},{16,24},{18,26},{24,28},{26,30},{28,20... | collective-permute-start | bytes 884744 | tf_op jit(solution)/shard_map/ppermute | solution.py:339
  631.6 391.7 %all-reduce.8.cloned.1.call-start = ((), (), s32[]{:S(2)}) async-start(), calls=%async_computation.8 | async-start | bytes 4718592 | tf_op jit(solution)/shard_map/psum | solution.py:582
  691.0 110.4 %collective-permute-start.157 = (bf16[192,768]{1,0:T(8,128)(2,1)}, bf16[192,768]{1,0:T(8,128)(2,1)S(1)}, u32[]{:S(2)}, u32[]{:S(2)}) collective-permute-start(bf16[192,768]{1,0:T(8,128)(2,1)} %fusion.74), channel_id=1, source_target_pairs={{4,12},{6,14},{12,20},{14,22},{20,28},{22,30},{28,24},{30,26},{24,... | collective-permute-start | bytes 884744 | tf_op jit(solution)/shard_map/ppermute | solution.py:335
  794.3 91.7 %collective-permute-start.179 = (bf16[192,768]{1,0:T(8,128)(2,1)S(1)}, bf16[192,768]{1,0:T(8,128)(2,1)S(1)}, u32[]{:S(2)}, u32[]{:S(2)}) collective-permute-start(bf16[192,768]{1,0:T(8,128)(2,1)S(1)} %copy-done.28), channel_id=1, source_target_pairs={{4,12},{6,14},{12,20},{14,22},{20,28},{22,30},{28,24},{30,26},{24,... | collective-permute-start | bytes 884744 | tf_op jit(solution)/shard_map/ppermute | solution.py:335
  961.0 68.0 %collective-permute-start.106 = (bf16[192,768]{1,0:T(8,128)(2,1)S(1)}, bf16[192,768]{1,0:T(8,128)(2,1)S(1)}, u32[]{:S(2)}, u32[]{:S(2)}) collective-permute-start(bf16[192,768]{1,0:T(8,128)(2,1)S(1)} %collective-permute-done.105), channel_id=1, source_target_pairs={{0,2},{2,0},{4,6},{6,4},{8,10},{10,8},{12,14},{14,12},{16,18},{18,... | collective-permute-start | bytes 884744 | tf_op jit(solution)/shard_map/ppermute | solution.py:345
  965.2 64.6 %collective-permute-start.194 = (bf16[192,768]{1,0:T(8,128)(2,1)S(1)}, bf16[192,768]{1,0:T(8,128)(2,1)S(1)}, u32[]{:S(2)}, u32[]{:S(2)}) collective-permute-start(bf16[192,768]{1,0:T(8,128)(2,1)S(1)} %collective-permute-done.193), channel_id=1, source_target_pairs={{0,2},{2,0},{4,6},{6,4},{8,10},{10,8},{12,14},{14,12},{16,18},{18,... | collective-permute-start | bytes 884744 | tf_op jit(solution)/shard_map/ppermute | solution.py:345
  (217 other events, 4073.7 us)
Sparse Core Ops, SparseCore 0:
  498.7 9.5 reduce-scatter.12
  511.1 9.8 reduce-scatter.10
  523.8 33.8 reduce-scatter.8
  631.8 44.0 reduce-scatter.6
  919.8 103.4 all-reduce.7

commit v2 on v1

--- a/solution.py
+++ b/solution.py
@@ -12,7 +12,6 @@
 neg_fill = -1e30
 CORES = 2
 PAIR = 2
-INSTANCES = 4
 F32 = jnp.float32
 BF16 = jnp.bfloat16
 
@@ -233,29 +232,28 @@
 
 
 def expert_kernel(
+    pieces,
     core_ref,
-    x_ref,
-    cot_ref,
-    gate_ref,
-    up_ref,
-    down_ref,
-    out_ref,
-    grad_in_ref,
-    grad_up_ref,
-    grad_down_ref,
-    grad_out,
-    out_acc,
-    in_acc,
+    *refs,
 ):
+    x_refs, cot_refs, gate_refs = (refs[i * pieces : (i + 1) * pieces] for i in range(3))
+    up_ref, down_ref, out_ref, grad_in_ref, grad_up_ref, grad_down_ref = refs[3 * pieces : -4]
+    rows_all, grad_out, out_acc, in_acc = refs[-4:]
     step = pl.program_id(1)
-    rows_in = x_ref[0]
 
     @pl.when(step == 0)
     def _():
-        grad_out[...] = (cot_ref[0].astype(F32) * gate_ref[0]).astype(BF16)
+        start = 0
+        for x_ref, cot_ref, gate_ref in zip(x_refs, cot_refs, gate_refs):
+            rows = slice(start, start + x_ref.shape[1])
+            start = rows.stop
+            rows_all[rows, :] = x_ref[0]
+            gate = jnp.broadcast_to(gate_ref[0], (128, x_ref.shape[1])).T[:, :1]
+            grad_out[rows, :] = (cot_ref[0].astype(F32) * gate).astype(BF16)
         out_acc[...] = jnp.zeros_like(out_acc)
         in_acc[...] = jnp.zeros_like(in_acc)
 
+    rows_in = rows_all[...]
     grad_rows = grad_out[...]
     up, down = up_ref[0, 0], down_ref[0, 0]
     pre = dot_nt(rows_in, up)
@@ -279,22 +277,26 @@
 
 
 def run_experts(core, rows_in, cot, gate, up, down, first, count):
-    _, slots, model = rows_in.shape
+    model = rows_in[0].shape[2]
+    sizes = [piece.shape[1] for piece in rows_in]
+    slots = sum(sizes)
     part = up.shape[2]
-    tile = next(t for t in (512, 384, 256, 128, part) if part % t == 0 and slots * t <= 1 << 18 or t == part)
-    row_spec = pl.BlockSpec((1, slots, model), lambda e, f, c: (first + e, 0, 0))
-    gate_spec = pl.BlockSpec((1, slots, 1), lambda e, f, c: (first + e, 0, 0))
+    fits = [t for t in (512, 384, 256, 128) if part % t == 0 and slots * t <= 1 << 18]
+    tile = (fits + [part])[0]
+    row_specs = [pl.BlockSpec((1, n, model), lambda e, f, c: (first + e, 0, 0)) for n in sizes]
+    gate_specs = [pl.BlockSpec((1, 1, n), lambda e, f, c: (first + e, 0, 0)) for n in sizes]
     weight_spec = pl.BlockSpec((1, 1, tile, model), lambda e, f, c: (first + e, c[0], f, 0))
     out_spec = pl.BlockSpec((1, slots, model), lambda e, f, c: (e, 0, 0))
     grad_spec = pl.BlockSpec((1, tile, model), lambda e, f, c: (e, f, 0))
     return pl.pallas_call(
-        expert_kernel,
+        functools.partial(expert_kernel, len(sizes)),
         grid_spec=pltpu.PrefetchScalarGridSpec(
             num_scalar_prefetch=1,
             grid=(count, part // tile),
-            in_specs=[row_spec, row_spec, gate_spec, weight_spec, weight_spec],
+            in_specs=row_specs + row_specs + gate_specs + [weight_spec, weight_spec],
             out_specs=[out_spec, out_spec, grad_spec, grad_spec],
             scratch_shapes=[
+                pltpu.VMEM((slots, model), BF16),
                 pltpu.VMEM((slots, model), BF16),
                 pltpu.VMEM((slots, model), F32),
                 pltpu.VMEM((slots, model), F32),
@@ -312,37 +314,60 @@
             bytes_accessed=8 * count * part * model,
             transcendentals=count * slots * part,
         ),
-    )(core, rows_in, cot, gate, up, down)
-
-
-def ring_order(chips):
-    return list(range(0, chips, 2)) + list(range(chips - 1 - chips % 2, 0, -2))
-
-
-def ring_sum(parts, place, order):
-    chips = len(order)
-    hop = [
-        (order[i] * CORES + c, order[(i + 1) % chips] * CORES + c)
-        for i in range(chips)
-        for c in range(CORES)
-    ]
-
-    def pick(index):
-        return lax.dynamic_index_in_dim(parts, index % chips, 0, keepdims=False)
-
-    held = pick(place)
-    for step in range(chips - 1):
-        arrived = lax.ppermute(held, "rep", hop)
-        held = (arrived.astype(F32) + pick(place - step - 1 + chips).astype(F32)).astype(BF16)
-    found = [((place + 1) % chips, held)]
-    for step in range(chips - 1):
-        held = lax.ppermute(held, "rep", hop)
-        found.append(((place - step + chips) % chips, held))
-    return found
+    )(core, *rows_in, *cot, *gate, up, down)
+
+
+class Ring:
+    def __init__(self, parts, chip, forward):
+        self.parts = parts
+        self.chips = chips = parts.shape[1]
+        order = list(range(0, chips, 2)) + list(range(chips - 1 - chips % 2, 0, -2))
+        self.place = jnp.where(chip % 2 == 0, chip // 2, chips - 1 - chip // 2)
+        if not forward:
+            order, self.place = order[::-1], chips - 1 - self.place
+        self.hop = [
+            (order[i] * CORES + c, order[(i + 1) % chips] * CORES + c)
+            for i in range(chips)
+            for c in range(CORES)
+        ]
+        self.held = self.pick(0)
+
+    def index(self, ahead):
+        return (self.place + ahead + self.chips) % self.chips
+
+    def pick(self, ahead):
+        return lax.dynamic_slice_in_dim(self.parts, self.index(ahead), 1, 1)
+
+    def move(self):
+        return lax.ppermute(self.held, "rep", self.hop)
+
+    def take(self, step, arrived):
+        if step < self.chips - 1:
+            arrived = (arrived.astype(F32) + self.pick(-step - 1).astype(F32)).astype(BF16)
+        self.held = arrived
+
+
+def tie(rings, values):
+    held, values = lax.optimization_barrier(([ring.held for ring in rings], values))
+    for ring, kept in zip(rings, held):
+        ring.held = kept
+    return values
+
+
+def fresh(shape, amount):
+    return pl.pallas_call(
+        lambda *refs: None,
+        out_shape=[jax.ShapeDtypeStruct(shape, F32) for _ in range(amount)],
+        out_specs=[pl.BlockSpec(memory_space=pl.ANY) for _ in range(amount)],
+    )()
+
+
+def swap_reps(values, reps, bit):
+    return lax.ppermute(values, "rep", [(r, r ^ bit) for r in range(reps)])
 
 
 def swap_cores(values, reps):
-    return lax.ppermute(values, "rep", [(r, r ^ 1) for r in range(reps)])
+    return swap_reps(values, reps, 1)
 
 
 def swap_groups(values):
@@ -396,18 +421,28 @@
             )
         return lax.all_gather(values, "grp", axis=0)
 
-    def gather_weight(values):
+    def gather_weight(values, after=None):
         if not two:
             return lax.all_gather(values, "grp", axis=0, tiled=True)
         rows = values.shape[0]
-        piece = rows // CORES
-        mine = swap_groups(lax.dynamic_slice_in_dim(values, core * piece, piece, 0))
-        theirs = swap_cores(mine, reps)
+        sharers = 4 if reps % 4 == 0 and rows % 64 == 0 else 2
+        piece = rows // sharers
+        place = rep_index % sharers
+        pieces = {0: swap_groups(lax.dynamic_slice_in_dim(values, place * piece, piece, 0))}
+        if sharers == 4:
+            pieces[2] = swap_reps(pieces[0], reps, 2)
+            if after is not None:
+                pieces[2], after[0] = lax.optimization_barrier((pieces[2], after[0]))
+        for bit in list(pieces):
+            pieces[bit | 1] = swap_cores(pieces[bit], reps)
         whole = jnp.zeros((2 * rows,) + values.shape[1:], values.dtype)
         whole = lax.dynamic_update_slice_in_dim(whole, values, grp_index * rows, 0)
         start = (1 - grp_index) * rows
-        whole = lax.dynamic_update_slice_in_dim(whole, mine, start + core * piece, 0)
-        return lax.dynamic_update_slice_in_dim(whole, theirs, start + (1 - core) * piece, 0)
+        for bit, fetched in pieces.items():
+            whole = lax.dynamic_update_slice_in_dim(
+                whole, fetched, start + (place ^ bit) * piece, 0
+            )
+        return whole
 
     small = jnp.concatenate(
         [router_weight.reshape(-1), gain_attn, gain_ffn, rel_table.reshape(-1)]
@@ -419,10 +454,10 @@
     full_table = full_table.reshape(buckets, head_count)
     gain_one = full_gain_attn.reshape(-1).astype(F32)
     gain_two = full_gain_ffn.reshape(-1).astype(F32)
-    full_qkv = gather_weight(query_key_value_weight)
-    tokens_all = gather_rotated(tokens, 1)
     seg_all = gather_rotated(segment_ids, 1)
-    full_out = gather_weight(output_weight)
+    arriving = [gather_rotated(tokens, 1)]
+    full_qkv = gather_weight(query_key_value_weight, arriving)
+    tokens_all = arriving[0]
 
     first_expert = grp_index * owned if two else 0
     expert_of = expert_ids[..., 0]
@@ -439,24 +474,24 @@
         placed = jnp.einsum("stc,std->csd", dispatch, rows, preferred_element_type=F32)
         return placed.astype(BF16).reshape(experts, slots, model)
 
-    def to_side(placed):
+    def to_side(*arrays):
         if two:
-            return jnp.concatenate([placed[:owned], swap_groups(placed[owned:])], axis=1)
-        moved = lax.all_to_all(
-            placed.reshape((groups, owned) + placed.shape[1:]), "grp", 0, 0, tiled=False
-        )
-        return jnp.moveaxis(moved, 0, 1).reshape((owned, groups * slots) + placed.shape[2:])
+            far = lax.optimization_barrier([swap_groups(placed[owned:]) for placed in arrays])
+            near = [[placed[:owned], other] for placed, other in zip(arrays, far)]
+        else:
+            near = []
+            for placed in arrays:
+                split = placed.reshape((groups, owned) + placed.shape[1:])
+                moved = lax.all_to_all(split, "grp", 0, 0, tiled=False)
+                near.append([moved[i] for i in range(groups)])
+        both = [pieces + [swap_cores(piece, reps) for piece in pieces] for pieces in near]
+        return both if len(both) > 1 else both[0]
 
     def from_side(rows):
         if two:
             return jnp.concatenate([rows[:, :slots], swap_groups(rows[:, slots:])], axis=0)
         moved = jnp.moveaxis(rows.reshape(owned, groups, slots, model), 1, 0)
         return lax.all_to_all(moved, "grp", 0, 0, tiled=False).reshape(experts, slots, model)
-
-    def to_cores(rows):
-        return jnp.concatenate([rows, swap_cores(rows, reps)], axis=1)
-
-    cot_rows = to_cores(to_side(to_slots(out_grad)))
 
     input_tokens = tokens.astype(F32)
     inverse_one, normed_own = rms_parts(input_tokens, gain_one)
@@ -466,15 +501,25 @@
         "std,de->ste", normed_all, full_qkv, preferred_element_type=F32
     ).astype(BF16)
 
-    bucket_hot = (rel_bucket[None, :] == jnp.arange(buckets)[:, None]).astype(BF16)
-    bucket_hot = jnp.pad(bucket_hot, ((0, 0), (0, 1)))
-    bias_line = jnp.einsum("bh,bo->ho", full_table, bucket_hot, preferred_element_type=F32)
+    bucket_line = jnp.pad(rel_bucket, (0, 1), constant_values=buckets)
     starts = [
         ((grp_index + b) % groups - grp_index) * span + length - span for b in range(groups)
     ]
-    window = jnp.stack(
-        [lax.dynamic_slice_in_dim(bias_line, at, 2 * span, 1) for at in starts], axis=1
+    bucket_window = jnp.stack(
+        [lax.dynamic_slice_in_dim(bucket_line, at, 2 * span, 0) for at in starts]
+    )
+    bucket_hot = bucket_window[None] == jnp.arange(buckets)[:, None, None]
+    bucket_hot = bucket_hot.reshape(buckets, groups * 2 * span)
+    window = jnp.einsum(
+        "bh,bo->ho", full_table, bucket_hot.astype(BF16), preferred_element_type=F32
     ).reshape(head_count // PAIR, PAIR * groups, 2 * span)
+
+    cot_slots = to_slots(out_grad)
+    projected, late_out, cot_slots = lax.optimization_barrier(
+        (projected, output_weight, cot_slots)
+    )
+    full_out = gather_weight(late_out)
+    cot_rows = to_side(cot_slots)
 
     attended = attention(projected, segment_ids, seg_all, window, span, head_count)
     residual = input_tokens + jnp.einsum(
@@ -490,26 +535,84 @@
     gate_slots = jnp.sum(jnp.where(in_slot, gate_prob[..., None], 0.0), axis=1)
     gate_slots = jnp.moveaxis(gate_slots.reshape(seqs, experts, most), 0, 2).reshape(experts, slots)
 
-    expert_in = to_cores(to_side(to_slots(normed_ffn)))
-    gate_rows = to_cores(to_side(gate_slots))[..., None]
+    expert_in, gate_rows = to_side(to_slots(normed_ffn), gate_slots[:, None, :])
     up_parts = w_up.reshape(owned, CORES, part, model)
     down_parts = w_down.reshape(owned, CORES, part, model)
-    core_id = core.astype(jnp.int32).reshape(1)
-    batches = min(INSTANCES, owned)
-    count = owned // batches
-    outs, grad_ins, grad_ups, grad_downs = [], [], [], []
-    for i in range(batches):
-        results = run_experts(
-            core_id, expert_in, cot_rows, gate_rows, up_parts, down_parts, i * count, count
+    shard = part // chips
+
+    sets, outs, grad_ins = [], [], []
+    amounts = [owned]
+    for i, count in enumerate(amounts):
+        first = sum(amounts[:i])
+        out, grad_in, grad_up, grad_down = run_experts(
+            core.astype(jnp.int32).reshape(1),
+            expert_in,
+            cot_rows,
+            gate_rows,
+            up_parts,
+            down_parts,
+            first,
+            count,
         )
-        for kept, result in zip((outs, grad_ins, grad_ups, grad_downs), results):
-            kept.append(result)
-
-    def finish(partials):
-        rows = jnp.concatenate(partials, axis=0)
-        near = rows.shape[1] // CORES
-        both = rows[:, :near].astype(F32) + swap_cores(rows[:, near:], reps).astype(F32)
-        placed = from_side(both.astype(BF16))
+        outs.append(out)
+        grad_ins.append(grad_in)
+        rings = [
+            Ring(grad.reshape(count, chips, shard, model), chip, forward)
+            for grad, forward in ((grad_up, True), (grad_down, False))
+        ]
+        if i + 1 < len(amounts):
+            expert_in = tie(rings, expert_in)
+        sets.append((first, rings))
+    total_rounds = 2 * (chips - 1)
+    rounds = iter(range(total_rounds))
+
+    def swap_held(held):
+        return [[swap_cores(piece, reps) for piece in pieces] for pieces in held]
+
+    def store(wholes, held, others, ahead):
+        stored = list(wholes)
+        for (first, rings), pieces, swapped in zip(sets, held, others):
+            for i, (ring, piece, other) in enumerate(zip(rings, pieces, swapped)):
+                for at, value in ((core, piece), (1 - core, other)):
+                    stored[i] = lax.dynamic_update_slice(
+                        stored[i],
+                        value.astype(F32)[:, None],
+                        (first, at, ring.index(ahead), 0, 0),
+                    )
+        return stored
+
+    wholes = []
+
+    def beside(stage=None, ins=()):
+        step = next(rounds, None)
+        if step is None:
+            return stage(*ins) if stage else ()
+        ins, kept = tie(sets[-1][1], (ins, list(wholes)))
+        held = [[ring.held for ring in rings] for _, rings in sets]
+        arrived = [[ring.move() for ring in rings] for _, rings in sets]
+        if step == chips - 2:
+            kept = list(fresh((owned, CORES, chips, shard, model), 2))
+        if step >= chips - 1:
+            others, ins = lax.optimization_barrier((swap_held(held), ins))
+            kept = store(kept, held, others, chips - step)
+        results = stage(*ins) if stage else ()
+        arrived[0], results, kept = lax.optimization_barrier((arrived[0], results, kept))
+        for (_, rings), values in zip(sets, arrived):
+            for ring, value in zip(rings, values):
+                ring.take(step, value)
+        wholes[:] = kept
+        return results
+
+    def side_sums(outs, grad_ins):
+        sums = []
+        for rows in (outs, grad_ins):
+            rows = jnp.concatenate(rows, axis=0)
+            near = rows.shape[1] // CORES
+            both = rows[:, :near].astype(F32) + swap_cores(rows[:, near:], reps).astype(F32)
+            sums.append(both.astype(BF16))
+        return from_side(sums[0]), sums[1]
+
+    def to_tokens(placed):
         return jnp.einsum(
             "stc,csd->std",
             dispatch,
@@ -517,70 +620,170 @@
             preferred_element_type=F32,
         )
 
-    order = ring_order(chips)
-    shard = part // chips
-    gathered = []
-    for grads, way in ((grad_ups, order), (grad_downs, order[::-1])):
-        place = jnp.asarray(np.argsort(way), jnp.int32)[chip]
-        whole = jnp.zeros((owned, CORES, chips, shard, model), F32)
-        for i, grad in enumerate(grads):
-            parts = jnp.moveaxis(grad.reshape(count, chips, shard, model), 1, 0)
-            for index, piece in ring_sum(parts.reshape(chips, count * shard, model), place, way):
-                other = swap_cores(piece, reps)
-                for at, value in ((core, piece), (1 - core, other)):
-                    value = value.astype(F32).reshape(count, 1, 1, shard, model)
-                    whole = lax.dynamic_update_slice(whole, value, (i * count, at, index, 0, 0))
-        gathered.append(whole.reshape(owned * hidden, model))
-
-    returned = finish(outs)
-    layer_out = (residual + gate_prob[..., None] * returned).astype(BF16)
     cotangent = out_grad.astype(F32)
-    grad_gate = jnp.sum(cotangent * returned, axis=-1)
-    grad_from_experts = finish(grad_ins)
-    grad_logits = (grad_gate[..., None] * router * (chosen_float - gate_prob[..., None])).astype(
-        BF16
-    )
-    grad_router = jnp.einsum("std,ste->de", normed_ffn, grad_logits, preferred_element_type=F32)
-    grad_normed_ffn = grad_from_experts + jnp.einsum(
-        "ste,de->std", grad_logits, full_router, preferred_element_type=F32
-    )
-    grad_mid, grad_gain_ffn = rms_back(grad_normed_ffn, residual, inverse_two, gain_two)
-    grad_residual = cotangent + grad_mid
-    grad_attn = grad_residual.astype(BF16)
-    grad_wout = jnp.einsum("std,ste->de", attended, grad_attn, preferred_element_type=F32)
-    grad_attended = jnp.einsum(
-        "ste,de->std", grad_attn, full_out, preferred_element_type=F32
-    ).astype(BF16)
-    grad_queries, key_terms, value_terms, diagonals = attention_back(
-        projected, grad_attended, segment_ids, seg_all, window, span, head_count
-    )
-    diagonals = jnp.sum(diagonals, axis=0).reshape(head_count, groups, 2 * span)
-    hot_window = jnp.stack(
-        [lax.dynamic_slice_in_dim(bucket_hot, at, 2 * span, 1) for at in starts], axis=1
-    ).astype(F32)
-    grad_table = jnp.einsum("bno,hno->bh", hot_window, diagonals, precision=lax.Precision.HIGHEST)
+
+    def ffn_end(placed, grad_sums):
+        grad_placed = from_side(grad_sums)
+        returned = to_tokens(placed)
+        layer_out = (residual + gate_prob[..., None] * returned).astype(BF16)
+        grad_gate = jnp.sum(cotangent * returned, axis=-1)
+        grad_logits = grad_gate[..., None] * router * (chosen_float - gate_prob[..., None])
+        grad_logits = grad_logits.astype(BF16)
+        grad_router = jnp.einsum("std,ste->de", normed_ffn, grad_logits, preferred_element_type=F32)
+        grad_normed_ffn = to_tokens(grad_placed) + jnp.einsum(
+            "ste,de->std", grad_logits, full_router, preferred_element_type=F32
+        )
+        grad_mid, grad_gain_ffn = rms_back(grad_normed_ffn, residual, inverse_two, gain_two)
+        grad_residual = cotangent + grad_mid
+        grad_attn = grad_residual.astype(BF16)
+        grad_attended = jnp.einsum(
+            "ste,de->std", grad_attn, full_out, preferred_element_type=F32
+        ).astype(BF16)
+        return layer_out, grad_router, grad_gain_ffn, grad_residual, grad_attn, grad_attended
+
+    def scores_back(grad_attended):
+        return attention_back(
+            projected, grad_attended, segment_ids, seg_all, window, span, head_count
+        )
 
     def own_keys(terms):
         if two:
-            return terms[:, :span].astype(F32) + swap_groups(terms[:, span:]).astype(F32)
+            total = terms[:, :span].astype(F32) + swap_groups(terms[:, span:]).astype(F32)
+            return total.astype(BF16)
         terms = jnp.roll(terms, grp_index * span, axis=1)
         return lax.psum_scatter(terms, "grp", scatter_dimension=1, tiled=True)
 
-    grad_keys, grad_values = own_keys(key_terms), own_keys(value_terms)
-    grad_mixed = jnp.concatenate(
-        [grad_queries, grad_keys.astype(BF16), grad_values.astype(BF16)], axis=-1
-    )
-    grad_qkv = jnp.einsum("std,ste->de", normed_own, grad_mixed, preferred_element_type=F32)
-    grad_normed = jnp.einsum("ste,de->std", grad_mixed, full_qkv, preferred_element_type=F32)
-    grad_input_part, grad_gain_attn = rms_back(grad_normed, input_tokens, inverse_one, gain_one)
-    tokens_grad = grad_residual + grad_input_part
-
-    shares = tuple(
-        lax.psum_scatter(value.astype(BF16), "grp", scatter_dimension=0, tiled=True)
-        for value in (grad_qkv, grad_wout, grad_router, grad_gain_attn, grad_gain_ffn, grad_table)
-    )
-    sums = tuple(value.astype(F32) for value in lax.psum(shares, "rep"))
-    return (layer_out, tokens_grad) + sums + tuple(gathered)
+    def keys_end(key_terms, diagonals, grad_attn):
+        grad_wout = jnp.einsum("std,ste->de", attended, grad_attn, preferred_element_type=F32)
+        diagonals = jnp.sum(diagonals, axis=0).reshape(head_count, groups * 2 * span)
+        grad_table = jnp.einsum(
+            "bo,ho->bh", bucket_hot.astype(F32), diagonals, precision=lax.Precision.HIGHEST
+        )
+        return own_keys(key_terms), grad_table, grad_wout
+
+    def projection_back(grad_queries, grad_keys, value_terms, grad_residual):
+        grad_values = own_keys(value_terms)
+        grad_mixed = jnp.concatenate([grad_queries, grad_keys, grad_values], axis=-1)
+        grad_qkv = jnp.einsum("std,ste->de", normed_own, grad_mixed, preferred_element_type=F32)
+        grad_normed = jnp.einsum("ste,de->std", grad_mixed, full_qkv, preferred_element_type=F32)
+        grad_input_part, grad_gain_attn = rms_back(
+            grad_normed, input_tokens, inverse_one, gain_one
+        )
+        return grad_qkv.astype(BF16), grad_gain_attn, grad_residual + grad_input_part
+
+    placed, grad_sums = beside(side_sums, (outs, grad_ins))
+    layer_out, grad_router, grad_gain_ffn, grad_residual, grad_attn, grad_attended = beside(
+        ffn_end, (placed, grad_sums)
+    )
+    grad_queries, key_terms, value_terms, diagonals = beside(scores_back, (grad_attended,))
+    grad_keys, grad_table, grad_wout = beside(keys_end, (key_terms, diagonals, grad_attn))
+    grad_qkv, grad_gain_attn, tokens_grad = beside(
+        projection_back, (grad_queries, grad_keys, value_terms, grad_residual)
+    )
+
+    tiny = (grad_router, grad_gain_attn, grad_gain_ffn, grad_table)
+    tiny = [value.astype(BF16).reshape(groups, -1) for value in tiny]
+    tiny_cuts = np.cumsum([value.shape[1] for value in tiny]).tolist()
+    flat = jnp.concatenate(tiny, axis=1)
+    flat = jnp.pad(flat, ((0, 0), (0, -flat.shape[1] % model))).reshape(groups, -1, model)
+    rows_out = model // groups
+    rows_qkv = 3 * rows_out
+    rows_all = rows_qkv + rows_out + flat.shape[1]
+    packed = jnp.concatenate(
+        [
+            grad_qkv.astype(BF16).reshape(groups, -1, model),
+            grad_wout.astype(BF16).reshape(groups, -1, model),
+            jnp.pad(flat, ((0, 0), (0, -rows_all % (reps * 8)), (0, 0))),
+        ],
+        axis=1,
+    )
+    packed = packed.reshape(groups, CORES, -1, model)
+
+    def halve(values, axis, place, swap):
+        mine = lax.dynamic_index_in_dim(values, place, axis, keepdims=False)
+        given = swap(lax.dynamic_index_in_dim(values, 1 - place, axis, keepdims=False))
+        return (mine.astype(F32) + given.astype(F32)).astype(BF16)
+
+    def share(packed):
+        values = halve(packed, 1, core, lambda v: swap_cores(v, reps))
+        if two:
+            return halve(values, 0, grp_index, swap_groups)
+        return lax.psum_scatter(values, "grp", scatter_dimension=0, tiled=False)
+
+    parts = beside(share, (packed,)).reshape(chips, -1, model)
+
+    upward, downward = chips // 2, chips - 1 - chips // 2
+    place, up_hop, down_hop = rings[0].place, rings[0].hop, rings[1].hop
+
+    def pick(ahead):
+        index = (place + ahead + chips) % chips
+        return lax.dynamic_index_in_dim(parts, index, 0, keepdims=False).astype(F32)
+
+    def put(whole, value, ahead):
+        index = (place + ahead + chips) % chips
+        return lax.dynamic_update_slice_in_dim(whole, value[None], index, 0)
+
+    def reduce_stage(step):
+        def stage(above, below):
+            above = lax.ppermute(above, "rep", up_hop)
+            if step < upward - 1:
+                above = (above.astype(F32) + pick(upward - 1 - step)).astype(BF16)
+            if step < downward:
+                below = lax.ppermute(below, "rep", down_hop)
+            if step < downward - 1:
+                below = (below.astype(F32) + pick(step + 1 - downward)).astype(BF16)
+            return above, below
+
+        return stage
+
+    def gather_stage(step):
+        def stage(above, below, whole):
+            above = lax.ppermute(above, "rep", up_hop)
+            whole = put(whole, above, -1 - step)
+            if step < downward:
+                below = lax.ppermute(below, "rep", down_hop)
+                whole = put(whole, below, 1 + step)
+            return above, below, whole
+
+        return stage
+
+    above, below = pick(upward).astype(BF16), pick(-downward).astype(BF16)
+    for step in range(upward):
+        above, below = beside(reduce_stage(step), (above, below))
+    own_sum = (above.astype(F32) + below.astype(F32) + pick(0)).astype(BF16)
+    above = below = own_sum
+    whole = put(jnp.zeros_like(parts), own_sum, 0)
+    for step in range(upward):
+        above, below, whole = beside(gather_stage(step), (above, below, whole))
+    whole = whole.reshape(1, -1, model)
+    others = swap_cores(whole, reps)
+    sums = jnp.where(
+        core == 0,
+        jnp.concatenate([whole, others], axis=0),
+        jnp.concatenate([others, whole], axis=0),
+    )
+    for _ in range(total_rounds - 6 - 2 * upward):
+        beside()
+
+    def unpack(sums):
+        sums = sums.reshape(-1, model)
+        tiny = jnp.split(
+            sums[rows_qkv + rows_out : rows_all].astype(F32).reshape(-1), tiny_cuts
+        )
+        return (
+            sums[:rows_qkv].astype(F32).reshape(model // groups, 3 * model),
+            sums[rows_qkv : rows_qkv + rows_out].astype(F32),
+            tiny[0].reshape(model // groups, experts),
+            tiny[1],
+            tiny[2],
+            tiny[3].reshape(buckets // groups, head_count),
+        )
+
+    small_sums = unpack(sums)
+    held = [[ring.held for ring in rings] for _, rings in sets]
+    wholes = store(wholes, held, swap_held(held), 2 - chips)
+    gathered = tuple(whole.reshape(owned * hidden, model) for whole in wholes)
+    return (layer_out, tokens_grad) + small_sums + gathered
 
 
 def solution(mesh):

time: 1050 us -> 697 us (0.66)
  other arithmetic: 213 us -> 115 us
  waiting for transfers between devices: 402 us -> 322 us
  starting transfers between devices: 134 us -> 67.1 us
  blocking collectives: 62.6 us -> 0 us
  local copies, waits for them, and re-layouts: 96.7 us -> 58.4 us
  between operations: 31.4 us -> 2.32 us
  Pallas kernels: 63.9 us -> 92.9 us
    ppermute x183 -> x74, waiting for transfers between devices: 307 us -> 213 us  [the longest x8 153 us: stage(): above = lax.ppermute(above, 'rep', up_hop)]
    ppermute x12 -> x13, waiting for transfers between devices: 40.4 us -> 110 us  [swap_groups(): return lax.ppermute(values, 'grp', [(0, 1), (1, 0)])]
    dynamic_update_slice x128 -> x33, other arithmetic: 126 us -> 57.7 us  [the longest x32 57.6 us: store(): lax.dynamic_update_slice(stored[i], value.astype(F32)[:, None], (first, a...]
    ppermute x183 -> x74, starting transfers between devices: 120 us -> 53.3 us  [the longest x28 28.8 us: move(): return lax.ppermute(self.held, 'rep', self.hop)]
    psum x1 -> x0, blocking collectives: 57.7 us -> none  [local(): sums = tuple((value.astype(F32) for value in lax.psum(shares, 'rep')))]
    psum x1 -> x0, waiting for transfers between devices: 54.7 us -> none  [local(): sums = tuple((value.astype(F32) for value in lax.psum(shares, 'rep')))]
    pallas_call x3 -> x0, other arithmetic: 38 us -> none  [run_experts(): pl.pallas_call(expert_kernel, grid_spec=pltpu.PrefetchScalarGridSpec(num_...]
    pallas_call x1 -> x2, Pallas kernels: 13.1 us -> 41.9 us  [the longest x1 41.9 us: run_experts(): pl.pallas_call(functools.partial(expert_kernel, len(sizes)), grid_spec=pl...]
  transfers between devices with their start and end apart: 200 -> 87, of which waited for: 90 -> 34; matrix products, arithmetic and copies ran while one was open for 27% -> 17% of each run, Pallas kernels for 5% -> 7%
where the time goes in v2:
time: 697 us; the launch traced here: 688 us
  waiting for transfers between devices  322 us (46%)
  other arithmetic  115 us (16%)
  Pallas kernels  92.9 us (13%)
  starting transfers between devices  67.1 us (10%)
  local copies, waits for them, and re-layouts  58.4 us (8%)
  matrix products  29.9 us (4%)
    ppermute x8, waiting for transfers between devices, stage(): above = lax.ppermute(above, 'rep', up_hop)  153 us
    ppermute x13, waiting for transfers between devices, swap_groups(): return lax.ppermute(values, 'grp', [(0, 1), (1, 0)])  110 us
    dynamic_update_slice x32, other arithmetic, store(): lax.dynamic_update_slice(stored[i], value.astype(F32)[:, None], (first, a...  57.6 us
    pallas_call x1, Pallas kernels, run_experts(): pl.pallas_call(functools.partial(expert_kernel, len(sizes)), grid_spec=pl...  41.9 us
    ppermute x28, waiting for transfers between devices, move(): return lax.ppermute(self.held, 'rep', self.hop)  35.7 us
    convert_element_type x14, other arithmetic, take(): (arrived.astype(F32) + self.pick(-step - 1).astype(F32)).astype(BF16)  34.7 us
    pallas_call x1, Pallas kernels, attention_back(): pl.pallas_call(functools.partial(attention_back_kernel, scale), grid=(seq...  31.8 us
    ppermute x28, starting transfers between devices, move(): return lax.ppermute(self.held, 'rep', self.hop)  28.8 us
  transfers between devices with their start and end apart: 87, of which 34 were waited for; matrix products, arithmetic and copies ran while one was open for 17% of the time, Pallas kernels for 7%

profile of v2, /device:TPU:0, one launch (start us, length us, event | category | flops | bytes accessed | tf_op | source)
XLA Modules:
  0.0 688.5 jit_solution(14085282481751323408)
XLA Ops:
  17.3 15.6 %collective-permute-done.6 = s32[1,512]{1,0:T(1,128)S(1)} collective-permute-done((s32[1,512]{1,0:T(1,128)}, s32[1,512]{1,0:T(1,128)S(1)}, u32[]{:S(2)}, u32[]{:S(2)}) %collective-permute-start.6) | collective-permute-done | bytes 2080 | tf_op jit(solution)/shard_map/ppermute | solution.py:374
  39.6 7.9 %collective-permute-done.1 = bf16[96,2304]{1,0:T(8,128)(2,1)S(1)} collective-permute-done((bf16[96,2304]{1,0:T(8,128)(2,1)}, bf16[96,2304]{1,0:T(8,128)(2,1)S(1)}, u32[]{:S(2)}, u32[]{:S(2)}) %collective-permute-start.1) | collective-permute-done | bytes 442400 | tf_op jit(solution)/shard_map/ppermute | solution.py:366
  50.3 6.3 fusion.3.q_ref.k_ref.v_ref
  60.0 19.2 %shard_map.204 = bf16[1,512,768]{2,1,0:T(8,128)(2,1)S(1)} custom-call(bf16[1,1024,2304]{2,1,0:T(8,128)(2,1)S(1)} %fusion.3.q_ref.k_ref.v_ref, bf16[1,1024,2304]{2,1,0:T(8,128)(2,1)S(1)} %fusion.3.q_ref.k_ref.v_ref, bf16[1,1024,2304]{2,1,0:T(8,128)(2,1)S(1)} %fusion.3.q_ref.k_ref.v_ref, s32[1,512,1]{2,1,0:T(8,128)S(1)} %copy.110.seg_q_ref, ...), custom_call_target="tpu_custom_call" | custom-call | flops 1610612736 | bytes 6291456 | tf_op jit(solution)/shard_map/pallas_call | solution.py:172
  100.2 13.9 %collective-permute-done.12.refs_9_ = f32[4,1,128]{2,1,0:T(1,128)} collective-permute-done((f32[4,1,128]{2,1,0:T(1,128)S(1)}, f32[4,1,128]{2,1,0:T(1,128)}, u32[]{:S(2)}, u32[]{:S(2)}) %collective-permute-start.12) | collective-permute-done | bytes 2080 | tf_op jit(solution)/shard_map/ppermute | solution.py:374
  117.3 41.9 %shard_map.205 = (bf16[4,512,768]{2,1,0:T(8,128)(2,1)}, bf16[4,512,768]{2,1,0:T(8,128)(2,1)}, bf16[4,1536,768]{2,1,0:T(8,128)(2,1)}, bf16[4,1536,768]{2,1,0:T(8,128)(2,1)}) custom-call(s32[1]{0:T(128)} %bitcast.core_ref, bf16[4,128,768]{2,1,0:T(8,128)(2,1)} %bitcast.447, bf16[4,128,768]{2,1,0:T(8,128)(2,1)} %collective-permute-done.11.refs_1_, ...), custom_call_target="tpu_custom_call" | custom-call | flops 28991029248 | bytes 37748736 | tf_op jit(solution)/shard_map/pallas_call | solution.py:291
  173.2 15.7 %collective-permute-done.23 = bf16[4,128,768]{2,1,0:T(8,128)(2,1)} collective-permute-done((bf16[4,128,768]{2,1,0:T(8,128)(2,1)}, bf16[4,128,768]{2,1,0:T(8,128)(2,1)}, u32[]{:S(2)}, u32[]{:S(2)}) %collective-permute-start.23) | collective-permute-done | bytes 786464 | tf_op jit(solution)/shard_map/ppermute | solution.py:374
  190.2 4.3 collective-permute-done.20
  205.3 12.9 %collective-permute-done.27 = bf16[4,128,768]{2,1,0:T(8,128)(2,1)S(1)} collective-permute-done((bf16[4,128,768]{2,1,0:T(8,128)(2,1)S(1)}, bf16[4,128,768]{2,1,0:T(8,128)(2,1)S(1)}, u32[]{:S(2)}, u32[]{:S(2)}) %collective-permute-start.27) | collective-permute-done | bytes 786464 | tf_op jit(solution)/shard_map/ppermute | solution.py:374
  237.6 31.8 %shard_map.206 = (bf16[1,512,768]{2,1,0:T(8,128)(2,1)S(1)}, bf16[1,1024,768]{2,1,0:T(8,128)(2,1)S(1)}, bf16[1,1024,768]{2,1,0:T(8,128)(2,1)S(1)}, f32[1,6,4,1024]{3,2,1,0:T(4,128)S(1)}) custom-call(bf16[1,1024,2304]{2,1,0:T(8,128)(2,1)} %copy-done, bf16[1,1024,2304]{2,1,0:T(8,128)(2,1)} %copy-done, bf16[1,1024,2304]{2,1,0:T(8,128)(2,1)} %copy-done, ...), custom_call_target="tpu_custom_call" | custom-call | flops 4026531840 | bytes 12582912 | tf_op jit(solution)/shard_map/pallas_call | solution.py:200
  282.8 12.2 %collective-permute-done.32 = bf16[1,512,768]{2,1,0:T(8,128)(2,1)} collective-permute-done((bf16[1,512,768]{2,1,0:T(8,128)(2,1)}, bf16[1,512,768]{2,1,0:T(8,128)(2,1)}, u32[]{:S(2)}, u32[]{:S(2)}) %collective-permute-start.32) | collective-permute-done | bytes 786464 | tf_op jit(solution)/shard_map/ppermute | solution.py:374
  313.1 11.5 %collective-permute-done.35 = bf16[1,512,768]{2,1,0:T(8,128)(2,1)} collective-permute-done((bf16[1,512,768]{2,1,0:T(8,128)(2,1)}, bf16[1,512,768]{2,1,0:T(8,128)(2,1)}, u32[]{:S(2)}, u32[]{:S(2)}) %collective-permute-start.35) | collective-permute-done | bytes 786464 | tf_op jit(solution)/shard_map/ppermute | solution.py:374
  326.1 4.9 fusion.34
  336.6 5.1 reshape.574
  354.3 4.9 collective-permute-done.38
  366.0 27.9 %collective-permute-done.39 = bf16[832,768]{1,0:T(8,128)(2,1)} collective-permute-done((bf16[832,768]{1,0:T(8,128)(2,1)}, bf16[832,768]{1,0:T(8,128)(2,1)}, u32[]{:S(2)}, u32[]{:S(2)}) %collective-permute-start.39) | collective-permute-done | bytes 1277984 | tf_op jit(solution)/shard_map/ppermute | solution.py:374
  405.5 26.6 %collective-permute-done.42 = bf16[104,768]{1,0:T(8,128)(2,1)} collective-permute-done((bf16[104,768]{1,0:T(8,128)(2,1)}, bf16[104,768]{1,0:T(8,128)(2,1)}, u32[]{:S(2)}, u32[]{:S(2)}) %collective-permute-start.42) | collective-permute-done | bytes 159776 | tf_op jit(solution)/shard_map/ppermute | solution.py:728
  450.6 19.6 %collective-permute-done.48 = bf16[104,768]{1,0:T(8,128)(2,1)S(1)} collective-permute-done((bf16[104,768]{1,0:T(8,128)(2,1)S(1)}, bf16[104,768]{1,0:T(8,128)(2,1)S(1)}, u32[]{:S(2)}, u32[]{:S(2)}) %collective-permute-start.48) | collective-permute-done | bytes 159776 | tf_op jit(solution)/shard_map/ppermute | solution.py:728
  482.0 20.9 %collective-permute-done.54 = bf16[104,768]{1,0:T(8,128)(2,1)S(1)} collective-permute-done((bf16[104,768]{1,0:T(8,128)(2,1)S(1)}, bf16[104,768]{1,0:T(8,128)(2,1)S(1)}, u32[]{:S(2)}, u32[]{:S(2)}) %collective-permute-start.54) | collective-permute-done | bytes 159776 | tf_op jit(solution)/shard_map/ppermute | solution.py:728
  512.6 20.0 %collective-permute-done.56 = bf16[4,1,192,768]{3,2,0,1:T(8,128)(2,1)S(1)} collective-permute-done((bf16[4,1,192,768]{3,2,0,1:T(8,128)(2,1)S(1)}, bf16[4,1,192,768]{3,2,0,1:T(8,128)(2,1)S(1)}, u32[]{:S(2)}, u32[]{:S(2)}) %collective-permute-start.56) | collective-permute-done | bytes 1179680 | tf_op jit(solution)/shard_map/ppermute | solution.py:342
  546.2 20.9 %collective-permute-done.65 = bf16[104,768]{1,0:T(8,128)(2,1)S(1)} collective-permute-done((bf16[104,768]{1,0:T(8,128)(2,1)S(1)}, bf16[104,768]{1,0:T(8,128)(2,1)S(1)}, u32[]{:S(2)}, u32[]{:S(2)}) %collective-permute-start.65) | collective-permute-done | bytes 159776 | tf_op jit(solution)/shard_map/ppermute | solution.py:741
  578.4 20.9 %collective-permute-done.71 = bf16[104,768]{1,0:T(8,128)(2,1)S(1)} collective-permute-done((bf16[104,768]{1,0:T(8,128)(2,1)S(1)}, bf16[104,768]{1,0:T(8,128)(2,1)S(1)}, u32[]{:S(2)}, u32[]{:S(2)}) %collective-permute-start.71) | collective-permute-done | bytes 159776 | tf_op jit(solution)/shard_map/ppermute | solution.py:741
  610.5 20.9 %collective-permute-done.77 = bf16[104,768]{1,0:T(8,128)(2,1)S(1)} collective-permute-done((bf16[104,768]{1,0:T(8,128)(2,1)S(1)}, bf16[104,768]{1,0:T(8,128)(2,1)S(1)}, u32[]{:S(2)}, u32[]{:S(2)}) %collective-permute-start.77) | collective-permute-done | bytes 159776 | tf_op jit(solution)/shard_map/ppermute | solution.py:741
  643.2 21.1 %collective-permute-done.83 = bf16[104,768]{1,0:T(8,128)(2,1)S(1)} collective-permute-done((bf16[104,768]{1,0:T(8,128)(2,1)S(1)}, bf16[104,768]{1,0:T(8,128)(2,1)S(1)}, u32[]{:S(2)}, u32[]{:S(2)}) %collective-permute-start.83) | collective-permute-done | bytes 159776 | tf_op jit(solution)/shard_map/ppermute | solution.py:741
  (422 shorter events, 279.1 us)
Async XLA Ops:
  2.5 33.5 %collective-permute-start = (bf16[96,2304]{1,0:T(8,128)(2,1)}, bf16[96,2304]{1,0:T(8,128)(2,1)}, u32[]{:S(2)}, u32[]{:S(2)}) collective-permute-start(bf16[96,2304]{1,0:T(8,128)(2,1)} %constant_dynamic-slice_fusion.1), channel_id=1, source_target_pairs={{0,1},{1,0},{2,3},{3,2},{4,5},{5,4},{6,7},{7,6},{8,9},{9,8},{10,11... | collective-permute-start | bytes 1327112 | tf_op jit(solution)/shard_map/ppermute | solution.py:374
  5.4 34.1 %collective-permute-start.2 = (bf16[1,512,768]{2,1,0:T(8,128)(2,1)}, bf16[1,512,768]{2,1,0:T(8,128)(2,1)S(1)}, u32[]{:S(2)}, u32[]{:S(2)}) collective-permute-start(bf16[1,512,768]{2,1,0:T(8,128)(2,1)} %param.13), channel_id=1, source_target_pairs={{0,1},{1,0},{2,3},{3,2},{4,5},{5,4},{6,7},{7,6},{8,9},{9,8},{10,11... | collective-permute-start | bytes 2359304 | tf_op jit(solution)/shard_map/ppermute | solution.py:374
  59.4 40.8 %collective-permute-start.15 = (bf16[4,128,768]{2,1,0:T(8,128)(2,1)}, bf16[4,128,768]{2,1,0:T(8,128)(2,1)}, u32[]{:S(2)}, u32[]{:S(2)}) collective-permute-start(bf16[4,128,768]{2,1,0:T(8,128)(2,1)} %get-tuple-element.401), channel_id=1, source_target_pairs={{0,1},{1,0},{2,3},{3,2},{4,5},{5,4},{6,7},{7,6},{8,9},{9,8},{10,11... | collective-permute-start | bytes 2359304 | tf_op jit(solution)/shard_map/ppermute | solution.py:374
  234.4 35.0 %collective-permute-start.28 = (bf16[4,1,192,768]{3,2,0,1:T(8,128)(2,1)}, bf16[4,1,192,768]{3,2,0,1:T(8,128)(2,1)}, u32[]{:S(2)}, u32[]{:S(2)}) collective-permute-start(bf16[4,1,192,768]{3,2,0,1:T(8,128)(2,1)} %add_convert_fusion.13), channel_id=1, source_target_pairs={{0,8},{2,10},{8,16},{10,18},{16,24},{18,26},{24,28},{26,30},{28,20... | collective-permute-start | bytes 3538952 | tf_op jit(solution)/shard_map/ppermute | solution.py:342
  236.0 33.4 %collective-permute-start.29 = (bf16[4,1,192,768]{3,2,0,1:T(8,128)(2,1)}, bf16[4,1,192,768]{3,2,0,1:T(8,128)(2,1)}, u32[]{:S(2)}, u32[]{:S(2)}) collective-permute-start(bf16[4,1,192,768]{3,2,0,1:T(8,128)(2,1)} %add_convert_fusion.12), channel_id=1, source_target_pairs={{4,12},{6,14},{12,20},{14,22},{20,28},{22,30},{28,24},{30,26},{24,... | collective-permute-start | bytes 3538952 | tf_op jit(solution)/shard_map/ppermute | solution.py:342
  363.5 30.4 %collective-permute-start.39 = (bf16[832,768]{1,0:T(8,128)(2,1)}, bf16[832,768]{1,0:T(8,128)(2,1)}, u32[]{:S(2)}, u32[]{:S(2)}) collective-permute-start(bf16[832,768]{1,0:T(8,128)(2,1)} %dynamic-slice_bitcast_fusion.1), channel_id=1, source_target_pairs={{0,1},{1,0},{2,3},{3,2},{4,5},{5,4},{6,7},{7,6},{8,9},{9,8},{10,11... | collective-permute-start | bytes 3833864 | tf_op jit(solution)/shard_map/ppermute | solution.py:374
  364.0 31.5 %collective-permute-start.36 = (bf16[4,1,192,768]{3,2,0,1:T(8,128)(2,1)}, bf16[4,1,192,768]{3,2,0,1:T(8,128)(2,1)}, u32[]{:S(2)}, u32[]{:S(2)}) collective-permute-start(bf16[4,1,192,768]{3,2,0,1:T(8,128)(2,1)} %add_convert_fusion.7), channel_id=1, source_target_pairs={{0,8},{2,10},{8,16},{10,18},{16,24},{18,26},{24,28},{26,30},{28,20... | collective-permute-start | bytes 3538952 | tf_op jit(solution)/shard_map/ppermute | solution.py:342
  365.5 30.1 %collective-permute-start.37 = (bf16[4,1,192,768]{3,2,0,1:T(8,128)(2,1)}, bf16[4,1,192,768]{3,2,0,1:T(8,128)(2,1)}, u32[]{:S(2)}, u32[]{:S(2)}) collective-permute-start(bf16[4,1,192,768]{3,2,0,1:T(8,128)(2,1)} %add_convert_fusion.6), channel_id=1, source_target_pairs={{4,12},{6,14},{12,20},{14,22},{20,28},{22,30},{28,24},{30,26},{24,... | collective-permute-start | bytes 3538952 | tf_op jit(solution)/shard_map/ppermute | solution.py:342
  401.3 33.8 %collective-permute-start.40 = (bf16[4,1,192,768]{3,2,0,1:T(8,128)(2,1)}, bf16[4,1,192,768]{3,2,0,1:T(8,128)(2,1)S(1)}, u32[]{:S(2)}, u32[]{:S(2)}) collective-permute-start(bf16[4,1,192,768]{3,2,0,1:T(8,128)(2,1)} %add_convert_fusion.5), channel_id=1, source_target_pairs={{0,8},{2,10},{8,16},{10,18},{16,24},{18,26},{24,28},{26,30},{28,20... | collective-permute-start | bytes 3538952 | tf_op jit(solution)/shard_map/ppermute | solution.py:342
  402.7 32.4 %collective-permute-start.41 = (bf16[4,1,192,768]{3,2,0,1:T(8,128)(2,1)S(1)}, bf16[4,1,192,768]{3,2,0,1:T(8,128)(2,1)S(1)}, u32[]{:S(2)}, u32[]{:S(2)}) collective-permute-start(bf16[4,1,192,768]{3,2,0,1:T(8,128)(2,1)S(1)} %add_convert_fusion.4), channel_id=1, source_target_pairs={{4,12},{6,14},{12,20},{14,22},{20,28},{22,30},{28,24},{30,26},{24,... | collective-permute-start | bytes 3538952 | tf_op jit(solution)/shard_map/ppermute | solution.py:342
  403.3 28.9 %collective-permute-start.42 = (bf16[104,768]{1,0:T(8,128)(2,1)}, bf16[104,768]{1,0:T(8,128)(2,1)}, u32[]{:S(2)}, u32[]{:S(2)}) collective-permute-start(bf16[104,768]{1,0:T(8,128)(2,1)} %get-tuple-element.265), channel_id=1, source_target_pairs={{0,8},{2,10},{8,16},{10,18},{16,24},{18,26},{24,28},{26,30},{28,20... | collective-permute-start | bytes 479240 | tf_op jit(solution)/shard_map/ppermute | solution.py:728
  438.8 32.2 %collective-permute-start.44 = (bf16[4,1,192,768]{3,2,0,1:T(8,128)(2,1)S(1)}, bf16[4,1,192,768]{3,2,0,1:T(8,128)(2,1)S(1)}, u32[]{:S(2)}, u32[]{:S(2)}) collective-permute-start(bf16[4,1,192,768]{3,2,0,1:T(8,128)(2,1)S(1)} %add_convert_fusion.3), channel_id=1, source_target_pairs={{0,8},{2,10},{8,16},{10,18},{16,24},{18,26},{24,28},{26,30},{28,20... | collective-permute-start | bytes 3538952 | tf_op jit(solution)/shard_map/ppermute | solution.py:342
  439.8 31.2 %collective-permute-start.45 = (bf16[4,1,192,768]{3,2,0,1:T(8,128)(2,1)S(1)}, bf16[4,1,192,768]{3,2,0,1:T(8,128)(2,1)S(1)}, u32[]{:S(2)}, u32[]{:S(2)}) collective-permute-start(bf16[4,1,192,768]{3,2,0,1:T(8,128)(2,1)S(1)} %add_convert_fusion.2), channel_id=1, source_target_pairs={{4,12},{6,14},{12,20},{14,22},{20,28},{22,30},{28,24},{30,26},{24,... | collective-permute-start | bytes 3538952 | tf_op jit(solution)/shard_map/ppermute | solution.py:342
  471.6 31.4 %collective-permute-start.50 = (bf16[4,1,192,768]{3,2,0,1:T(8,128)(2,1)S(1)}, bf16[4,1,192,768]{3,2,0,1:T(8,128)(2,1)S(1)}, u32[]{:S(2)}, u32[]{:S(2)}) collective-permute-start(bf16[4,1,192,768]{3,2,0,1:T(8,128)(2,1)S(1)} %collective-permute-done.44), channel_id=1, source_target_pairs={{0,8},{2,10},{8,16},{10,18},{16,24},{18,26},{24,28},{26,30},{28,20... | collective-permute-start | bytes 3538952 | tf_op jit(solution)/shard_map/ppermute | solution.py:342
  472.1 30.9 %collective-permute-start.51 = (bf16[4,1,192,768]{3,2,0,1:T(8,128)(2,1)S(1)}, bf16[4,1,192,768]{3,2,0,1:T(8,128)(2,1)S(1)}, u32[]{:S(2)}, u32[]{:S(2)}) collective-permute-start(bf16[4,1,192,768]{3,2,0,1:T(8,128)(2,1)S(1)} %collective-permute-done.45), channel_id=1, source_target_pairs={{4,12},{6,14},{12,20},{14,22},{20,28},{22,30},{28,24},{30,26},{24,... | collective-permute-start | bytes 3538952 | tf_op jit(solution)/shard_map/ppermute | solution.py:342
  503.7 28.8 %collective-permute-start.56 = (bf16[4,1,192,768]{3,2,0,1:T(8,128)(2,1)S(1)}, bf16[4,1,192,768]{3,2,0,1:T(8,128)(2,1)S(1)}, u32[]{:S(2)}, u32[]{:S(2)}) collective-permute-start(bf16[4,1,192,768]{3,2,0,1:T(8,128)(2,1)S(1)} %collective-permute-done.50), channel_id=1, source_target_pairs={{0,8},{2,10},{8,16},{10,18},{16,24},{18,26},{24,28},{26,30},{28,20... | collective-permute-start | bytes 3538952 | tf_op jit(solution)/shard_map/ppermute | solution.py:342
  535.7 31.6 %collective-permute-start.61 = (bf16[4,1,192,768]{3,2,0,1:T(8,128)(2,1)S(1)}, bf16[4,1,192,768]{3,2,0,1:T(8,128)(2,1)S(1)}, u32[]{:S(2)}, u32[]{:S(2)}) collective-permute-start(bf16[4,1,192,768]{3,2,0,1:T(8,128)(2,1)S(1)} %collective-permute-done.56), channel_id=1, source_target_pairs={{0,8},{2,10},{8,16},{10,18},{16,24},{18,26},{24,28},{26,30},{28,20... | collective-permute-start | bytes 3538952 | tf_op jit(solution)/shard_map/ppermute | solution.py:342
  536.2 31.1 %collective-permute-start.62 = (bf16[4,1,192,768]{3,2,0,1:T(8,128)(2,1)S(1)}, bf16[4,1,192,768]{3,2,0,1:T(8,128)(2,1)S(1)}, u32[]{:S(2)}, u32[]{:S(2)}) collective-permute-start(bf16[4,1,192,768]{3,2,0,1:T(8,128)(2,1)S(1)} %collective-permute-done.57), channel_id=1, source_target_pairs={{4,12},{6,14},{12,20},{14,22},{20,28},{22,30},{28,24},{30,26},{24,... | collective-permute-start | bytes 3538952 | tf_op jit(solution)/shard_map/ppermute | solution.py:342
  567.9 31.6 %collective-permute-start.67 = (bf16[4,1,192,768]{3,2,0,1:T(8,128)(2,1)S(1)}, bf16[4,1,192,768]{3,2,0,1:T(8,128)(2,1)S(1)}, u32[]{:S(2)}, u32[]{:S(2)}) collective-permute-start(bf16[4,1,192,768]{3,2,0,1:T(8,128)(2,1)S(1)} %collective-permute-done.61), channel_id=1, source_target_pairs={{0,8},{2,10},{8,16},{10,18},{16,24},{18,26},{24,28},{26,30},{28,20... | collective-permute-start | bytes 3538952 | tf_op jit(solution)/shard_map/ppermute | solution.py:342
  568.4 31.1 %collective-permute-start.68 = (bf16[4,1,192,768]{3,2,0,1:T(8,128)(2,1)S(1)}, bf16[4,1,192,768]{3,2,0,1:T(8,128)(2,1)S(1)}, u32[]{:S(2)}, u32[]{:S(2)}) collective-permute-start(bf16[4,1,192,768]{3,2,0,1:T(8,128)(2,1)S(1)} %collective-permute-done.62), channel_id=1, source_target_pairs={{4,12},{6,14},{12,20},{14,22},{20,28},{22,30},{28,24},{30,26},{24,... | collective-permute-start | bytes 3538952 | tf_op jit(solution)/shard_map/ppermute | solution.py:342
  600.1 32.2 %collective-permute-start.73 = (bf16[4,1,192,768]{3,2,0,1:T(8,128)(2,1)S(1)}, bf16[4,1,192,768]{3,2,0,1:T(8,128)(2,1)S(1)}, u32[]{:S(2)}, u32[]{:S(2)}) collective-permute-start(bf16[4,1,192,768]{3,2,0,1:T(8,128)(2,1)S(1)} %collective-permute-done.67), channel_id=1, source_target_pairs={{0,8},{2,10},{8,16},{10,18},{16,24},{18,26},{24,28},{26,30},{28,20... | collective-permute-start | bytes 3538952 | tf_op jit(solution)/shard_map/ppermute | solution.py:342
  601.2 31.1 %collective-permute-start.74 = (bf16[4,1,192,768]{3,2,0,1:T(8,128)(2,1)S(1)}, bf16[4,1,192,768]{3,2,0,1:T(8,128)(2,1)S(1)}, u32[]{:S(2)}, u32[]{:S(2)}) collective-permute-start(bf16[4,1,192,768]{3,2,0,1:T(8,128)(2,1)S(1)} %collective-permute-done.68), channel_id=1, source_target_pairs={{4,12},{6,14},{12,20},{14,22},{20,28},{22,30},{28,24},{30,26},{24,... | collective-permute-start | bytes 3538952 | tf_op jit(solution)/shard_map/ppermute | solution.py:342
  632.9 31.4 %collective-permute-start.79 = (bf16[4,1,192,768]{3,2,0,1:T(8,128)(2,1)S(1)}, bf16[4,1,192,768]{3,2,0,1:T(8,128)(2,1)}, u32[]{:S(2)}, u32[]{:S(2)}) collective-permute-start(bf16[4,1,192,768]{3,2,0,1:T(8,128)(2,1)S(1)} %collective-permute-done.73), channel_id=1, source_target_pairs={{0,8},{2,10},{8,16},{10,18},{16,24},{18,26},{24,28},{26,30},{28,20... | collective-permute-start | bytes 3538952 | tf_op jit(solution)/shard_map/ppermute | solution.py:342
  634.5 29.8 %collective-permute-start.80 = (bf16[4,1,192,768]{3,2,0,1:T(8,128)(2,1)S(1)}, bf16[4,1,192,768]{3,2,0,1:T(8,128)(2,1)}, u32[]{:S(2)}, u32[]{:S(2)}) collective-permute-start(bf16[4,1,192,768]{3,2,0,1:T(8,128)(2,1)S(1)} %collective-permute-done.74), channel_id=1, source_target_pairs={{4,12},{6,14},{12,20},{14,22},{20,28},{22,30},{28,24},{30,26},{24,... | collective-permute-start | bytes 3538952 | tf_op jit(solution)/shard_map/ppermute | solution.py:342
  (111 other events, 1428.1 us)

commit v3 on v2

--- a/solution.py
+++ b/solution.py
@@ -281,7 +281,7 @@
     sizes = [piece.shape[1] for piece in rows_in]
     slots = sum(sizes)
     part = up.shape[2]
-    fits = [t for t in (512, 384, 256, 128) if part % t == 0 and slots * t <= 1 << 18]
+    fits = [t for t in (768, 512, 384, 256, 128) if part % t == 0 and slots * t <= 3 << 17]
     tile = (fits + [part])[0]
     row_specs = [pl.BlockSpec((1, n, model), lambda e, f, c: (first + e, 0, 0)) for n in sizes]
     gate_specs = [pl.BlockSpec((1, 1, n), lambda e, f, c: (first + e, 0, 0)) for n in sizes]
@@ -341,6 +341,7 @@
     def move(self):
         return lax.ppermute(self.held, "rep", self.hop)
 
+
     def take(self, step, arrived):
         if step < self.chips - 1:
             arrived = (arrived.astype(F32) + self.pick(-step - 1).astype(F32)).astype(BF16)
@@ -407,23 +408,25 @@
     part = hidden // CORES
     two = groups == 2
 
-    def gather_rotated(values, axis):
+    def fetch(values):
+        return swap_groups(values) if two else lax.all_gather(values, "grp", axis=0)
+
+    def rotated(values, fetched, axis):
         if two:
-            return jnp.concatenate([values, swap_groups(values)], axis=axis)
-        whole = lax.all_gather(values, "grp", axis=axis, tiled=True)
+            return jnp.concatenate([values, fetched], axis=axis)
+        whole = jnp.concatenate([fetched[i] for i in range(groups)], axis=axis)
         return jnp.roll(whole, -grp_index * values.shape[axis], axis=axis)
 
-    def gather_stacked(values):
-        if two:
-            other = swap_groups(values)
-            return jnp.where(
-                grp_index == 0, jnp.stack([values, other]), jnp.stack([other, values])
-            )
-        return lax.all_gather(values, "grp", axis=0)
-
-    def gather_weight(values, after=None):
+    def stacked(values, fetched):
         if not two:
-            return lax.all_gather(values, "grp", axis=0, tiled=True)
+            return fetched
+        return jnp.where(
+            grp_index == 0, jnp.stack([values, fetched]), jnp.stack([fetched, values])
+        )
+
+    def gather_weight(values, after):
+        if not two:
+            return lax.all_gather(values, "grp", axis=0, tiled=True), after
         rows = values.shape[0]
         sharers = 4 if reps % 4 == 0 and rows % 64 == 0 else 2
         piece = rows // sharers
@@ -431,8 +434,7 @@
         pieces = {0: swap_groups(lax.dynamic_slice_in_dim(values, place * piece, piece, 0))}
         if sharers == 4:
             pieces[2] = swap_reps(pieces[0], reps, 2)
-            if after is not None:
-                pieces[2], after[0] = lax.optimization_barrier((pieces[2], after[0]))
+            pieces[2], after = lax.optimization_barrier((pieces[2], after))
         for bit in list(pieces):
             pieces[bit | 1] = swap_cores(pieces[bit], reps)
         whole = jnp.zeros((2 * rows,) + values.shape[1:], values.dtype)
@@ -442,22 +444,38 @@
             whole = lax.dynamic_update_slice_in_dim(
                 whole, fetched, start + (place ^ bit) * piece, 0
             )
-        return whole
+        return whole, after
+
+    def gather_whole(values):
+        if not two:
+            return lax.all_gather(values, "grp", axis=0, tiled=True)
+        rows = values.shape[0]
+        whole = jnp.zeros((2 * rows,) + values.shape[1:], values.dtype)
+        whole = lax.dynamic_update_slice_in_dim(whole, values, grp_index * rows, 0)
+        return lax.dynamic_update_slice_in_dim(
+            whole, swap_groups(values), (1 - grp_index) * rows, 0
+        )
 
     small = jnp.concatenate(
         [router_weight.reshape(-1), gain_attn, gain_ffn, rel_table.reshape(-1)]
     )
-    small = gather_stacked(small)
+    small_far, tokens_far = fetch(small), fetch(tokens)
+    full_qkv, (small_far, tokens_far) = gather_weight(
+        query_key_value_weight, (small_far, tokens_far)
+    )
+    small = stacked(small, small_far)
     cuts = np.cumsum([router_weight.size, gain_attn.size, gain_ffn.size]).tolist()
     full_router, full_gain_attn, full_gain_ffn, full_table = jnp.split(small, cuts, axis=1)
     full_router = full_router.reshape(model, experts)
     full_table = full_table.reshape(buckets, head_count)
     gain_one = full_gain_attn.reshape(-1).astype(F32)
     gain_two = full_gain_ffn.reshape(-1).astype(F32)
-    seg_all = gather_rotated(segment_ids, 1)
-    arriving = [gather_rotated(tokens, 1)]
-    full_qkv = gather_weight(query_key_value_weight, arriving)
-    tokens_all = arriving[0]
+    tokens_far, late_out, late_ids = lax.optimization_barrier(
+        (tokens_far, output_weight, segment_ids)
+    )
+    tokens_all = rotated(tokens, tokens_far, 1)
+    seg_all = rotated(late_ids, fetch(late_ids), 1)
+    full_out = gather_whole(late_out)
 
     first_expert = grp_index * owned if two else 0
     expert_of = expert_ids[..., 0]
@@ -501,6 +519,9 @@
         "std,de->ste", normed_all, full_qkv, preferred_element_type=F32
     ).astype(BF16)
 
+    projected, cot_slots = lax.optimization_barrier((projected, to_slots(out_grad)))
+    cot_rows = to_side(cot_slots)
+
     bucket_line = jnp.pad(rel_bucket, (0, 1), constant_values=buckets)
     starts = [
         ((grp_index + b) % groups - grp_index) * span + length - span for b in range(groups)
@@ -513,13 +534,6 @@
     window = jnp.einsum(
         "bh,bo->ho", full_table, bucket_hot.astype(BF16), preferred_element_type=F32
     ).reshape(head_count // PAIR, PAIR * groups, 2 * span)
-
-    cot_slots = to_slots(out_grad)
-    projected, late_out, cot_slots = lax.optimization_barrier(
-        (projected, output_weight, cot_slots)
-    )
-    full_out = gather_weight(late_out)
-    cot_rows = to_side(cot_slots)
 
     attended = attention(projected, segment_ids, seg_all, window, span, head_count)
     residual = input_tokens + jnp.einsum(
@@ -653,64 +667,81 @@
         terms = jnp.roll(terms, grp_index * span, axis=1)
         return lax.psum_scatter(terms, "grp", scatter_dimension=1, tiled=True)
 
-    def keys_end(key_terms, diagonals, grad_attn):
+    def weight_grad(grad_part):
+        grad = jnp.einsum("std,ste->de", normed_own, grad_part, preferred_element_type=F32)
+        return grad.astype(BF16).reshape(groups, -1, model)
+
+    def keys_end(key_terms, diagonals, grad_attn, grad_queries):
         grad_wout = jnp.einsum("std,ste->de", attended, grad_attn, preferred_element_type=F32)
+        grad_wout = grad_wout.astype(BF16).reshape(groups, -1, model)
         diagonals = jnp.sum(diagonals, axis=0).reshape(head_count, groups * 2 * span)
         grad_table = jnp.einsum(
             "bo,ho->bh", bucket_hot.astype(F32), diagonals, precision=lax.Precision.HIGHEST
         )
-        return own_keys(key_terms), grad_table, grad_wout
-
-    def projection_back(grad_queries, grad_keys, value_terms, grad_residual):
-        grad_values = own_keys(value_terms)
-        grad_mixed = jnp.concatenate([grad_queries, grad_keys, grad_values], axis=-1)
-        grad_qkv = jnp.einsum("std,ste->de", normed_own, grad_mixed, preferred_element_type=F32)
-        grad_normed = jnp.einsum("ste,de->std", grad_mixed, full_qkv, preferred_element_type=F32)
-        grad_input_part, grad_gain_attn = rms_back(
-            grad_normed, input_tokens, inverse_one, gain_one
-        )
-        return grad_qkv.astype(BF16), grad_gain_attn, grad_residual + grad_input_part
-
-    placed, grad_sums = beside(side_sums, (outs, grad_ins))
-    layer_out, grad_router, grad_gain_ffn, grad_residual, grad_attn, grad_attended = beside(
-        ffn_end, (placed, grad_sums)
-    )
-    grad_queries, key_terms, value_terms, diagonals = beside(scores_back, (grad_attended,))
-    grad_keys, grad_table, grad_wout = beside(keys_end, (key_terms, diagonals, grad_attn))
-    grad_qkv, grad_gain_attn, tokens_grad = beside(
-        projection_back, (grad_queries, grad_keys, value_terms, grad_residual)
-    )
-
-    tiny = (grad_router, grad_gain_attn, grad_gain_ffn, grad_table)
-    tiny = [value.astype(BF16).reshape(groups, -1) for value in tiny]
-    tiny_cuts = np.cumsum([value.shape[1] for value in tiny]).tolist()
-    flat = jnp.concatenate(tiny, axis=1)
-    flat = jnp.pad(flat, ((0, 0), (0, -flat.shape[1] % model))).reshape(groups, -1, model)
-    rows_out = model // groups
-    rows_qkv = 3 * rows_out
-    rows_all = rows_qkv + rows_out + flat.shape[1]
-    packed = jnp.concatenate(
-        [
-            grad_qkv.astype(BF16).reshape(groups, -1, model),
-            grad_wout.astype(BF16).reshape(groups, -1, model),
-            jnp.pad(flat, ((0, 0), (0, -rows_all % (reps * 8)), (0, 0))),
-        ],
-        axis=1,
-    )
-    packed = packed.reshape(groups, CORES, -1, model)
+        return own_keys(key_terms), grad_table, grad_wout, weight_grad(grad_queries)
 
     def halve(values, axis, place, swap):
         mine = lax.dynamic_index_in_dim(values, place, axis, keepdims=False)
         given = swap(lax.dynamic_index_in_dim(values, 1 - place, axis, keepdims=False))
         return (mine.astype(F32) + given.astype(F32)).astype(BF16)
 
-    def share(packed):
-        values = halve(packed, 1, core, lambda v: swap_cores(v, reps))
+    rows_out = model // groups
+    tiny_sizes = [router_weight.size, gain_ffn.size, rel_table.size]
+    tiny_cuts = np.cumsum(tiny_sizes).tolist()
+    rows_tiny = -(-tiny_cuts[-1] // model)
+    rows_all = 4 * rows_out + rows_tiny
+    rows_all += -rows_all % (reps * 8)
+
+    def keys_back(
+        grad_keys, value_terms, far_values, grad_wq, grad_wout, grad_router, grad_gain_ffn, grad_table
+    ):
         if two:
-            return halve(values, 0, grp_index, swap_groups)
-        return lax.psum_scatter(values, "grp", scatter_dimension=0, tiled=False)
-
-    parts = beside(share, (packed,)).reshape(chips, -1, model)
+            grad_values = value_terms[:, :span].astype(F32) + far_values.astype(F32)
+            grad_values = grad_values.astype(BF16)
+        else:
+            grad_values = own_keys(value_terms)
+        tiny = (grad_router, grad_gain_ffn, grad_table)
+        tiny = jnp.concatenate([value.astype(BF16).reshape(groups, -1) for value in tiny], axis=1)
+        room = (rows_all - 4 * rows_out) * model - tiny.shape[1]
+        tiny = jnp.pad(tiny, ((0, 0), (0, room))).reshape(groups, -1, model)
+        packed = jnp.concatenate(
+            [grad_wq, weight_grad(grad_keys), weight_grad(grad_values), grad_wout, tiny], axis=1
+        ).reshape(groups, CORES, -1, model)
+        return halve(packed, 1, core, lambda v: swap_cores(v, reps)), grad_values
+
+    def input_back(grad_queries, grad_keys, grad_values, grad_residual):
+        grad_mixed = jnp.concatenate([grad_queries, grad_keys, grad_values], axis=-1)
+        grad_normed = jnp.einsum("ste,de->std", grad_mixed, full_qkv, preferred_element_type=F32)
+        return grad_residual + rms_back(grad_normed, input_tokens, inverse_one, gain_one)[0]
+
+    def group_share(parts):
+        if two:
+            return halve(parts, 0, grp_index, swap_groups)
+        return lax.psum_scatter(parts, "grp", scatter_dimension=0, tiled=False)
+
+    placed, grad_sums = beside(side_sums, (outs, grad_ins))
+    layer_out, grad_router, grad_gain_ffn, grad_residual, grad_attn, grad_attended = beside(
+        ffn_end, (placed, grad_sums)
+    )
+    grad_queries, key_terms, value_terms, diagonals = beside(scores_back, (grad_attended,))
+    far_values = swap_groups(value_terms[:, span:]) if two else value_terms
+    grad_keys, grad_table, grad_wout, grad_wq = beside(
+        keys_end, (key_terms, diagonals, grad_attn, grad_queries)
+    )
+    parts, grad_values = beside(
+        keys_back,
+        (
+            grad_keys,
+            value_terms,
+            far_values,
+            grad_wq,
+            grad_wout,
+            grad_router,
+            grad_gain_ffn,
+            grad_table,
+        ),
+    )
+    parts = beside(group_share, (parts,)).reshape(chips, -1, model)
 
     upward, downward = chips // 2, chips - 1 - chips // 2
     place, up_hop, down_hop = rings[0].place, rings[0].hop, rings[1].hop
@@ -748,7 +779,12 @@
         return stage
 
     above, below = pick(upward).astype(BF16), pick(-downward).astype(BF16)
-    for step in range(upward):
+    mixed = (grad_queries, grad_keys, grad_values, grad_residual)
+    (above, below), tokens_grad = beside(
+        lambda above, below, *mixed: (reduce_stage(0)(above, below), input_back(*mixed)),
+        (above, below) + mixed,
+    )
+    for step in range(1, upward):
         above, below = beside(reduce_stage(step), (above, below))
     own_sum = (above.astype(F32) + below.astype(F32) + pick(0)).astype(BF16)
     above = below = own_sum
@@ -765,21 +801,20 @@
     for _ in range(total_rounds - 6 - 2 * upward):
         beside()
 
-    def unpack(sums):
-        sums = sums.reshape(-1, model)
-        tiny = jnp.split(
-            sums[rows_qkv + rows_out : rows_all].astype(F32).reshape(-1), tiny_cuts
-        )
-        return (
-            sums[:rows_qkv].astype(F32).reshape(model // groups, 3 * model),
-            sums[rows_qkv : rows_qkv + rows_out].astype(F32),
-            tiny[0].reshape(model // groups, experts),
-            tiny[1],
-            tiny[2],
-            tiny[3].reshape(buckets // groups, head_count),
-        )
-
-    small_sums = unpack(sums)
+    sums = sums.reshape(-1, model)
+    blocks = [sums[i * rows_out : (i + 1) * rows_out].astype(F32) for i in range(4)]
+    tiny = sums[4 * rows_out : 4 * rows_out + rows_tiny].astype(F32).reshape(-1)
+    tiny = jnp.split(tiny, tiny_cuts)
+    sum_qkv = jnp.concatenate(blocks[:3], axis=1)
+    sum_gain = jnp.sum(sum_qkv * query_key_value_weight.astype(F32), axis=1)
+    small_sums = (
+        sum_qkv,
+        blocks[3],
+        tiny[0].reshape(rows_out, experts),
+        sum_gain / gain_attn.astype(F32),
+        tiny[1],
+        tiny[2].reshape(buckets // groups, head_count),
+    )
     held = [[ring.held for ring in rings] for _, rings in sets]
     wholes = store(wholes, held, swap_held(held), 2 - chips)
     gathered = tuple(whole.reshape(owned * hidden, model) for whole in wholes)

time: 697 us -> 679 us (0.974)
  waiting for transfers between devices: 322 us -> 303 us
    ppermute x28, waiting for transfers between devices: 35.7 us -> 70.3 us  [move(): return lax.ppermute(self.held, 'rep', self.hop)]
    ppermute x8, waiting for transfers between devices: 153 us -> 127 us  [stage(): above = lax.ppermute(above, 'rep', up_hop)]
    ppermute x32 -> x29, waiting for transfers between devices: 20.6 us -> 5.55 us  [swap_reps(): return lax.ppermute(values, 'rep', [(r, r ^ bit) for r in range(reps)])]
    ppermute x13, waiting for transfers between devices: 110 us -> 98.8 us  [swap_groups(): return lax.ppermute(values, 'grp', [(0, 1), (1, 0)])]
    reshape x9 -> x5, local copies, waits for them, and re-layouts: 12.7 us -> 1.8 us  [the longest x1 1.33 us: local(): tiny = sums[4 * rows_out:4 * rows_out + rows_tiny].astype(F32).reshape(-1)]
    unnamed x101 -> x117, local copies, waits for them, and re-layouts: 18.6 us -> 19.9 us
  transfers between devices with their start and end apart: 87 -> 84, of which waited for: 34 -> 32; matrix products, arithmetic and copies ran while one was open for 17% -> 21% of each run, Pallas kernels for 7% -> 8%
where the time goes in v3:
time: 679 us; the launch traced here: 670 us
  waiting for transfers between devices  303 us (45%)
  other arithmetic  116 us (17%)
  Pallas kernels  91.4 us (13%)
  starting transfers between devices  67.6 us (10%)
  local copies, waits for them, and re-layouts  59.1 us (9%)
  matrix products  31 us (5%)
    ppermute x8, waiting for transfers between devices, stage(): above = lax.ppermute(above, 'rep', up_hop)  127 us
    ppermute x13, waiting for transfers between devices, swap_groups(): return lax.ppermute(values, 'grp', [(0, 1), (1, 0)])  98.8 us
    ppermute x28, waiting for transfers between devices, move(): return lax.ppermute(self.held, 'rep', self.hop)  70.3 us
    dynamic_update_slice x32, other arithmetic, store(): lax.dynamic_update_slice(stored[i], value.astype(F32)[:, None], (first, a...  57.6 us
    pallas_call x1, Pallas kernels, run_experts(): pl.pallas_call(functools.partial(expert_kernel, len(sizes)), grid_spec=pl...  40.6 us
    convert_element_type x14, other arithmetic, take(): (arrived.astype(F32) + self.pick(-step - 1).astype(F32)).astype(BF16)  34.3 us
    pallas_call x1, Pallas kernels, attention_back(): pl.pallas_call(functools.partial(attention_back_kernel, scale), grid=(seq...  31.7 us
    ppermute x28, starting transfers between devices, move(): return lax.ppermute(self.held, 'rep', self.hop)  28.9 us
  transfers between devices with their start and end apart: 84, of which 32 were waited for; matrix products, arithmetic and copies ran while one was open for 21% of the time, Pallas kernels for 8%

profile of v3, /device:TPU:0, one launch (start us, length us, event | category | flops | bytes accessed | tf_op | source)
XLA Modules:
  0.0 670.4 jit_solution(6245065990270614851)
XLA Ops:
  20.9 12.0 %collective-permute-done.3 = bf16[1,512,768]{2,1,0:T(8,128)(2,1)S(1)} collective-permute-done((bf16[1,512,768]{2,1,0:T(8,128)(2,1)}, bf16[1,512,768]{2,1,0:T(8,128)(2,1)S(1)}, u32[]{:S(2)}, u32[]{:S(2)}) %collective-permute-start.3) | collective-permute-done | bytes 786464 | tf_op jit(solution)/shard_map/ppermute | solution.py:375
  47.1 7.0 %fusion.1.q_ref.k_ref.v_ref = bf16[1,1024,2304]{2,1,0:T(8,128)(2,1)S(1)} fusion(bf16[768,2304]{1,0:T(8,128)(2,1)} %constant_dynamic-update-slice_fusion.2, bf16[512,768]{1,0:T(8,128)(2,1)S(1)} %bitcast.465, bf16[512,768]{1,0:T(8,128)(2,1)S(1)} %bitcast.449, f32[768]{0:T(1024)S(1)} %reshape.656, f32[1024]{0:T(1024)S(1)} %add_rsqrt_fusion), kind=kOutput, calls=%fused_computation.3 | convolution fusion | flops 3631742976 | bytes 9837568 | tf_op jit(solution)/shard_map/std,de->ste/dot_general | solution.py:518
  57.2 19.2 %shard_map.204 = bf16[1,512,768]{2,1,0:T(8,128)(2,1)S(1)} custom-call(bf16[1,1024,2304]{2,1,0:T(8,128)(2,1)S(1)} %fusion.1.q_ref.k_ref.v_ref, bf16[1,1024,2304]{2,1,0:T(8,128)(2,1)S(1)} %fusion.1.q_ref.k_ref.v_ref, bf16[1,1024,2304]{2,1,0:T(8,128)(2,1)S(1)} %fusion.1.q_ref.k_ref.v_ref, s32[1,512,1]{2,1,0:T(8,128)S(1)} %copy.110.seg_q_ref, ...), custom_call_target="tpu_custom_call" | custom-call | flops 1610612736 | bytes 6291456 | tf_op jit(solution)/shard_map/pallas_call | solution.py:172
  94.9 12.4 %collective-permute-done.9.refs_9_ = f32[4,1,128]{2,1,0:T(1,128)} collective-permute-done((f32[4,1,128]{2,1,0:T(1,128)S(1)}, f32[4,1,128]{2,1,0:T(1,128)}, u32[]{:S(2)}, u32[]{:S(2)}) %collective-permute-start.9) | collective-permute-done | bytes 2080 | tf_op jit(solution)/shard_map/ppermute | solution.py:375
  110.8 40.6 %shard_map.205 = (bf16[4,512,768]{2,1,0:T(8,128)(2,1)}, bf16[4,512,768]{2,1,0:T(8,128)(2,1)}, bf16[4,1536,768]{2,1,0:T(8,128)(2,1)}, bf16[4,1536,768]{2,1,0:T(8,128)(2,1)}) custom-call(s32[1]{0:T(128)} %bitcast.core_ref, bf16[4,128,768]{2,1,0:T(8,128)(2,1)} %bitcast.467, bf16[4,128,768]{2,1,0:T(8,128)(2,1)} %collective-permute-done.8.refs_1_, ...), custom_call_target="tpu_custom_call" | custom-call | flops 28991029248 | bytes 37748736 | tf_op jit(solution)/shard_map/pallas_call | solution.py:291
  151.4 3.4 dynamic-slice_bitcast_fusion.2
  164.7 16.7 %collective-permute-done.20 = bf16[4,128,768]{2,1,0:T(8,128)(2,1)} collective-permute-done((bf16[4,128,768]{2,1,0:T(8,128)(2,1)}, bf16[4,128,768]{2,1,0:T(8,128)(2,1)}, u32[]{:S(2)}, u32[]{:S(2)}) %collective-permute-start.20) | collective-permute-done | bytes 786464 | tf_op jit(solution)/shard_map/ppermute | solution.py:375
  182.6 4.0 collective-permute-done.17
  196.5 13.9 %collective-permute-done.24 = bf16[4,128,768]{2,1,0:T(8,128)(2,1)S(1)} collective-permute-done((bf16[4,128,768]{2,1,0:T(8,128)(2,1)S(1)}, bf16[4,128,768]{2,1,0:T(8,128)(2,1)S(1)}, u32[]{:S(2)}, u32[]{:S(2)}) %collective-permute-start.24) | collective-permute-done | bytes 786464 | tf_op jit(solution)/shard_map/ppermute | solution.py:375
  214.6 3.3 fusion.50.do_ref
  229.0 31.7 %shard_map.206 = (bf16[1,512,768]{2,1,0:T(8,128)(2,1)S(1)}, bf16[1,1024,768]{2,1,0:T(8,128)(2,1)S(1)}, bf16[1,1024,768]{2,1,0:T(8,128)(2,1)S(1)}, f32[1,6,4,1024]{3,2,1,0:T(4,128)S(1)}) custom-call(bf16[1,1024,2304]{2,1,0:T(8,128)(2,1)} %copy-done, bf16[1,1024,2304]{2,1,0:T(8,128)(2,1)} %copy-done, bf16[1,1024,2304]{2,1,0:T(8,128)(2,1)} %copy-done, ...), custom_call_target="tpu_custom_call" | custom-call | flops 4026531840 | bytes 12582912 | tf_op jit(solution)/shard_map/pallas_call | solution.py:200
  276.8 14.1 %collective-permute-done.29 = bf16[1,512,768]{2,1,0:T(8,128)(2,1)} collective-permute-done((bf16[1,512,768]{2,1,0:T(8,128)(2,1)}, bf16[1,512,768]{2,1,0:T(8,128)(2,1)}, u32[]{:S(2)}, u32[]{:S(2)}) %collective-permute-start.29) | collective-permute-done | bytes 786464 | tf_op jit(solution)/shard_map/ppermute | solution.py:375
  299.5 3.6 collective-permute-done.30
  321.4 20.6 %collective-permute-done.31 = bf16[4,1,192,768]{3,2,0,1:T(8,128)(2,1)} collective-permute-done((bf16[4,1,192,768]{3,2,0,1:T(8,128)(2,1)}, bf16[4,1,192,768]{3,2,0,1:T(8,128)(2,1)}, u32[]{:S(2)}, u32[]{:S(2)}) %collective-permute-start.31) | collective-permute-done | bytes 1179680 | tf_op jit(solution)/shard_map/ppermute | solution.py:342
  353.9 26.1 %collective-permute-done.36 = bf16[832,768]{1,0:T(8,128)(2,1)} collective-permute-done((bf16[832,768]{1,0:T(8,128)(2,1)}, bf16[832,768]{1,0:T(8,128)(2,1)}, u32[]{:S(2)}, u32[]{:S(2)}) %collective-permute-start.36) | collective-permute-done | bytes 1277984 | tf_op jit(solution)/shard_map/ppermute | solution.py:375
  390.5 4.1 fusion.32
  397.0 18.9 %collective-permute-done.37 = bf16[4,1,192,768]{3,2,0,1:T(8,128)(2,1)S(1)} collective-permute-done((bf16[4,1,192,768]{3,2,0,1:T(8,128)(2,1)S(1)}, bf16[4,1,192,768]{3,2,0,1:T(8,128)(2,1)S(1)}, u32[]{:S(2)}, u32[]{:S(2)}) %collective-permute-start.37) | collective-permute-done | bytes 1179680 | tf_op jit(solution)/shard_map/ppermute | solution.py:342
  432.7 19.6 %collective-permute-done.45 = bf16[104,768]{1,0:T(8,128)(2,1)S(1)} collective-permute-done((bf16[104,768]{1,0:T(8,128)(2,1)S(1)}, bf16[104,768]{1,0:T(8,128)(2,1)S(1)}, u32[]{:S(2)}, u32[]{:S(2)}) %collective-permute-start.45) | collective-permute-done | bytes 159776 | tf_op jit(solution)/shard_map/ppermute | solution.py:759
  463.9 20.9 %collective-permute-done.51 = bf16[104,768]{1,0:T(8,128)(2,1)S(1)} collective-permute-done((bf16[104,768]{1,0:T(8,128)(2,1)S(1)}, bf16[104,768]{1,0:T(8,128)(2,1)S(1)}, u32[]{:S(2)}, u32[]{:S(2)}) %collective-permute-start.51) | collective-permute-done | bytes 159776 | tf_op jit(solution)/shard_map/ppermute | solution.py:759
  494.7 19.9 %collective-permute-done.53 = bf16[4,1,192,768]{3,2,0,1:T(8,128)(2,1)S(1)} collective-permute-done((bf16[4,1,192,768]{3,2,0,1:T(8,128)(2,1)S(1)}, bf16[4,1,192,768]{3,2,0,1:T(8,128)(2,1)S(1)}, u32[]{:S(2)}, u32[]{:S(2)}) %collective-permute-start.53) | collective-permute-done | bytes 1179680 | tf_op jit(solution)/shard_map/ppermute | solution.py:342
  528.3 20.9 %collective-permute-done.62 = bf16[104,768]{1,0:T(8,128)(2,1)S(1)} collective-permute-done((bf16[104,768]{1,0:T(8,128)(2,1)S(1)}, bf16[104,768]{1,0:T(8,128)(2,1)S(1)}, u32[]{:S(2)}, u32[]{:S(2)}) %collective-permute-start.62) | collective-permute-done | bytes 159776 | tf_op jit(solution)/shard_map/ppermute | solution.py:772
  560.5 20.9 %collective-permute-done.68 = bf16[104,768]{1,0:T(8,128)(2,1)S(1)} collective-permute-done((bf16[104,768]{1,0:T(8,128)(2,1)S(1)}, bf16[104,768]{1,0:T(8,128)(2,1)S(1)}, u32[]{:S(2)}, u32[]{:S(2)}) %collective-permute-start.68) | collective-permute-done | bytes 159776 | tf_op jit(solution)/shard_map/ppermute | solution.py:772
  592.7 20.9 %collective-permute-done.74 = bf16[104,768]{1,0:T(8,128)(2,1)S(1)} collective-permute-done((bf16[104,768]{1,0:T(8,128)(2,1)S(1)}, bf16[104,768]{1,0:T(8,128)(2,1)S(1)}, u32[]{:S(2)}, u32[]{:S(2)}) %collective-permute-start.74) | collective-permute-done | bytes 159776 | tf_op jit(solution)/shard_map/ppermute | solution.py:772
  625.2 21.1 %collective-permute-done.80 = bf16[104,768]{1,0:T(8,128)(2,1)S(1)} collective-permute-done((bf16[104,768]{1,0:T(8,128)(2,1)S(1)}, bf16[104,768]{1,0:T(8,128)(2,1)S(1)}, u32[]{:S(2)}, u32[]{:S(2)}) %collective-permute-start.80) | collective-permute-done | bytes 159776 | tf_op jit(solution)/shard_map/ppermute | solution.py:772
  (426 shorter events, 272.3 us)
Async XLA Ops:
  36.0 42.6 %collective-permute-start.7 = (bf16[384,768]{1,0:T(8,128)(2,1)}, bf16[384,768]{1,0:T(8,128)(2,1)}, u32[]{:S(2)}, u32[]{:S(2)}) collective-permute-start(bf16[384,768]{1,0:T(8,128)(2,1)} %param.18), channel_id=1, source_target_pairs={{0,1},{1,0},{2,3},{3,2},{4,5},{5,4},{6,7},{7,6},{8,9},{9,8},{10,11... | collective-permute-start | bytes 1769480 | tf_op jit(solution)/shard_map/ppermute | solution.py:375
  55.4 39.5 %collective-permute-start.12 = (bf16[4,128,768]{2,1,0:T(8,128)(2,1)}, bf16[4,128,768]{2,1,0:T(8,128)(2,1)}, u32[]{:S(2)}, u32[]{:S(2)}) collective-permute-start(bf16[4,128,768]{2,1,0:T(8,128)(2,1)} %get-tuple-element.431), channel_id=1, source_target_pairs={{0,1},{1,0},{2,3},{3,2},{4,5},{5,4},{6,7},{7,6},{8,9},{9,8},{10,11... | collective-permute-start | bytes 2359304 | tf_op jit(solution)/shard_map/ppermute | solution.py:375
  158.3 28.4 %collective-permute-start.17 = (bf16[4,1,192,768]{3,2,0,1:T(8,128)(2,1)}, bf16[4,1,192,768]{3,2,0,1:T(8,128)(2,1)}, u32[]{:S(2)}, u32[]{:S(2)}) collective-permute-start(bf16[4,1,192,768]{3,2,0,1:T(8,128)(2,1)} %get-tuple-element.219), channel_id=1, source_target_pairs={{0,8},{2,10},{8,16},{10,18},{16,24},{18,26},{24,28},{26,30},{28,20... | collective-permute-start | bytes 3538952 | tf_op jit(solution)/shard_map/ppermute | solution.py:342
  225.6 35.1 %collective-permute-start.25 = (bf16[4,1,192,768]{3,2,0,1:T(8,128)(2,1)}, bf16[4,1,192,768]{3,2,0,1:T(8,128)(2,1)}, u32[]{:S(2)}, u32[]{:S(2)}) collective-permute-start(bf16[4,1,192,768]{3,2,0,1:T(8,128)(2,1)} %add_convert_fusion.13), channel_id=1, source_target_pairs={{0,8},{2,10},{8,16},{10,18},{16,24},{18,26},{24,28},{26,30},{28,20... | collective-permute-start | bytes 3538952 | tf_op jit(solution)/shard_map/ppermute | solution.py:342
  227.2 33.5 %collective-permute-start.26 = (bf16[4,1,192,768]{3,2,0,1:T(8,128)(2,1)}, bf16[4,1,192,768]{3,2,0,1:T(8,128)(2,1)}, u32[]{:S(2)}, u32[]{:S(2)}) collective-permute-start(bf16[4,1,192,768]{3,2,0,1:T(8,128)(2,1)} %add_convert_fusion.12), channel_id=1, source_target_pairs={{4,12},{6,14},{12,20},{14,22},{20,28},{22,30},{28,24},{30,26},{24,... | collective-permute-start | bytes 3538952 | tf_op jit(solution)/shard_map/ppermute | solution.py:342
  271.8 31.4 %collective-permute-start.30 = (bf16[1,512,768]{2,1,0:T(8,128)(2,1)S(1)}, bf16[1,512,768]{2,1,0:T(8,128)(2,1)}, u32[]{:S(2)}, u32[]{:S(2)}) collective-permute-start(bf16[1,512,768]{2,1,0:T(8,128)(2,1)S(1)} %slice.103), channel_id=1, source_target_pairs={{0,1},{1,0},{2,3},{3,2},{4,5},{5,4},{6,7},{7,6},{8,9},{9,8},{10,11... | collective-permute-start | bytes 2359304 | tf_op jit(solution)/shard_map/ppermute | solution.py:375
  313.4 28.7 %collective-permute-start.31 = (bf16[4,1,192,768]{3,2,0,1:T(8,128)(2,1)}, bf16[4,1,192,768]{3,2,0,1:T(8,128)(2,1)}, u32[]{:S(2)}, u32[]{:S(2)}) collective-permute-start(bf16[4,1,192,768]{3,2,0,1:T(8,128)(2,1)} %add_convert_fusion.9), channel_id=1, source_target_pairs={{0,8},{2,10},{8,16},{10,18},{16,24},{18,26},{24,28},{26,30},{28,20... | collective-permute-start | bytes 3538952 | tf_op jit(solution)/shard_map/ppermute | solution.py:342
  315.0 28.4 %collective-permute-start.32 = (bf16[4,1,192,768]{3,2,0,1:T(8,128)(2,1)}, bf16[4,1,192,768]{3,2,0,1:T(8,128)(2,1)}, u32[]{:S(2)}, u32[]{:S(2)}) collective-permute-start(bf16[4,1,192,768]{3,2,0,1:T(8,128)(2,1)} %add_convert_fusion.8), channel_id=1, source_target_pairs={{4,12},{6,14},{12,20},{14,22},{20,28},{22,30},{28,24},{30,26},{24,... | collective-permute-start | bytes 3538952 | tf_op jit(solution)/shard_map/ppermute | solution.py:342
  350.3 29.7 %collective-permute-start.36 = (bf16[832,768]{1,0:T(8,128)(2,1)}, bf16[832,768]{1,0:T(8,128)(2,1)}, u32[]{:S(2)}, u32[]{:S(2)}) collective-permute-start(bf16[832,768]{1,0:T(8,128)(2,1)} %dynamic-slice_bitcast_fusion.1), channel_id=1, source_target_pairs={{0,1},{1,0},{2,3},{3,2},{4,5},{5,4},{6,7},{7,6},{8,9},{9,8},{10,11... | collective-permute-start | bytes 3833864 | tf_op jit(solution)/shard_map/ppermute | solution.py:375
  351.8 29.8 %collective-permute-start.34 = (bf16[4,1,192,768]{3,2,0,1:T(8,128)(2,1)}, bf16[4,1,192,768]{3,2,0,1:T(8,128)(2,1)}, u32[]{:S(2)}, u32[]{:S(2)}) collective-permute-start(bf16[4,1,192,768]{3,2,0,1:T(8,128)(2,1)} %add_convert_fusion.7), channel_id=1, source_target_pairs={{0,8},{2,10},{8,16},{10,18},{16,24},{18,26},{24,28},{26,30},{28,20... | collective-permute-start | bytes 3538952 | tf_op jit(solution)/shard_map/ppermute | solution.py:342
  353.3 28.3 %collective-permute-start.35 = (bf16[4,1,192,768]{3,2,0,1:T(8,128)(2,1)}, bf16[4,1,192,768]{3,2,0,1:T(8,128)(2,1)}, u32[]{:S(2)}, u32[]{:S(2)}) collective-permute-start(bf16[4,1,192,768]{3,2,0,1:T(8,128)(2,1)} %add_convert_fusion.6), channel_id=1, source_target_pairs={{4,12},{6,14},{12,20},{14,22},{20,28},{22,30},{28,24},{30,26},{24,... | collective-permute-start | bytes 3538952 | tf_op jit(solution)/shard_map/ppermute | solution.py:342
  420.9 31.9 %collective-permute-start.41 = (bf16[4,1,192,768]{3,2,0,1:T(8,128)(2,1)S(1)}, bf16[4,1,192,768]{3,2,0,1:T(8,128)(2,1)S(1)}, u32[]{:S(2)}, u32[]{:S(2)}) collective-permute-start(bf16[4,1,192,768]{3,2,0,1:T(8,128)(2,1)S(1)} %add_convert_fusion.3), channel_id=1, source_target_pairs={{0,8},{2,10},{8,16},{10,18},{16,24},{18,26},{24,28},{26,30},{28,20... | collective-permute-start | bytes 3538952 | tf_op jit(solution)/shard_map/ppermute | solution.py:342
  421.7 31.2 %collective-permute-start.42 = (bf16[4,1,192,768]{3,2,0,1:T(8,128)(2,1)S(1)}, bf16[4,1,192,768]{3,2,0,1:T(8,128)(2,1)S(1)}, u32[]{:S(2)}, u32[]{:S(2)}) collective-permute-start(bf16[4,1,192,768]{3,2,0,1:T(8,128)(2,1)S(1)} %add_convert_fusion.2), channel_id=1, source_target_pairs={{4,12},{6,14},{12,20},{14,22},{20,28},{22,30},{28,24},{30,26},{24,... | collective-permute-start | bytes 3538952 | tf_op jit(solution)/shard_map/ppermute | solution.py:342
  453.4 31.4 %collective-permute-start.47 = (bf16[4,1,192,768]{3,2,0,1:T(8,128)(2,1)S(1)}, bf16[4,1,192,768]{3,2,0,1:T(8,128)(2,1)S(1)}, u32[]{:S(2)}, u32[]{:S(2)}) collective-permute-start(bf16[4,1,192,768]{3,2,0,1:T(8,128)(2,1)S(1)} %collective-permute-done.41), channel_id=1, source_target_pairs={{0,8},{2,10},{8,16},{10,18},{16,24},{18,26},{24,28},{26,30},{28,20... | collective-permute-start | bytes 3538952 | tf_op jit(solution)/shard_map/ppermute | solution.py:342
  454.2 30.7 %collective-permute-start.48 = (bf16[4,1,192,768]{3,2,0,1:T(8,128)(2,1)S(1)}, bf16[4,1,192,768]{3,2,0,1:T(8,128)(2,1)S(1)}, u32[]{:S(2)}, u32[]{:S(2)}) collective-permute-start(bf16[4,1,192,768]{3,2,0,1:T(8,128)(2,1)S(1)} %collective-permute-done.42), channel_id=1, source_target_pairs={{4,12},{6,14},{12,20},{14,22},{20,28},{22,30},{28,24},{30,26},{24,... | collective-permute-start | bytes 3538952 | tf_op jit(solution)/shard_map/ppermute | solution.py:342
  485.8 28.8 %collective-permute-start.53 = (bf16[4,1,192,768]{3,2,0,1:T(8,128)(2,1)S(1)}, bf16[4,1,192,768]{3,2,0,1:T(8,128)(2,1)S(1)}, u32[]{:S(2)}, u32[]{:S(2)}) collective-permute-start(bf16[4,1,192,768]{3,2,0,1:T(8,128)(2,1)S(1)} %collective-permute-done.47), channel_id=1, source_target_pairs={{0,8},{2,10},{8,16},{10,18},{16,24},{18,26},{24,28},{26,30},{28,20... | collective-permute-start | bytes 3538952 | tf_op jit(solution)/shard_map/ppermute | solution.py:342
  517.8 31.6 %collective-permute-start.58 = (bf16[4,1,192,768]{3,2,0,1:T(8,128)(2,1)S(1)}, bf16[4,1,192,768]{3,2,0,1:T(8,128)(2,1)S(1)}, u32[]{:S(2)}, u32[]{:S(2)}) collective-permute-start(bf16[4,1,192,768]{3,2,0,1:T(8,128)(2,1)S(1)} %collective-permute-done.53), channel_id=1, source_target_pairs={{0,8},{2,10},{8,16},{10,18},{16,24},{18,26},{24,28},{26,30},{28,20... | collective-permute-start | bytes 3538952 | tf_op jit(solution)/shard_map/ppermute | solution.py:342
  518.3 31.1 %collective-permute-start.59 = (bf16[4,1,192,768]{3,2,0,1:T(8,128)(2,1)S(1)}, bf16[4,1,192,768]{3,2,0,1:T(8,128)(2,1)S(1)}, u32[]{:S(2)}, u32[]{:S(2)}) collective-permute-start(bf16[4,1,192,768]{3,2,0,1:T(8,128)(2,1)S(1)} %collective-permute-done.54), channel_id=1, source_target_pairs={{4,12},{6,14},{12,20},{14,22},{20,28},{22,30},{28,24},{30,26},{24,... | collective-permute-start | bytes 3538952 | tf_op jit(solution)/shard_map/ppermute | solution.py:342
  550.0 31.6 %collective-permute-start.64 = (bf16[4,1,192,768]{3,2,0,1:T(8,128)(2,1)S(1)}, bf16[4,1,192,768]{3,2,0,1:T(8,128)(2,1)S(1)}, u32[]{:S(2)}, u32[]{:S(2)}) collective-permute-start(bf16[4,1,192,768]{3,2,0,1:T(8,128)(2,1)S(1)} %collective-permute-done.58), channel_id=1, source_target_pairs={{0,8},{2,10},{8,16},{10,18},{16,24},{18,26},{24,28},{26,30},{28,20... | collective-permute-start | bytes 3538952 | tf_op jit(solution)/shard_map/ppermute | solution.py:342
  550.5 31.1 %collective-permute-start.65 = (bf16[4,1,192,768]{3,2,0,1:T(8,128)(2,1)S(1)}, bf16[4,1,192,768]{3,2,0,1:T(8,128)(2,1)S(1)}, u32[]{:S(2)}, u32[]{:S(2)}) collective-permute-start(bf16[4,1,192,768]{3,2,0,1:T(8,128)(2,1)S(1)} %collective-permute-done.59), channel_id=1, source_target_pairs={{4,12},{6,14},{12,20},{14,22},{20,28},{22,30},{28,24},{30,26},{24,... | collective-permute-start | bytes 3538952 | tf_op jit(solution)/shard_map/ppermute | solution.py:342
  582.2 32.1 %collective-permute-start.70 = (bf16[4,1,192,768]{3,2,0,1:T(8,128)(2,1)S(1)}, bf16[4,1,192,768]{3,2,0,1:T(8,128)(2,1)S(1)}, u32[]{:S(2)}, u32[]{:S(2)}) collective-permute-start(bf16[4,1,192,768]{3,2,0,1:T(8,128)(2,1)S(1)} %collective-permute-done.64), channel_id=1, source_target_pairs={{0,8},{2,10},{8,16},{10,18},{16,24},{18,26},{24,28},{26,30},{28,20... | collective-permute-start | bytes 3538952 | tf_op jit(solution)/shard_map/ppermute | solution.py:342
  583.2 31.1 %collective-permute-start.71 = (bf16[4,1,192,768]{3,2,0,1:T(8,128)(2,1)S(1)}, bf16[4,1,192,768]{3,2,0,1:T(8,128)(2,1)S(1)}, u32[]{:S(2)}, u32[]{:S(2)}) collective-permute-start(bf16[4,1,192,768]{3,2,0,1:T(8,128)(2,1)S(1)} %collective-permute-done.65), channel_id=1, source_target_pairs={{4,12},{6,14},{12,20},{14,22},{20,28},{22,30},{28,24},{30,26},{24,... | collective-permute-start | bytes 3538952 | tf_op jit(solution)/shard_map/ppermute | solution.py:342
  614.9 31.4 %collective-permute-start.76 = (bf16[4,1,192,768]{3,2,0,1:T(8,128)(2,1)S(1)}, bf16[4,1,192,768]{3,2,0,1:T(8,128)(2,1)}, u32[]{:S(2)}, u32[]{:S(2)}) collective-permute-start(bf16[4,1,192,768]{3,2,0,1:T(8,128)(2,1)S(1)} %collective-permute-done.70), channel_id=1, source_target_pairs={{0,8},{2,10},{8,16},{10,18},{16,24},{18,26},{24,28},{26,30},{28,20... | collective-permute-start | bytes 3538952 | tf_op jit(solution)/shard_map/ppermute | solution.py:342
  616.5 29.8 %collective-permute-start.77 = (bf16[4,1,192,768]{3,2,0,1:T(8,128)(2,1)S(1)}, bf16[4,1,192,768]{3,2,0,1:T(8,128)(2,1)}, u32[]{:S(2)}, u32[]{:S(2)}) collective-permute-start(bf16[4,1,192,768]{3,2,0,1:T(8,128)(2,1)S(1)} %collective-permute-done.71), channel_id=1, source_target_pairs={{4,12},{6,14},{12,20},{14,22},{20,28},{22,30},{28,24},{30,26},{24,... | collective-permute-start | bytes 3538952 | tf_op jit(solution)/shard_map/ppermute | solution.py:342
  (114 other events, 1371.1 us)

commit v4 on v3

--- a/solution.py
+++ b/solution.py
@@ -124,7 +124,8 @@
             probs = parts * (1.0 / jnp.sum(parts, axis=1, keepdims=True))
             grad_probs = dot_nt(grad_out, values)
             delta = jnp.sum(probs * grad_probs, axis=1, keepdims=True)
-            grad_scores = (probs * (grad_probs - delta)).astype(BF16)
+            wide = probs * (grad_probs - delta)
+            grad_scores = wide.astype(BF16)
             dv_acc[...] += dot_tn(grad_out, probs.astype(BF16))
             dk_acc[...] += dot_tn(queries, grad_scores)
             dq = (dot_nn(grad_scores, keys) * scale.astype(np.float32)).astype(BF16)
@@ -132,7 +133,6 @@
                 dq_ref[0, rows, :] = dq
             else:
                 dq_ref[0, rows, :] = jnp.where(mine, dq, dq_ref[0, rows, :])
-            wide = grad_scores.astype(F32)
             start = span - tile - tile * a
             for b in range(blocks):
                 sum_ref[b, :, start : start + span] += wide[:, b * span : (b + 1) * span]
@@ -474,7 +474,8 @@
         (tokens_far, output_weight, segment_ids)
     )
     tokens_all = rotated(tokens, tokens_far, 1)
-    seg_all = rotated(late_ids, fetch(late_ids), 1)
+    ids_far, late_out = lax.optimization_barrier((fetch(late_ids), late_out))
+    seg_all = rotated(late_ids, ids_far, 1)
     full_out = gather_whole(late_out)
 
     first_expert = grp_index * owned if two else 0
@@ -489,21 +490,21 @@
     dispatch = in_slot.astype(BF16)
 
     def to_slots(rows):
-        placed = jnp.einsum("stc,std->csd", dispatch, rows, preferred_element_type=F32)
-        return placed.astype(BF16).reshape(experts, slots, model)
-
-    def to_side(*arrays):
+        parts = jnp.split(dispatch, 2, axis=2) if two else [dispatch]
+        placed = [
+            jnp.einsum("stc,std->csd", part, rows, preferred_element_type=F32) for part in parts
+        ]
+        return [value.astype(BF16).reshape(-1, slots, model) for value in placed]
+
+    def to_side(parts):
         if two:
-            far = lax.optimization_barrier([swap_groups(placed[owned:]) for placed in arrays])
-            near = [[placed[:owned], other] for placed, other in zip(arrays, far)]
-        else:
-            near = []
-            for placed in arrays:
-                split = placed.reshape((groups, owned) + placed.shape[1:])
-                moved = lax.all_to_all(split, "grp", 0, 0, tiled=False)
-                near.append([moved[i] for i in range(groups)])
-        both = [pieces + [swap_cores(piece, reps) for piece in pieces] for pieces in near]
-        return both if len(both) > 1 else both[0]
+            return [parts[0], swap_groups(parts[1])]
+        split = parts[0].reshape((groups, owned) + parts[0].shape[1:])
+        moved = lax.all_to_all(split, "grp", 0, 0, tiled=False)
+        return [moved[i] for i in range(groups)]
+
+    def to_cores(pieces):
+        return pieces + [swap_cores(piece, reps) for piece in pieces]
 
     def from_side(rows):
         if two:
@@ -519,7 +520,9 @@
         "std,de->ste", normed_all, full_qkv, preferred_element_type=F32
     ).astype(BF16)
 
-    projected, cot_slots = lax.optimization_barrier((projected, to_slots(out_grad)))
+    projected, full_out, cot_slots = lax.optimization_barrier(
+        (projected, full_out, to_slots(out_grad))
+    )
     cot_rows = to_side(cot_slots)
 
     bucket_line = jnp.pad(rel_bucket, (0, 1), constant_values=buckets)
@@ -536,6 +539,8 @@
     ).reshape(head_count // PAIR, PAIR * groups, 2 * span)
 
     attended = attention(projected, segment_ids, seg_all, window, span, head_count)
+    attended, cot_rows = lax.optimization_barrier((attended, cot_rows))
+    cot_rows = to_cores(cot_rows)
     residual = input_tokens + jnp.einsum(
         "std,de->ste", attended, full_out, preferred_element_type=F32
     )
@@ -549,7 +554,11 @@
     gate_slots = jnp.sum(jnp.where(in_slot, gate_prob[..., None], 0.0), axis=1)
     gate_slots = jnp.moveaxis(gate_slots.reshape(seqs, experts, most), 0, 2).reshape(experts, slots)
 
-    expert_in, gate_rows = to_side(to_slots(normed_ffn), gate_slots[:, None, :])
+    gate_parts = jnp.split(gate_slots[:, None, :], groups if two else 1)
+    expert_in, gate_rows = lax.optimization_barrier(
+        (to_side(to_slots(normed_ffn)), to_side(gate_parts))
+    )
+    expert_in, gate_rows = to_cores(expert_in), to_cores(gate_rows)
     up_parts = w_up.reshape(owned, CORES, part, model)
     down_parts = w_down.reshape(owned, CORES, part, model)
     shard = part // chips

time: 679 us -> 673 us (level)
  local copies, waits for them, and re-layouts: 59.1 us -> 45.7 us
    slice x5 -> x0, local copies, waits for them, and re-layouts: 7.09 us -> none  [the longest x3 4.8 us: to_side(): placed[owned:]]
    unnamed x117 -> x125, local copies, waits for them, and re-layouts: 19.9 us -> 20.3 us
  transfers between devices with their start and end apart: 84 -> 84, of which waited for: 32 -> 35; matrix products, arithmetic and copies ran while one was open for 21% -> 19% of each run, Pallas kernels for 8% -> 8%
where the time goes in v4:
time: 673 us; the launch traced here: 664 us
  waiting for transfers between devices  306 us (45%)
  other arithmetic  115 us (17%)
  Pallas kernels  91.7 us (14%)
  starting transfers between devices  69.3 us (10%)
  local copies, waits for them, and re-layouts  45.7 us (7%)
  matrix products  34.1 us (5%)
    ppermute x8, waiting for transfers between devices, stage(): above = lax.ppermute(above, 'rep', up_hop)  127 us
    ppermute x13, waiting for transfers between devices, swap_groups(): return lax.ppermute(values, 'grp', [(0, 1), (1, 0)])  99.8 us
    ppermute x28, waiting for transfers between devices, move(): return lax.ppermute(self.held, 'rep', self.hop)  71.5 us
    dynamic_update_slice x32, other arithmetic, store(): lax.dynamic_update_slice(stored[i], value.astype(F32)[:, None], (first, a...  57.6 us
    pallas_call x1, Pallas kernels, run_experts(): pl.pallas_call(functools.partial(expert_kernel, len(sizes)), grid_spec=pl...  40.6 us
    convert_element_type x14, other arithmetic, take(): (arrived.astype(F32) + self.pick(-step - 1).astype(F32)).astype(BF16)  34.3 us
    pallas_call x1, Pallas kernels, attention_back(): pl.pallas_call(functools.partial(attention_back_kernel, scale), grid=(seq...  32 us
    ppermute x28, starting transfers between devices, move(): return lax.ppermute(self.held, 'rep', self.hop)  28.9 us
  transfers between devices with their start and end apart: 84, of which 35 were waited for; matrix products, arithmetic and copies ran while one was open for 19% of the time, Pallas kernels for 8%

profile of v4, /device:TPU:0, one launch (start us, length us, event | category | flops | bytes accessed | tf_op | source)
XLA Modules:
  0.0 664.3 jit_solution(10600684155079884757)
XLA Ops:
  20.9 11.0 %collective-permute-done.3 = bf16[1,512,768]{2,1,0:T(8,128)(2,1)S(1)} collective-permute-done((bf16[1,512,768]{2,1,0:T(8,128)(2,1)}, bf16[1,512,768]{2,1,0:T(8,128)(2,1)S(1)}, u32[]{:S(2)}, u32[]{:S(2)}) %collective-permute-start.3) | collective-permute-done | bytes 786464 | tf_op jit(solution)/shard_map/ppermute | solution.py:375
  41.5 8.5 %fusion.1.q_ref.k_ref.v_ref = bf16[1,1024,2304]{2,1,0:T(8,128)(2,1)} fusion(bf16[768,2304]{1,0:T(8,128)(2,1)} %constant_dynamic-update-slice_fusion.2, bf16[512,768]{1,0:T(8,128)(2,1)S(1)} %bitcast.478, bf16[512,768]{1,0:T(8,128)(2,1)S(1)} %bitcast.463, f32[768]{0:T(1024)S(1)} %reshape.673, f32[1024]{0:T(1024)S(1)} %add_rsqrt_fusion), kind=kOutput, calls=%fused_computation.3 | convolution fusion | flops 3631742976 | bytes 9837568 | tf_op jit(solution)/shard_map/std,de->ste/dot_general | solution.py:519
  57.2 19.2 %shard_map.204 = bf16[1,512,768]{2,1,0:T(8,128)(2,1)S(1)} custom-call(bf16[1,1024,2304]{2,1,0:T(8,128)(2,1)S(1)} %copy-done, bf16[1,1024,2304]{2,1,0:T(8,128)(2,1)S(1)} %copy-done, bf16[1,1024,2304]{2,1,0:T(8,128)(2,1)S(1)} %copy-done, s32[1,512,1]{2,1,0:T(8,128)S(1)} %copy.106.seg_q_ref, s32[1,1,1024]{2,1,0:T(1,128)S(1)} %add_bitcast_fusion.1.seg_k_ref, ...), custom_call_target="tpu_custom_call" | custom-call | flops 1610612736 | bytes 6291456 | tf_op jit(solution)/shard_map/pallas_call | solution.py:172
  85.7 13.5 %collective-permute-done.10.refs_9_ = f32[4,1,128]{2,1,0:T(1,128)S(1)} collective-permute-done((f32[4,1,128]{2,1,0:T(1,128)S(1)}, f32[4,1,128]{2,1,0:T(1,128)S(1)}, u32[]{:S(2)}, u32[]{:S(2)}) %collective-permute-start.10) | collective-permute-done | bytes 2080 | tf_op jit(solution)/shard_map/ppermute | solution.py:375
  103.0 40.6 %shard_map.205 = (bf16[4,512,768]{2,1,0:T(8,128)(2,1)}, bf16[4,512,768]{2,1,0:T(8,128)(2,1)}, bf16[4,1536,768]{2,1,0:T(8,128)(2,1)}, bf16[4,1536,768]{2,1,0:T(8,128)(2,1)}) custom-call(s32[1]{0:T(128)} %bitcast.core_ref, bf16[4,128,768]{2,1,0:T(8,128)(2,1)} %bitcast.29.refs_0_, bf16[4,128,768]{2,1,0:T(8,128)(2,1)} %collective-permute-done.9.refs_1_, ...), custom_call_target="tpu_custom_call" | custom-call | flops 28991029248 | bytes 37748736 | tf_op jit(solution)/shard_map/pallas_call | solution.py:291
  143.6 3.4 dynamic-slice_bitcast_fusion.2
  158.0 15.5 %collective-permute-done.20 = bf16[4,128,768]{2,1,0:T(8,128)(2,1)} collective-permute-done((bf16[4,128,768]{2,1,0:T(8,128)(2,1)}, bf16[4,128,768]{2,1,0:T(8,128)(2,1)}, u32[]{:S(2)}, u32[]{:S(2)}) %collective-permute-start.20) | collective-permute-done | bytes 786464 | tf_op jit(solution)/shard_map/ppermute | solution.py:375
  174.8 4.0 collective-permute-done.17
  189.6 12.9 %collective-permute-done.24 = bf16[4,128,768]{2,1,0:T(8,128)(2,1)S(1)} collective-permute-done((bf16[4,128,768]{2,1,0:T(8,128)(2,1)S(1)}, bf16[4,128,768]{2,1,0:T(8,128)(2,1)S(1)}, u32[]{:S(2)}, u32[]{:S(2)}) %collective-permute-start.24) | collective-permute-done | bytes 786464 | tf_op jit(solution)/shard_map/ppermute | solution.py:375
  206.7 3.3 fusion.37.do_ref
  222.4 32.0 %shard_map.206 = (bf16[1,512,768]{2,1,0:T(8,128)(2,1)S(1)}, bf16[1,1024,768]{2,1,0:T(8,128)(2,1)S(1)}, bf16[1,1024,768]{2,1,0:T(8,128)(2,1)S(1)}, f32[1,6,4,1024]{3,2,1,0:T(4,128)S(1)}) custom-call(bf16[1,1024,2304]{2,1,0:T(8,128)(2,1)} %fusion.1.q_ref.k_ref.v_ref, bf16[1,1024,2304]{2,1,0:T(8,128)(2,1)} %fusion.1.q_ref.k_ref.v_ref, ...), custom_call_target="tpu_custom_call" | custom-call | flops 4026531840 | bytes 12582912 | tf_op jit(solution)/shard_map/pallas_call | solution.py:200
  270.1 14.5 %collective-permute-done.29 = bf16[1,512,768]{2,1,0:T(8,128)(2,1)} collective-permute-done((bf16[1,512,768]{2,1,0:T(8,128)(2,1)}, bf16[1,512,768]{2,1,0:T(8,128)(2,1)}, u32[]{:S(2)}, u32[]{:S(2)}) %collective-permute-start.29) | collective-permute-done | bytes 786464 | tf_op jit(solution)/shard_map/ppermute | solution.py:375
  293.4 3.6 collective-permute-done.30
  315.3 20.6 %collective-permute-done.31 = bf16[4,1,192,768]{3,2,0,1:T(8,128)(2,1)} collective-permute-done((bf16[4,1,192,768]{3,2,0,1:T(8,128)(2,1)}, bf16[4,1,192,768]{3,2,0,1:T(8,128)(2,1)}, u32[]{:S(2)}, u32[]{:S(2)}) %collective-permute-start.31) | collective-permute-done | bytes 1179680 | tf_op jit(solution)/shard_map/ppermute | solution.py:342
  346.6 27.3 %collective-permute-done.36 = bf16[832,768]{1,0:T(8,128)(2,1)} collective-permute-done((bf16[832,768]{1,0:T(8,128)(2,1)}, bf16[832,768]{1,0:T(8,128)(2,1)}, u32[]{:S(2)}, u32[]{:S(2)}) %collective-permute-start.36) | collective-permute-done | bytes 1277984 | tf_op jit(solution)/shard_map/ppermute | solution.py:375
  384.4 4.1 fusion.22
  390.9 18.9 %collective-permute-done.37 = bf16[4,1,192,768]{3,2,0,1:T(8,128)(2,1)S(1)} collective-permute-done((bf16[4,1,192,768]{3,2,0,1:T(8,128)(2,1)S(1)}, bf16[4,1,192,768]{3,2,0,1:T(8,128)(2,1)S(1)}, u32[]{:S(2)}, u32[]{:S(2)}) %collective-permute-start.37) | collective-permute-done | bytes 1179680 | tf_op jit(solution)/shard_map/ppermute | solution.py:342
  426.6 19.6 %collective-permute-done.45 = bf16[104,768]{1,0:T(8,128)(2,1)S(1)} collective-permute-done((bf16[104,768]{1,0:T(8,128)(2,1)S(1)}, bf16[104,768]{1,0:T(8,128)(2,1)S(1)}, u32[]{:S(2)}, u32[]{:S(2)}) %collective-permute-start.45) | collective-permute-done | bytes 159776 | tf_op jit(solution)/shard_map/ppermute | solution.py:768
  457.8 20.9 %collective-permute-done.51 = bf16[104,768]{1,0:T(8,128)(2,1)S(1)} collective-permute-done((bf16[104,768]{1,0:T(8,128)(2,1)S(1)}, bf16[104,768]{1,0:T(8,128)(2,1)S(1)}, u32[]{:S(2)}, u32[]{:S(2)}) %collective-permute-start.51) | collective-permute-done | bytes 159776 | tf_op jit(solution)/shard_map/ppermute | solution.py:768
  488.6 19.9 %collective-permute-done.53 = bf16[4,1,192,768]{3,2,0,1:T(8,128)(2,1)S(1)} collective-permute-done((bf16[4,1,192,768]{3,2,0,1:T(8,128)(2,1)S(1)}, bf16[4,1,192,768]{3,2,0,1:T(8,128)(2,1)S(1)}, u32[]{:S(2)}, u32[]{:S(2)}) %collective-permute-start.53) | collective-permute-done | bytes 1179680 | tf_op jit(solution)/shard_map/ppermute | solution.py:342
  522.2 20.9 %collective-permute-done.62 = bf16[104,768]{1,0:T(8,128)(2,1)S(1)} collective-permute-done((bf16[104,768]{1,0:T(8,128)(2,1)S(1)}, bf16[104,768]{1,0:T(8,128)(2,1)S(1)}, u32[]{:S(2)}, u32[]{:S(2)}) %collective-permute-start.62) | collective-permute-done | bytes 159776 | tf_op jit(solution)/shard_map/ppermute | solution.py:781
  554.4 20.9 %collective-permute-done.68 = bf16[104,768]{1,0:T(8,128)(2,1)S(1)} collective-permute-done((bf16[104,768]{1,0:T(8,128)(2,1)S(1)}, bf16[104,768]{1,0:T(8,128)(2,1)S(1)}, u32[]{:S(2)}, u32[]{:S(2)}) %collective-permute-start.68) | collective-permute-done | bytes 159776 | tf_op jit(solution)/shard_map/ppermute | solution.py:781
  586.6 20.9 %collective-permute-done.74 = bf16[104,768]{1,0:T(8,128)(2,1)S(1)} collective-permute-done((bf16[104,768]{1,0:T(8,128)(2,1)S(1)}, bf16[104,768]{1,0:T(8,128)(2,1)S(1)}, u32[]{:S(2)}, u32[]{:S(2)}) %collective-permute-start.74) | collective-permute-done | bytes 159776 | tf_op jit(solution)/shard_map/ppermute | solution.py:781
  619.1 21.1 %collective-permute-done.80 = bf16[104,768]{1,0:T(8,128)(2,1)S(1)} collective-permute-done((bf16[104,768]{1,0:T(8,128)(2,1)S(1)}, bf16[104,768]{1,0:T(8,128)(2,1)S(1)}, u32[]{:S(2)}, u32[]{:S(2)}) %collective-permute-start.80) | collective-permute-done | bytes 159776 | tf_op jit(solution)/shard_map/ppermute | solution.py:781
  (433 shorter events, 264.8 us)
Async XLA Ops:
  150.2 28.6 %collective-permute-start.17 = (bf16[4,1,192,768]{3,2,0,1:T(8,128)(2,1)}, bf16[4,1,192,768]{3,2,0,1:T(8,128)(2,1)}, u32[]{:S(2)}, u32[]{:S(2)}) collective-permute-start(bf16[4,1,192,768]{3,2,0,1:T(8,128)(2,1)} %get-tuple-element.237), channel_id=1, source_target_pairs={{0,8},{2,10},{8,16},{10,18},{16,24},{18,26},{24,28},{26,30},{28,20... | collective-permute-start | bytes 3538952 | tf_op jit(solution)/shard_map/ppermute | solution.py:342
  151.6 28.3 %collective-permute-start.18 = (bf16[4,1,192,768]{3,2,0,1:T(8,128)(2,1)}, bf16[4,1,192,768]{3,2,0,1:T(8,128)(2,1)}, u32[]{:S(2)}, u32[]{:S(2)}) collective-permute-start(bf16[4,1,192,768]{3,2,0,1:T(8,128)(2,1)} %get-tuple-element.238), channel_id=1, source_target_pairs={{4,12},{6,14},{12,20},{14,22},{20,28},{22,30},{28,24},{30,26},{24,... | collective-permute-start | bytes 3538952 | tf_op jit(solution)/shard_map/ppermute | solution.py:342
  219.0 35.4 %collective-permute-start.25 = (bf16[4,1,192,768]{3,2,0,1:T(8,128)(2,1)}, bf16[4,1,192,768]{3,2,0,1:T(8,128)(2,1)}, u32[]{:S(2)}, u32[]{:S(2)}) collective-permute-start(bf16[4,1,192,768]{3,2,0,1:T(8,128)(2,1)} %add_convert_fusion.13), channel_id=1, source_target_pairs={{0,8},{2,10},{8,16},{10,18},{16,24},{18,26},{24,28},{26,30},{28,20... | collective-permute-start | bytes 3538952 | tf_op jit(solution)/shard_map/ppermute | solution.py:342
  220.6 33.8 %collective-permute-start.26 = (bf16[4,1,192,768]{3,2,0,1:T(8,128)(2,1)}, bf16[4,1,192,768]{3,2,0,1:T(8,128)(2,1)}, u32[]{:S(2)}, u32[]{:S(2)}) collective-permute-start(bf16[4,1,192,768]{3,2,0,1:T(8,128)(2,1)} %add_convert_fusion.12), channel_id=1, source_target_pairs={{4,12},{6,14},{12,20},{14,22},{20,28},{22,30},{28,24},{30,26},{24,... | collective-permute-start | bytes 3538952 | tf_op jit(solution)/shard_map/ppermute | solution.py:342
  264.3 32.8 %collective-permute-start.30 = (bf16[1,512,768]{2,1,0:T(8,128)(2,1)S(1)}, bf16[1,512,768]{2,1,0:T(8,128)(2,1)}, u32[]{:S(2)}, u32[]{:S(2)}) collective-permute-start(bf16[1,512,768]{2,1,0:T(8,128)(2,1)S(1)} %slice.65), channel_id=1, source_target_pairs={{0,1},{1,0},{2,3},{3,2},{4,5},{5,4},{6,7},{7,6},{8,9},{9,8},{10,11... | collective-permute-start | bytes 2359304 | tf_op jit(solution)/shard_map/ppermute | solution.py:375
  307.3 28.7 %collective-permute-start.31 = (bf16[4,1,192,768]{3,2,0,1:T(8,128)(2,1)}, bf16[4,1,192,768]{3,2,0,1:T(8,128)(2,1)}, u32[]{:S(2)}, u32[]{:S(2)}) collective-permute-start(bf16[4,1,192,768]{3,2,0,1:T(8,128)(2,1)} %add_convert_fusion.9), channel_id=1, source_target_pairs={{0,8},{2,10},{8,16},{10,18},{16,24},{18,26},{24,28},{26,30},{28,20... | collective-permute-start | bytes 3538952 | tf_op jit(solution)/shard_map/ppermute | solution.py:342
  308.9 28.4 %collective-permute-start.32 = (bf16[4,1,192,768]{3,2,0,1:T(8,128)(2,1)}, bf16[4,1,192,768]{3,2,0,1:T(8,128)(2,1)}, u32[]{:S(2)}, u32[]{:S(2)}) collective-permute-start(bf16[4,1,192,768]{3,2,0,1:T(8,128)(2,1)} %add_convert_fusion.8), channel_id=1, source_target_pairs={{4,12},{6,14},{12,20},{14,22},{20,28},{22,30},{28,24},{30,26},{24,... | collective-permute-start | bytes 3538952 | tf_op jit(solution)/shard_map/ppermute | solution.py:342
  344.2 29.7 %collective-permute-start.36 = (bf16[832,768]{1,0:T(8,128)(2,1)}, bf16[832,768]{1,0:T(8,128)(2,1)}, u32[]{:S(2)}, u32[]{:S(2)}) collective-permute-start(bf16[832,768]{1,0:T(8,128)(2,1)} %dynamic-slice_bitcast_fusion.1), channel_id=1, source_target_pairs={{0,1},{1,0},{2,3},{3,2},{4,5},{5,4},{6,7},{7,6},{8,9},{9,8},{10,11... | collective-permute-start | bytes 3833864 | tf_op jit(solution)/shard_map/ppermute | solution.py:375
  344.6 30.9 %collective-permute-start.34 = (bf16[4,1,192,768]{3,2,0,1:T(8,128)(2,1)}, bf16[4,1,192,768]{3,2,0,1:T(8,128)(2,1)}, u32[]{:S(2)}, u32[]{:S(2)}) collective-permute-start(bf16[4,1,192,768]{3,2,0,1:T(8,128)(2,1)} %add_convert_fusion.7), channel_id=1, source_target_pairs={{0,8},{2,10},{8,16},{10,18},{16,24},{18,26},{24,28},{26,30},{28,20... | collective-permute-start | bytes 3538952 | tf_op jit(solution)/shard_map/ppermute | solution.py:342
  346.1 29.5 %collective-permute-start.35 = (bf16[4,1,192,768]{3,2,0,1:T(8,128)(2,1)}, bf16[4,1,192,768]{3,2,0,1:T(8,128)(2,1)}, u32[]{:S(2)}, u32[]{:S(2)}) collective-permute-start(bf16[4,1,192,768]{3,2,0,1:T(8,128)(2,1)} %add_convert_fusion.6), channel_id=1, source_target_pairs={{4,12},{6,14},{12,20},{14,22},{20,28},{22,30},{28,24},{30,26},{24,... | collective-permute-start | bytes 3538952 | tf_op jit(solution)/shard_map/ppermute | solution.py:342
  414.8 31.9 %collective-permute-start.41 = (bf16[4,1,192,768]{3,2,0,1:T(8,128)(2,1)S(1)}, bf16[4,1,192,768]{3,2,0,1:T(8,128)(2,1)S(1)}, u32[]{:S(2)}, u32[]{:S(2)}) collective-permute-start(bf16[4,1,192,768]{3,2,0,1:T(8,128)(2,1)S(1)} %add_convert_fusion.3), channel_id=1, source_target_pairs={{0,8},{2,10},{8,16},{10,18},{16,24},{18,26},{24,28},{26,30},{28,20... | collective-permute-start | bytes 3538952 | tf_op jit(solution)/shard_map/ppermute | solution.py:342
  415.5 31.2 %collective-permute-start.42 = (bf16[4,1,192,768]{3,2,0,1:T(8,128)(2,1)S(1)}, bf16[4,1,192,768]{3,2,0,1:T(8,128)(2,1)S(1)}, u32[]{:S(2)}, u32[]{:S(2)}) collective-permute-start(bf16[4,1,192,768]{3,2,0,1:T(8,128)(2,1)S(1)} %add_convert_fusion.2), channel_id=1, source_target_pairs={{4,12},{6,14},{12,20},{14,22},{20,28},{22,30},{28,24},{30,26},{24,... | collective-permute-start | bytes 3538952 | tf_op jit(solution)/shard_map/ppermute | solution.py:342
  447.3 31.4 %collective-permute-start.47 = (bf16[4,1,192,768]{3,2,0,1:T(8,128)(2,1)S(1)}, bf16[4,1,192,768]{3,2,0,1:T(8,128)(2,1)S(1)}, u32[]{:S(2)}, u32[]{:S(2)}) collective-permute-start(bf16[4,1,192,768]{3,2,0,1:T(8,128)(2,1)S(1)} %collective-permute-done.41), channel_id=1, source_target_pairs={{0,8},{2,10},{8,16},{10,18},{16,24},{18,26},{24,28},{26,30},{28,20... | collective-permute-start | bytes 3538952 | tf_op jit(solution)/shard_map/ppermute | solution.py:342
  448.1 30.7 %collective-permute-start.48 = (bf16[4,1,192,768]{3,2,0,1:T(8,128)(2,1)S(1)}, bf16[4,1,192,768]{3,2,0,1:T(8,128)(2,1)S(1)}, u32[]{:S(2)}, u32[]{:S(2)}) collective-permute-start(bf16[4,1,192,768]{3,2,0,1:T(8,128)(2,1)S(1)} %collective-permute-done.42), channel_id=1, source_target_pairs={{4,12},{6,14},{12,20},{14,22},{20,28},{22,30},{28,24},{30,26},{24,... | collective-permute-start | bytes 3538952 | tf_op jit(solution)/shard_map/ppermute | solution.py:342
  479.7 28.8 %collective-permute-start.53 = (bf16[4,1,192,768]{3,2,0,1:T(8,128)(2,1)S(1)}, bf16[4,1,192,768]{3,2,0,1:T(8,128)(2,1)S(1)}, u32[]{:S(2)}, u32[]{:S(2)}) collective-permute-start(bf16[4,1,192,768]{3,2,0,1:T(8,128)(2,1)S(1)} %collective-permute-done.47), channel_id=1, source_target_pairs={{0,8},{2,10},{8,16},{10,18},{16,24},{18,26},{24,28},{26,30},{28,20... | collective-permute-start | bytes 3538952 | tf_op jit(solution)/shard_map/ppermute | solution.py:342
  480.2 28.3 %collective-permute-start.54 = (bf16[4,1,192,768]{3,2,0,1:T(8,128)(2,1)S(1)}, bf16[4,1,192,768]{3,2,0,1:T(8,128)(2,1)S(1)}, u32[]{:S(2)}, u32[]{:S(2)}) collective-permute-start(bf16[4,1,192,768]{3,2,0,1:T(8,128)(2,1)S(1)} %collective-permute-done.48), channel_id=1, source_target_pairs={{4,12},{6,14},{12,20},{14,22},{20,28},{22,30},{28,24},{30,26},{24,... | collective-permute-start | bytes 3538952 | tf_op jit(solution)/shard_map/ppermute | solution.py:342
  511.7 31.6 %collective-permute-start.58 = (bf16[4,1,192,768]{3,2,0,1:T(8,128)(2,1)S(1)}, bf16[4,1,192,768]{3,2,0,1:T(8,128)(2,1)S(1)}, u32[]{:S(2)}, u32[]{:S(2)}) collective-permute-start(bf16[4,1,192,768]{3,2,0,1:T(8,128)(2,1)S(1)} %collective-permute-done.53), channel_id=1, source_target_pairs={{0,8},{2,10},{8,16},{10,18},{16,24},{18,26},{24,28},{26,30},{28,20... | collective-permute-start | bytes 3538952 | tf_op jit(solution)/shard_map/ppermute | solution.py:342
  512.2 31.1 %collective-permute-start.59 = (bf16[4,1,192,768]{3,2,0,1:T(8,128)(2,1)S(1)}, bf16[4,1,192,768]{3,2,0,1:T(8,128)(2,1)S(1)}, u32[]{:S(2)}, u32[]{:S(2)}) collective-permute-start(bf16[4,1,192,768]{3,2,0,1:T(8,128)(2,1)S(1)} %collective-permute-done.54), channel_id=1, source_target_pairs={{4,12},{6,14},{12,20},{14,22},{20,28},{22,30},{28,24},{30,26},{24,... | collective-permute-start | bytes 3538952 | tf_op jit(solution)/shard_map/ppermute | solution.py:342
  543.9 31.6 %collective-permute-start.64 = (bf16[4,1,192,768]{3,2,0,1:T(8,128)(2,1)S(1)}, bf16[4,1,192,768]{3,2,0,1:T(8,128)(2,1)S(1)}, u32[]{:S(2)}, u32[]{:S(2)}) collective-permute-start(bf16[4,1,192,768]{3,2,0,1:T(8,128)(2,1)S(1)} %collective-permute-done.58), channel_id=1, source_target_pairs={{0,8},{2,10},{8,16},{10,18},{16,24},{18,26},{24,28},{26,30},{28,20... | collective-permute-start | bytes 3538952 | tf_op jit(solution)/shard_map/ppermute | solution.py:342
  544.4 31.1 %collective-permute-start.65 = (bf16[4,1,192,768]{3,2,0,1:T(8,128)(2,1)S(1)}, bf16[4,1,192,768]{3,2,0,1:T(8,128)(2,1)S(1)}, u32[]{:S(2)}, u32[]{:S(2)}) collective-permute-start(bf16[4,1,192,768]{3,2,0,1:T(8,128)(2,1)S(1)} %collective-permute-done.59), channel_id=1, source_target_pairs={{4,12},{6,14},{12,20},{14,22},{20,28},{22,30},{28,24},{30,26},{24,... | collective-permute-start | bytes 3538952 | tf_op jit(solution)/shard_map/ppermute | solution.py:342
  576.1 32.1 %collective-permute-start.70 = (bf16[4,1,192,768]{3,2,0,1:T(8,128)(2,1)S(1)}, bf16[4,1,192,768]{3,2,0,1:T(8,128)(2,1)S(1)}, u32[]{:S(2)}, u32[]{:S(2)}) collective-permute-start(bf16[4,1,192,768]{3,2,0,1:T(8,128)(2,1)S(1)} %collective-permute-done.64), channel_id=1, source_target_pairs={{0,8},{2,10},{8,16},{10,18},{16,24},{18,26},{24,28},{26,30},{28,20... | collective-permute-start | bytes 3538952 | tf_op jit(solution)/shard_map/ppermute | solution.py:342
  577.1 31.1 %collective-permute-start.71 = (bf16[4,1,192,768]{3,2,0,1:T(8,128)(2,1)S(1)}, bf16[4,1,192,768]{3,2,0,1:T(8,128)(2,1)S(1)}, u32[]{:S(2)}, u32[]{:S(2)}) collective-permute-start(bf16[4,1,192,768]{3,2,0,1:T(8,128)(2,1)S(1)} %collective-permute-done.65), channel_id=1, source_target_pairs={{4,12},{6,14},{12,20},{14,22},{20,28},{22,30},{28,24},{30,26},{24,... | collective-permute-start | bytes 3538952 | tf_op jit(solution)/shard_map/ppermute | solution.py:342
  608.8 31.4 %collective-permute-start.76 = (bf16[4,1,192,768]{3,2,0,1:T(8,128)(2,1)S(1)}, bf16[4,1,192,768]{3,2,0,1:T(8,128)(2,1)}, u32[]{:S(2)}, u32[]{:S(2)}) collective-permute-start(bf16[4,1,192,768]{3,2,0,1:T(8,128)(2,1)S(1)} %collective-permute-done.70), channel_id=1, source_target_pairs={{0,8},{2,10},{8,16},{10,18},{16,24},{18,26},{24,28},{26,30},{28,20... | collective-permute-start | bytes 3538952 | tf_op jit(solution)/shard_map/ppermute | solution.py:342
  610.4 29.8 %collective-permute-start.77 = (bf16[4,1,192,768]{3,2,0,1:T(8,128)(2,1)S(1)}, bf16[4,1,192,768]{3,2,0,1:T(8,128)(2,1)}, u32[]{:S(2)}, u32[]{:S(2)}) collective-permute-start(bf16[4,1,192,768]{3,2,0,1:T(8,128)(2,1)S(1)} %collective-permute-done.71), channel_id=1, source_target_pairs={{4,12},{6,14},{12,20},{14,22},{20,28},{22,30},{28,24},{30,26},{24,... | collective-permute-start | bytes 3538952 | tf_op jit(solution)/shard_map/ppermute | solution.py:342
  (118 other events, 1330.9 us)
